TPU v7x, 512 devices: a whole 4x4x16 slice. The times are simulated.
512 devices in a mesh: space: 64 (over z, x), coil: 8 (over y, core).
Axes of the slice: x: 4, y: 4, z: 16, core: 2. Of those that a mesh axis runs over, the one named last changes fastest.
Arguments:
- sample_values: bfloat16 [16, 2, 262144], P('coil', None, 'space'), may hold values from -6 to 6
- sample_offsets: bfloat16 [3, 262144], P(None, 'space'), may hold values from 0 to 1
- sample_cells: int32 [262144], P('space'), may hold values from 0 to 262143, as said below
- sample_slots: int32 [262144], P('space'), may hold values from 0 to 4096, as said below
- sensitivity: bfloat16 [16, 2, 256, 256, 256], P('coil', None, None, 'space'), may hold values from -5 to 5
Outputs:
- image: float32 [2, 256, 256, 256], P(None, 'coil', 'space')
Inputs may be any that keep to these rules, and one draw needn't show every extreme that they name: Slots q * 64 to (q + 1) * 64 - 1 of each space index hold samples for space index q. sample_slots gives a used sample's place in q's buffer of 16 tiles of 256 slots: tile (sample_slots // 256) covers rows 16 times the tile number onward, and no two used samples for one destination share a place; the value 16 * 256 marks an unused slot. Some destination has all its places used, so it receives 64 samples from every space index. `sample_cells`: (x * 256 + y) * 256 + z with x the plane within the destination's 4 planes; for a used sample y // 16 equals sample_slots // 256.
All inputs are finite; a program needn't handle non-finite values.
Results may differ from a plain program's by a relative error of at most 0.006.
The roundings to bfloat16 on the way count: a program that leaves them out, or rounds other values in their place, can miss the bound.
Values may be sent and summed in bfloat16 or wider, within the bound.
No kernel may reach another device: no remote copies, remote signals or barrier semaphores. Data moves between devices by JAX's collectives and lax.ppermute only.
A program may use at most 128 MiB of HBM per device.

v0:
```python
import math

import jax
import jax.numpy as jnp
from jax import lax
from jax.sharding import PartitionSpec as P

GX = 256
GY = 256
GZ = 256
TY = 16
TCAP = 256


BETA = 9.0


def from_behind(shard, axis, by):
    length = lax.axis_size(axis)
    return lax.ppermute(shard, axis, [(i, (i + by) % length) for i in range(length)])


def bessel_zero(value):
    quarter = 0.25 * value * value
    term = jnp.ones_like(value)
    total = term
    for order in range(1, 31):
        term = term * quarter / float(order * order)
        total = total + term
    return total


def kaiser(distance):
    inner = jnp.maximum(1.0 - (0.5 * distance) ** 2, 0.0)
    return bessel_zero(BETA * jnp.sqrt(inner)) / bessel_zero(jnp.zeros((), jnp.float32) + BETA)


def tap_weights(fraction):
    shifts = jnp.arange(4, dtype=jnp.float32)
    return kaiser(fraction[None, :] + 1.0 - shifts[:, None])


def dft_table(length):
    counter = jnp.arange(length, dtype=jnp.int32)
    product = counter[:, None] * counter[None, :] % length
    phases = product.astype(jnp.float32) * (2.0 * math.pi / length)
    factor = 1.0 / math.sqrt(length)
    cosine = jnp.cos(phases) * factor
    sine = jnp.sin(phases) * factor
    return jnp.stack([jnp.stack([cosine, sine], 1), jnp.stack([-sine, cosine], 1)], 0).astype(
        jnp.bfloat16
    )


def weigh(images, maps):
    image_f = images.astype(jnp.float32)
    map_f = maps.astype(jnp.float32)
    real_part = jnp.sum(map_f[:, 0] * image_f[:, 0] + map_f[:, 1] * image_f[:, 1], axis=0)
    imag_part = jnp.sum(map_f[:, 0] * image_f[:, 1] - map_f[:, 1] * image_f[:, 0], axis=0)
    return jnp.stack([real_part, imag_part], 0)


def dense_taps(weights, location, extent, wrapped):
    positions = jnp.arange(extent, dtype=jnp.int32)
    dense = jnp.zeros(location.shape + (extent,), jnp.float32)
    for step_count in range(4):
        spot = location + step_count
        if wrapped:
            spot = (spot - 1) % extent
        dense = dense + jnp.where(
            positions[None, :] == spot[:, None], weights[step_count][:, None], 0.0
        )
    return dense


def grid_blocks(values, offsets, cells, plane_shift, planes, tiles, coil_dev):
    send_dev = values.shape[1]
    fractions = offsets.astype(jnp.float32)
    plane_local = cells // (GY * GZ) + plane_shift
    row_global = cells // GZ % GY
    depth_index = cells % GZ
    tile_index = jnp.arange(send_dev, dtype=jnp.int32) // TCAP
    row_local = row_global - tile_index * TY
    dense_x = dense_taps(tap_weights(fractions[0]), plane_local, planes + 3, False).T
    dense_y = dense_taps(tap_weights(fractions[1]), row_local, TY + 3, False).T
    dense_z = dense_taps(tap_weights(fractions[2]), depth_index, GZ, True).astype(jnp.bfloat16)
    spread = (
        values.astype(jnp.float32).reshape(coil_dev, 2, 1, 1, send_dev)
        * dense_x[None, None, :, None, :]
        * dense_y[None, None, None, :, :]
    ).astype(jnp.bfloat16)
    row_count = coil_dev * 2 * (planes + 3) * (TY + 3)
    return jnp.einsum(
        "nts,tsz->tnz",
        spread.reshape(row_count, tiles, TCAP),
        dense_z.reshape(tiles, TCAP, GZ),
        preferred_element_type=jnp.float32,
    )


def body(sample_values, sample_offsets, sample_cells, sample_slots, sensitivity):
    coil_dev = sample_values.shape[0]
    send_dev = sample_values.shape[2]
    planes = GX // lax.axis_size("space")
    tiles = GY // TY
    stacked_values = sample_values.reshape(coil_dev * 2, send_dev)
    labels = jnp.stack([sample_cells, sample_slots], 0)
    got_values, got_offsets, got_labels = (
        lax.all_to_all(stacked_values, "space", split_axis=1, concat_axis=1, tiled=True),
        lax.all_to_all(sample_offsets, "space", split_axis=1, concat_axis=1, tiled=True),
        lax.all_to_all(labels, "space", split_axis=1, concat_axis=1, tiled=True),
    )
    target = got_labels[1]
    tile_values = (
        jnp.zeros((coil_dev * 2, send_dev), jnp.bfloat16).at[:, target].set(got_values, mode="drop")
    )
    tile_offsets = (
        jnp.zeros((3, send_dev), jnp.bfloat16).at[:, target].set(got_offsets, mode="drop")
    )
    tile_cells = jnp.zeros((send_dev,), jnp.int32).at[target].set(got_labels[0], mode="drop")
    blocks = grid_blocks(tile_values, tile_offsets, tile_cells, 0, planes, tiles, coil_dev)
    blocks = blocks.reshape(tiles, coil_dev, 2, planes + 3, TY + 3, GZ)
    inner_rows = blocks[:, :, :, :, 1 : TY + 1]
    leading = blocks[:, :, :, :, 0]
    trailing = blocks[:, :, :, :, TY + 1 :]
    inner_rows = inner_rows.at[:, :, :, :, TY - 1].add(jnp.roll(leading, -1, axis=0))
    inner_rows = inner_rows.at[:, :, :, :, 0:2].add(jnp.roll(trailing, 1, axis=0))
    padded = jnp.moveaxis(inner_rows, 0, 3).reshape(coil_dev, 2, planes + 3, GY, GZ)
    own_planes = padded[:, :, 1 : planes + 1]
    from_lower = from_behind(padded[:, :, planes + 1 :], "space", 1)
    from_upper = from_behind(padded[:, :, 0:1], "space", -1)
    own_planes = own_planes.at[:, :, 0:2].add(from_lower)
    own_planes = own_planes.at[:, :, planes - 1 :].add(from_upper)
    grid = own_planes.astype(jnp.bfloat16)
    along_z = jnp.einsum(
        "crxyz,rzsn->csxyn", grid, dft_table(GZ), preferred_element_type=jnp.float32
    ).astype(jnp.bfloat16)
    along_y = jnp.einsum(
        "crxyz,rysn->csxnz", along_z, dft_table(GY), preferred_element_type=jnp.float32
    ).astype(jnp.bfloat16)
    turned = lax.all_to_all(along_y, "space", split_axis=3, concat_axis=2, tiled=True)
    coil_image = jnp.einsum(
        "crxyz,rxsn->csnyz", turned, dft_table(GX), preferred_element_type=jnp.float32
    ).astype(jnp.bfloat16)
    partial_term = weigh(coil_image, sensitivity)
    return lax.psum_scatter(partial_term, "coil", scatter_dimension=1, tiled=True)


def solution(mesh):
    placed = (
        P("coil", None, "space"),
        P(None, "space"),
        P("space"),
        P("space"),
        P("coil", None, None, "space", None),
    )
    return jax.shard_map(
        body, mesh=mesh, in_specs=placed, out_specs=P(None, "coil", "space", None), check_vma=False
    )
```

profile of v0, /device:TPU:1, one launch (start us, length us, event | category | flops | bytes accessed | tf_op | source)
XLA Modules:
  0.0 375.0 jit_solution(6242659567821372552)
XLA Ops:
  6.5 0.9 all_to_all.37
  7.4 0.7 copy.57
  8.1 19.1 %all-to-all-start.2 = ((bf16[3,64,64]{2,0,1:T(4,128)(2,1)}), bf16[3,64,64]{2,0,1:T(4,128)(2,1)S(1)}, u32[]{:S(2)}, u32[]{:S(2)}) async-start(bf16[3,64,64]{2,0,1:T(4,128)(2,1)} %copy.57), calls=%async_computation.2 | async-start | bytes 131072 | tf_op jit(solution)/shard_map/all_to_all | solution.py:110
  27.2 0.8 stack.32
  28.0 0.8 stack.66
  28.9 0.7 reshape.774
  29.6 11.6 %all-to-all-done.2 = bf16[3,64,64]{2,0,1:T(4,128)(2,1)S(1)} async-done(((bf16[3,64,64]{2,0,1:T(4,128)(2,1)}), bf16[3,64,64]{2,0,1:T(4,128)(2,1)S(1)}, u32[]{:S(2)}, u32[]{:S(2)}) %all-to-all-start.2) | async-done | bytes 24608 | tf_op jit(solution)/shard_map/all_to_all | solution.py:110
  41.2 4.6 %all-to-all-start = ((s32[64,1,128]{2,1,0:T(1,128)}), s32[64,1,128]{2,1,0:T(1,128)S(1)}, u32[]{:S(2)}, u32[]{:S(2)}) async-start(s32[64,1,128]{2,1,0:T(1,128)} %reshape.774), calls=%async_computation | async-start | bytes 65536 | tf_op jit(solution)/shard_map/all_to_all | solution.py:111
  45.8 0.9 all_to_all.34
  46.8 0.7 reshape.776
  47.5 0.1 reshape.714
  47.6 0.5 copy.59
  48.1 11.1 %all-to-all-done = s32[64,1,128]{2,1,0:T(1,128)S(1)} async-done(((s32[64,1,128]{2,1,0:T(1,128)}), s32[64,1,128]{2,1,0:T(1,128)S(1)}, u32[]{:S(2)}, u32[]{:S(2)}) %all-to-all-start) | async-done | bytes 32800 | tf_op jit(solution)/shard_map/all_to_all | solution.py:111
  59.2 4.6 %all-to-all-start.1 = ((bf16[64,2,128]{2,1,0:T(2,128)(2,1)}), bf16[64,2,128]{2,1,0:T(2,128)(2,1)S(1)}, u32[]{:S(2)}, u32[]{:S(2)}) async-start(bf16[64,2,128]{2,1,0:T(2,128)(2,1)} %reshape.776), calls=%async_computation.1 | async-start | bytes 65536 | tf_op jit(solution)/shard_map/all_to_all | solution.py:109
  63.8 0.6 broadcast.1025
  64.4 0.8 reduce.40
  65.2 0.1 reshape.775
  65.3 0.2 slice_reduce_fusion
  65.7 15.5 %scatter_custom_fusion.1 = s32[4096]{0:T(1024)S(1)} fusion(s32[4096]{0:T(1024)S(1)} %bitcast.125, s32[4096]{0:T(1024)S(1)} %reshape.709, s32[]{:T(128)} %constant.330.clone.1), kind=kCustom, calls=%fused_computation.143 | custom fusion | bytes 16388 | tf_op jit(solution)/shard_map/scatter | solution.py:120
  81.3 11.7 %scatter_custom_fusion.2 = bf16[3,4096]{0,1:T(8,128)(2,1)S(1)} fusion(s32[4096]{0:T(1024)S(1)} %bitcast.126, bf16[4096,3]{1,0:T(8,128)(2,1)S(1)} %copy.59, bf16[]{:T(256)} %constant.335.clone.1), kind=kCustom, calls=%fused_computation.50 | custom fusion | bytes 24578 | tf_op jit(solution)/shard_map/scatter | solution.py:118
  92.9 0.1 convert_element_type.74
  93.1 2.8 fusion.3
  95.9 0.9 add_multiply_fusion
  96.9 0.5 add_multiply_fusion.2
  97.5 0.1 reshape.698
  97.6 0.5 copy.55
  98.2 11.1 %scatter_custom_fusion = bf16[4,4096]{0,1:T(8,128)(2,1)S(1)} fusion(s32[4096]{0:T(1024)S(1)} %bitcast.127, bf16[4096,4]{1,0:T(8,128)(2,1)S(1)} %copy.55, bf16[]{:T(256)} %constant.335.clone.1), kind=kCustom, calls=%fused_computation.52 | custom fusion | bytes 32770 | tf_op jit(solution)/shard_map/scatter | solution.py:115
  109.3 0.4 copy.81
  109.9 0.1 select_add_fusion
  110.0 3.5 multiply_convert_fusion
  113.6 8.7 %convert_element_type.76 = bf16[532,16,256]{2,1,0:T(8,128)(2,1)} reshape(bf16[2,2,7,19,4096]{4,3,2,1,0:T(8,128)(2,1)} %multiply_convert_fusion) | data formatting | bytes 8716288 | tf_op jit(solution)/shard_map/convert_element_type | solution.py:91
  122.2 0.2 slice_reduce_fusion.5
  122.5 12.8 %fusion = f32[16,532,256]{2,1,0:T(8,128)} fusion(bf16[532,16,256]{2,1,0:T(8,128)(2,1)} %convert_element_type.76, f32[16,256]{1,0:T(8,128)S(1)} %broadcast_in_dim.173, s32[16,256]{1,0:T(8,128)S(1)} %eq.256, f32[16,256]{1,0:T(8,128)S(1)} %broadcast_in_dim.171, s32[16,256]{1,0:T(8,128)S(1)} %eq.252, f32[16,256]{1,0:T(8,128)S(1)} %broadcast_in_dim.169, ...), kind=kOutput, calls=%fused_computation.4 | convolution fusion | flops 1128267776 | bytes 13205504 | tf_op jit(solution)/shard_map/nts,tsz->tnz/dot_general | solution.py:93
  135.3 6.3 %copy.61 = f32[16,532,256]{2,0,1:T(8,128)S(1)} copy(f32[16,532,256]{2,1,0:T(8,128)} %fusion) | data formatting | bytes 17432576 | tf_op jit(solution)/shard_map/nts,tsz->tnz/dot_general | solution.py:93
  141.6 1.3 slice.320
  143.1 0.1 fusion.34
  143.2 0.4 fusion.25
  143.6 6.5 %copy.62 = f32[2,2,7,16,16,256]{5,4,3,2,1,0:T(8,128)S(1)} copy(f32[2,2,7,16,16,256]{5,3,4,2,1,0:T(8,128)S(1)} %bitcast.105) | data formatting | bytes 14680064 | tf_op jit(solution)/shard_map/transpose | solution.py:128
  150.1 0.2 slice.329
  150.3 2.8 collective-permute-start
  153.2 6.0 %collective-permute-start.1 = (f32[2,2,1,256,256]{4,3,2,1,0:T(8,128)S(1)}, f32[2,2,1,256,256]{4,3,2,1,0:T(8,128)S(1)}, u32[]{:S(2)}, u32[]{:S(2)}) collective-permute-start(f32[2,2,1,256,256]{4,3,2,1,0:T(8,128)S(1)} %slice.331), channel_id=1, source_target_pairs={{0,504},{8,0},{16,8},{24,16},{32,24},{40,32},{48,40},{56,48},{64,5... | collective-permute-start | bytes 3145736 | tf_op jit(solution)/shard_map/ppermute | solution.py:20
  159.2 1.0 fusion.41
  160.2 1.1 negate_convert_fusion
  161.4 2.3 slice.327
  163.7 35.5 %collective-permute-done = f32[2,2,2,256,256]{4,3,2,1,0:T(8,128)S(1)} collective-permute-done((f32[2,2,2,256,256]{4,3,2,1,0:T(8,128)S(1)}, f32[2,2,2,256,256]{4,3,2,1,0:T(8,128)S(1)}, u32[]{:S(2)}, u32[]{:S(2)}) %collective-permute-start) | collective-permute-done | bytes 2097184 | tf_op jit(solution)/shard_map/ppermute | solution.py:20
  199.2 1.6 fusion.2
  200.8 2.3 fusion.20
  203.1 4.6 %fusion.17 = bf16[2,2,4,256,256]{4,3,2,0,1:T(8,128)(2,1)S(1)} fusion(bf16[1,256,2,256]{1,3,0,2:T(8,128)(2,1)S(1)} %get-tuple-element.67, bf16[1,256,2,256]{1,3,0,2:T(8,128)(2,1)S(1)} %get-tuple-element.66, f32[2,2,4,256,256]{4,3,2,1,0:T(8,128)} %fusion.20), kind=kOutput, calls=%fused_computation.41 | convolution fusion | flops 2152726528 | bytes 6815744 | tf_op jit(solution)/shard_map/crxyz,rysn->csxnz/dot_general | solution.py:138
  207.7 3.0 copy.65
  210.6 11.8 %all-to-all-start.3 = ((bf16[2,2,4,256,256]{4,2,0,1,3:T(4,128)(2,1)}), bf16[2,2,4,256,256]{4,2,0,1,3:T(4,128)(2,1)S(1)}, u32[]{:S(2)}, u32[]{:S(2)}) async-start(bf16[2,2,4,256,256]{4,2,0,1,3:T(4,128)(2,1)} %copy.65), calls=%async_computation.3 | async-start | bytes 4194304 | tf_op jit(solution)/shard_map/all_to_all | solution.py:141
  222.5 0.3 reduce-scatter.5.cloned.1.call-start
  222.8 4.0 %copy_convert_fusion = f32[2,2,256,4,256]{4,2,3,0,1:T(8,128)} fusion(bf16[2,2,256,4,256]{4,3,2,1,0:T(4,128)(2,1)} %param.17), kind=kLoop, calls=%fused_computation.28 | loop fusion | flops 1048576 | bytes 6291456 | tf_op jit(solution)/shard_map/convert_element_type | solution.py:57
  226.8 87.6 %all-to-all-done.3 = bf16[2,2,4,256,256]{4,2,0,1,3:T(4,128)(2,1)S(1)} async-done(((bf16[2,2,4,256,256]{4,2,0,1,3:T(4,128)(2,1)}), bf16[2,2,4,256,256]{4,2,0,1,3:T(4,128)(2,1)S(1)}, u32[]{:S(2)}, u32[]{:S(2)}) %all-to-all-start.3) | async-done | bytes 2097184 | tf_op jit(solution)/shard_map/all_to_all | solution.py:141
  314.4 2.3 copy.95
  316.7 2.5 reshape.726
  319.3 1.3 convert_bitcast_fusion
  320.5 0.9 copy-done
  321.4 0.9 add_reduce_fusion
  322.4 0.1 pad_maximum_fusion
  322.5 1.4 copy.94
  323.9 2.1 reshape.729
  326.1 40.0 %reduce-scatter.5.cloned.1.call-done = f32[32,2048]{1,0:T(8,128)} async-done(((f32[256,2048]{1,0:T(8,128)}), f32[32,2048]{1,0:T(8,128)}) %reduce-scatter.5.cloned.1.call-update) | async-done | bytes 262160
  366.0 1.1 reshape.730
  367.2 0.7 copy.79
  (33 shorter events, 1.1 us)
Async XLA Ops:
  8.1 33.1 %all-to-all-start.2 = ((bf16[3,64,64]{2,0,1:T(4,128)(2,1)}), bf16[3,64,64]{2,0,1:T(4,128)(2,1)S(1)}, u32[]{:S(2)}, u32[]{:S(2)}) async-start(bf16[3,64,64]{2,0,1:T(4,128)(2,1)} %copy.57), calls=%async_computation.2 | async-start | bytes 131072 | tf_op jit(solution)/shard_map/all_to_all | solution.py:110
  41.2 18.0 %all-to-all-start = ((s32[64,1,128]{2,1,0:T(1,128)}), s32[64,1,128]{2,1,0:T(1,128)S(1)}, u32[]{:S(2)}, u32[]{:S(2)}) async-start(s32[64,1,128]{2,1,0:T(1,128)} %reshape.774), calls=%async_computation | async-start | bytes 65536 | tf_op jit(solution)/shard_map/all_to_all | solution.py:111
  59.2 38.2 %all-to-all-start.1 = ((bf16[64,2,128]{2,1,0:T(2,128)(2,1)}), bf16[64,2,128]{2,1,0:T(2,128)(2,1)S(1)}, u32[]{:S(2)}, u32[]{:S(2)}) async-start(bf16[64,2,128]{2,1,0:T(2,128)(2,1)} %reshape.776), calls=%async_computation.1 | async-start | bytes 65536 | tf_op jit(solution)/shard_map/all_to_all | solution.py:109
  150.3 48.9 %collective-permute-start = (f32[2,2,2,256,256]{4,3,2,1,0:T(8,128)S(1)}, f32[2,2,2,256,256]{4,3,2,1,0:T(8,128)S(1)}, u32[]{:S(2)}, u32[]{:S(2)}) collective-permute-start(f32[2,2,2,256,256]{4,3,2,1,0:T(8,128)S(1)} %slice.329), channel_id=1, source_target_pairs={{0,8},{8,16},{16,24},{24,32},{32,40},{40,48},{48,56},{56,64},{64,7... | collective-permute-start | bytes 6291464 | tf_op jit(solution)/shard_map/ppermute | solution.py:20
  153.2 47.6 %collective-permute-start.1 = (f32[2,2,1,256,256]{4,3,2,1,0:T(8,128)S(1)}, f32[2,2,1,256,256]{4,3,2,1,0:T(8,128)S(1)}, u32[]{:S(2)}, u32[]{:S(2)}) collective-permute-start(f32[2,2,1,256,256]{4,3,2,1,0:T(8,128)S(1)} %slice.331), channel_id=1, source_target_pairs={{0,504},{8,0},{16,8},{24,16},{32,24},{40,32},{48,40},{56,48},{64,5... | collective-permute-start | bytes 3145736 | tf_op jit(solution)/shard_map/ppermute | solution.py:20
  210.6 103.7 %all-to-all-start.3 = ((bf16[2,2,4,256,256]{4,2,0,1,3:T(4,128)(2,1)}), bf16[2,2,4,256,256]{4,2,0,1,3:T(4,128)(2,1)S(1)}, u32[]{:S(2)}, u32[]{:S(2)}) async-start(bf16[2,2,4,256,256]{4,2,0,1,3:T(4,128)(2,1)} %copy.65), calls=%async_computation.3 | async-start | bytes 4194304 | tf_op jit(solution)/shard_map/all_to_all | solution.py:141
  222.5 143.6 %reduce-scatter.5.cloned.1.call-start = ((), (), s32[]{:S(2)}) async-start(), calls=%async_computation.5 | async-start | bytes 2359296
  319.3 2.2 copy-start
Sparse Core Ops, SparseCore 0:
  326.2 39.8 reduce-scatter.4
where the time goes:
time: 383 us; the launch traced here: 375 us
  waiting for transfers between devices  186 us (49%)
  local copies, waits for them, and re-layouts  86.5 us (23%)
  starting transfers between devices  49.3 us (13%)
  other arithmetic  20.6 us (5%)
  matrix products  18.6 us (5%)
  between operations  14.1 us (4%)
    all_to_all x1, waiting for transfers between devices, body(): lax.all_to_all(along_y, 'space', split_axis=3, concat_axis=2, tiled=True)  87.6 us
    unnamed x2, waiting for transfers between devices  40 us
    ppermute x2, waiting for transfers between devices, from_behind(): lax.ppermute(shard, axis, [(i, (i + by) % length) for i in range(length)])  35.5 us
    all_to_all x1, starting transfers between devices, body(): lax.all_to_all(sample_offsets, 'space', split_axis=1, concat_axis=1, tile...  19.1 us
    scatter x1, local copies, waits for them, and re-layouts, body(): jnp.zeros((send_dev,), jnp.int32).at[target].set(got_labels[0], mode='drop')  15.5 us
    dot_general x1, matrix products, grid_blocks(): jnp.einsum('nts,tsz->tnz', spread.reshape(row_count, tiles, TCAP), dense_...  12.8 us
    all_to_all x1, starting transfers between devices, body(): lax.all_to_all(along_y, 'space', split_axis=3, concat_axis=2, tiled=True)  11.8 us
    scatter x1, local copies, waits for them, and re-layouts, body(): jnp.zeros((3, send_dev), jnp.bfloat16).at[:, target]  11.7 us
  transfers between devices with their start and end apart: 7, of which 5 were waited for; matrix products, arithmetic and copies ran while one was open for 13% of the time, Pallas kernels for 0%

commit v1 on v0

v1 whole, which is shorter than its diff:
```python
import math

import jax
import jax.numpy as jnp
import ml_dtypes
import numpy as np
from jax import lax
from jax.experimental import pallas as pl
from jax.experimental.pallas import tpu as pltpu
from jax.sharding import Mesh
from jax.sharding import PartitionSpec as P

GX = 256
GY = 256
GZ = 256
SLOTS = 4096
CAP = 64

BETA = 9.0
TERMS = 31

GROUPS = 8
BLOCKS = 8
ZN = 16
LANES = 256
STEP = 4
COILS = 4
ROWS = 16
TAPS = 4
SPAN = 7
PAIR = 2 * COILS * ROWS
HALO = 4


def series():
    quarter = 0.25 * BETA * BETA
    terms = [quarter**k / float(math.factorial(k)) ** 2 for k in range(TERMS)]
    total = math.fsum(terms)
    return [float(np.float32(t / total)) for t in terms]


def waves():
    counter = np.arange(256)
    phase = (counter[:, None] * counter[None, :] % 256).astype(np.float32) * np.float32(
        2.0 * math.pi / 256
    )
    scale = np.float32(1.0 / 16.0)
    both = np.stack([np.cos(phase) * scale, np.sin(phase) * scale], 0)
    return both.astype(ml_dtypes.bfloat16).astype(np.float32)


def z_table():
    cosine, sine = waves()
    return np.block([[cosine, sine], [-sine, cosine]]).astype(ml_dtypes.bfloat16)


def y_table():
    both = waves().reshape(2, ZN, ROWS, 256)
    return both.transpose(1, 0, 2, 3).reshape(ZN, 2 * ROWS, 256).astype(ml_dtypes.bfloat16)


def x_columns(planes, part):
    cosine, sine = waves()
    if part == 0:
        return np.concatenate([cosine[:, planes], sine[:, planes]], 0)
    return np.concatenate([-sine[:, planes], cosine[:, planes]], 0)


def x_tables():
    main = []
    for chunk in range(2):
        cols = []
        for group in range(GROUPS):
            planes = (32 * group + 16 * chunk + np.arange(16) - 1) % GX
            cols += [x_columns(planes, 0), x_columns(planes, 1)]
        main.append(np.concatenate(cols, 1))
    halo = []
    for coil in range(2):
        cols = []
        for group in range(GROUPS):
            planes = (32 * group + 32 + np.arange(HALO) - 1) % GX
            real = np.arange(HALO) < 3
            for other in range(2):
                keep = real & (other == coil)
                cols += [x_columns(planes, part) * keep for part in range(2)]
        halo.append(np.concatenate(cols, 1))
    return np.stack(main).astype(ml_dtypes.bfloat16), np.stack(halo).astype(ml_dtypes.bfloat16)


def tap_rows(first, second, lanes):
    row = lax.broadcasted_iota(jnp.int32, (8, lanes), 0)
    offset = jnp.where(row < TAPS, first, second)
    distance = offset + (1.0 - (row % TAPS).astype(jnp.float32))
    inner = jnp.maximum(1.0 - 0.25 * distance * distance, 0.0)
    coefficients = series()
    total = jnp.full((8, lanes), coefficients[-1], jnp.float32)
    for value in coefficients[-2::-1]:
        total = total * inner + value
    return total


def dense_rows(weights, base, lanes):
    high = base // 16
    low = base % 16
    row = lax.broadcasted_iota(jnp.int32, (16, lanes), 0)
    pattern = jnp.zeros((16, lanes), jnp.float32)
    for tap in range(TAPS):
        pattern = jnp.where(row == (low + tap) % 16, weights[tap], pattern)
    place = jnp.where(row < low, (high + 1) % 16, high).astype(jnp.float32)
    pattern = pattern.astype(jnp.bfloat16)
    place = place.astype(jnp.bfloat16)
    zero = jnp.zeros((16, lanes), jnp.bfloat16)
    return [
        jnp.where(place == jnp.bfloat16(block), pattern, zero) for block in range(16)
    ]


def build(packed, y_tab, pair_ref, dense_ref, at, lanes):
    taps_xy = tap_rows(packed[4:5], packed[5:6], lanes)
    taps_z = tap_rows(packed[6:7], packed[6:7], lanes)
    cell = packed.astype(jnp.int32)
    base_x = cell[12:13]
    base_y = (cell[13:14] + 255) % 256
    base_z = (cell[14:15] + 255) % 256
    z_blocks = dense_rows([taps_z[t : t + 1] for t in range(TAPS)], base_z, lanes)
    for block in range(16):
        dense_ref[block * 16 : (block + 1) * 16, at : at + lanes] = z_blocks[block]
    y_blocks = dense_rows([taps_xy[4 + t : 5 + t] for t in range(TAPS)], base_y, lanes)
    turn = jnp.dot(y_tab, jnp.concatenate(y_blocks, 0), preferred_element_type=jnp.float32)
    turn_re, turn_im = turn[:ROWS], turn[ROWS:]
    real, imag = [], []
    for coil in range(COILS):
        row = (coil // 2) * 8 + (coil % 2) * 2
        value_re, value_im = packed[row : row + 1], packed[row + 1 : row + 2]
        real.append((value_re * turn_re - value_im * turn_im).astype(jnp.bfloat16))
        imag.append((value_re * turn_im + value_im * turn_re).astype(jnp.bfloat16))
    values = real + imag
    row = lax.broadcasted_iota(jnp.int32, (8, lanes), 0)
    dense_x = jnp.zeros((8, lanes), jnp.float32)
    for tap in range(TAPS):
        dense_x = jnp.where(row == base_x + tap, taps_xy[tap : tap + 1], dense_x)
    for plane in range(SPAN):
        weight = jnp.broadcast_to(dense_x[plane : plane + 1], (ROWS, lanes)).astype(jnp.bfloat16)
        for part in range(2 * COILS):
            start = plane * PAIR + part * ROWS
            pair_ref[start : start + ROWS, at : at + lanes] = values[part] * weight


def emit(grid_planes, z_tab, flat):
    planes = grid_planes.shape[0]
    half = PAIR // 2
    grid = grid_planes.astype(jnp.bfloat16)
    joined = jnp.concatenate([grid[:, :half], grid[:, half:]], axis=2)
    along = jnp.dot(
        joined.reshape(planes * half, 2 * GZ), z_tab, preferred_element_type=jnp.float32
    )
    return jnp.swapaxes(along.reshape(planes, half, 2 * GZ), 0, 1)


def grid_kernel(blocks, samples_ref, y_ref, z_ref, carry_ref, main_ref, last_ref, pair_ref, dense_ref, acc_ref):
    q = pl.program_id(0)
    planes = 4 * blocks

    @pl.when(q == 0)
    def _():
        acc_ref[0:HALO] = carry_ref[...]
        acc_ref[HALO:] = jnp.zeros((planes, PAIR, GZ), jnp.float32)

    y_tab = y_ref[...]

    def step(index, _):
        for part in range(STEP):
            packed = samples_ref[index * STEP + part, 0].astype(jnp.float32)
            build(packed, y_tab, pair_ref, dense_ref, part * LANES, LANES)
        product = lax.dot_general(
            pair_ref[...], dense_ref[...], (((1,), (1,)), ((), ())), preferred_element_type=jnp.float32
        )
        here = pl.ds(4 * q, SPAN)
        acc_ref[here] = acc_ref[here] + product.reshape(SPAN, PAIR, GZ)
        return 0

    lax.fori_loop(0, ZN // STEP, step, 0)

    @pl.when(q == blocks - 1)
    def _():
        z_tab = z_ref[...]
        out = emit(acc_ref[0:planes], z_tab, None).astype(jnp.bfloat16)
        for coil in range(COILS):
            for row in range(ROWS):
                line = out[coil * ROWS + row]
                for part in range(2):
                    main_ref[
                        (row // 4) * 2 + coil // 2,
                        coil % 2,
                        part,
                        :,
                        (row % 4) * GZ : (row % 4 + 1) * GZ,
                    ] = line[:, part * GZ : (part + 1) * GZ]
        last_ref[...] = acc_ref[planes:]


def grid_chunk(samples, y_tab, z_tab, carry):
    blocks = samples.shape[1]
    planes = 4 * blocks
    return pl.pallas_call(
        lambda *refs: grid_kernel(blocks, *refs),
        grid=(blocks,),
        in_specs=[
            pl.BlockSpec((ZN, 1, 16, LANES), lambda q: (0, q, 0, 0)),
            pl.BlockSpec((2 * ROWS, GY), lambda q: (0, 0)),
            pl.BlockSpec((2 * GZ, 2 * GZ), lambda q: (0, 0)),
            pl.BlockSpec((HALO, PAIR, GZ), lambda q: (0, 0, 0)),
        ],
        out_specs=[
            pl.BlockSpec((GROUPS, 2, 2, planes, 4 * GZ), lambda q: (0, 0, 0, 0, 0)),
            pl.BlockSpec((HALO, PAIR, GZ), lambda q: (0, 0, 0)),
        ],
        out_shape=[
            jax.ShapeDtypeStruct((GROUPS, 2, 2, planes, 4 * GZ), jnp.bfloat16),
            jax.ShapeDtypeStruct((HALO, PAIR, GZ), jnp.float32),
        ],
        scratch_shapes=[
            pltpu.VMEM((SPAN * PAIR, STEP * LANES), jnp.bfloat16),
            pltpu.VMEM((GZ, STEP * LANES), jnp.bfloat16),
            pltpu.VMEM((planes + HALO, PAIR, GZ), jnp.float32),
        ],
        compiler_params=pltpu.CompilerParams(vmem_limit_bytes=48 * 2**20),
        name="grid_chunk",
    )(samples, y_tab, z_tab, carry)


def halo_kernel(last_ref, z_ref, out_ref):
    rows = emit(last_ref[...], z_ref[...], None)
    for coil in range(0, COILS, 2):
        for row in range(ROWS):
            pieces = []
            for inner in range(2):
                line = rows[(coil + inner) * ROWS + row]
                pieces += [line[:, :GZ], line[:, GZ:]]
            out_ref[(row // 4) * 2 + coil // 2, :, (row % 4) * GZ : (row % 4 + 1) * GZ] = (
                jnp.concatenate(pieces, 0).astype(jnp.bfloat16)
            )


def halo_rows(last, z_tab):
    return pl.pallas_call(
        halo_kernel,
        out_shape=jax.ShapeDtypeStruct((GROUPS, 16, 4 * GZ), jnp.bfloat16),
        compiler_params=pltpu.CompilerParams(vmem_limit_bytes=32 * 2**20),
        name="halo_rows",
    )(last, z_tab)


def combine_kernel(first_ref, second_ref, halo_ref, main_ref, edge_ref, maps_ref, out_ref):
    total = [None, None]
    edge_rows = halo_ref[...].reshape(GROUPS * 16, GZ)
    for coil in range(2):
        image = jnp.dot(
            edge_ref[coil], edge_rows, preferred_element_type=jnp.float32
        )
        for chunk, ref in enumerate((first_ref, second_ref)):
            rows = ref[:, coil].reshape(GROUPS * 32, GZ)
            image = image + jnp.dot(main_ref[chunk], rows, preferred_element_type=jnp.float32)
        image_re, image_im = image[:GX], image[GX:]
        map_re = maps_ref[coil, 0].astype(jnp.float32)
        map_im = maps_ref[coil, 1].astype(jnp.float32)
        real = map_re * image_re + map_im * image_im
        imag = map_re * image_im - map_im * image_re
        total = [real, imag] if coil == 0 else [total[0] + real, total[1] + imag]
    out_ref[0] = total[0].astype(out_ref.dtype)
    out_ref[1] = total[1].astype(out_ref.dtype)


def combine(first, second, halo, maps, dtype):
    main_tab, edge_tab = x_tables()
    return pl.pallas_call(
        combine_kernel,
        grid=(4,),
        in_specs=[
            pl.BlockSpec((GROUPS, 2, 2, 16, GZ), lambda y: (0, 0, 0, 0, y)),
            pl.BlockSpec((GROUPS, 2, 2, 16, GZ), lambda y: (0, 0, 0, 0, y)),
            pl.BlockSpec((GROUPS, 16, GZ), lambda y: (0, 0, y)),
            pl.BlockSpec((2, 2 * GX, GROUPS * 32), lambda y: (0, 0, 0)),
            pl.BlockSpec((2, 2 * GX, GROUPS * 16), lambda y: (0, 0, 0)),
            pl.BlockSpec((2, 2, GX, GZ), lambda y: (0, 0, 0, y)),
        ],
        out_specs=pl.BlockSpec((2, GX, GZ), lambda y: (0, 0, y)),
        out_shape=jax.ShapeDtypeStruct((2, GX, 4 * GZ), dtype),
        compiler_params=pltpu.CompilerParams(vmem_limit_bytes=48 * 2**20),
        name="combine",
    )(first, second, halo, jnp.asarray(main_tab), jnp.asarray(edge_tab), maps)


def pack(values, offsets, cells, slots):
    used = slots < SLOTS
    kept = jnp.where(used[None, :], values.reshape(4, SLOTS), jnp.zeros((), jnp.bfloat16))
    spots = jnp.stack([cells // (GY * GZ), cells // GZ % GY, cells % GZ], 0).astype(jnp.bfloat16)
    about = jnp.where(lax.axis_index("core") == 0, offsets, spots)
    rows = jnp.concatenate([kept, about, jnp.zeros((1, SLOTS), jnp.bfloat16)], 0)
    return rows.reshape(8, GROUPS, BLOCKS * CAP).swapaxes(0, 1)


def body(sample_values, sample_offsets, sample_cells, sample_slots, sensitivity):
    packed = pack(sample_values, sample_offsets, sample_cells, sample_slots)
    got = lax.all_to_all(packed, ("x", "core"), split_axis=0, concat_axis=0, tiled=True)
    got = got.reshape(4, 2, 8, BLOCKS, CAP).transpose(3, 1, 2, 0, 4).reshape(BLOCKS, 16, LANES)
    samples = lax.all_gather(got, "z", axis=0, tiled=False)
    y_tab = lax.dynamic_index_in_dim(jnp.asarray(y_table()), lax.axis_index("z"), 0, keepdims=False)
    z_tab = jnp.asarray(z_table())
    carry = jnp.zeros((HALO, PAIR, GZ), jnp.float32)
    parts = []
    for chunk in range(2):
        part, carry = grid_chunk(samples[:, 4 * chunk : 4 * chunk + 4], y_tab, z_tab, carry)
        parts.append(part)
    halo = halo_rows(carry, z_tab)
    turned = [
        lax.all_to_all(part, ("x", "core"), split_axis=0, concat_axis=0, tiled=True)
        for part in parts + [halo]
    ]
    maps = sensitivity.reshape(2, 2, GX, 4 * GZ)
    partial = combine(*turned, maps, jnp.float32)
    image = lax.psum_scatter(partial, ("y", "core"), scatter_dimension=1, tiled=True)
    return image.reshape(2, GX // 8, 4, GZ)


def solution(mesh):
    fine = Mesh(mesh.devices.reshape(16, 4, 4, 2), ("z", "x", "y", "core"))
    space, coil = ("z", "x"), ("y", "core")
    placed = (
        P(coil, None, space),
        P(None, space),
        P(space),
        P(space),
        P(coil, None, None, space, None),
    )
    return jax.shard_map(
        body, mesh=fine, in_specs=placed, out_specs=P(None, coil, space, None), check_vma=False
    )
```

time: 383 us -> 236 us (0.62); the launches traced: 375 us -> 234 us
  waiting for transfers between devices: 186 us -> 106 us
  local copies, waits for them, and re-layouts: 86.5 us -> 10.3 us
  blocking collectives: 0 us -> 54 us
  Pallas kernels: 0 us -> 44.9 us
  starting transfers between devices: 49.3 us -> 4.54 us
  other arithmetic: 20.6 us -> 1.73 us
  matrix products: 18.6 us -> 0 us
    all_to_all x4 -> x1, waiting for transfers between devices: 110 us -> 10.5 us  [body(): lax.all_to_all(part, ('x', 'core'), split_axis=0, concat_axis=0, tiled=True)]
    all_gather x0 -> x1, waiting for transfers between devices: none -> 60.1 us  [body(): samples = lax.all_gather(got, 'z', axis=0, tiled=False)]
    all_to_all x0 -> x3, blocking collectives: none -> 54 us  [the longest x2 39.2 us: body(): lax.all_to_all(part, ('x', 'core'), split_axis=0, concat_axis=0, tiled=True)]
    pallas_call x0 -> x4, Pallas kernels: none -> 44.9 us  [the longest x2 39.1 us: grid_chunk(): pl.pallas_call(lambda *refs: grid_kernel(blocks, *refs), grid=(blocks,),...]
    unnamed x2, waiting for transfers between devices: 40 us -> 0.03 us
    scatter x3 -> x0, local copies, waits for them, and re-layouts: 38.3 us -> none  [the longest x1 15.5 us: body(): jnp.zeros((send_dev,), jnp.int32).at[target].set(got_labels[0], mode='drop')]
    all_to_all x4 -> x1, starting transfers between devices: 40.1 us -> 4.5 us  [body(): lax.all_to_all(part, ('x', 'core'), split_axis=0, concat_axis=0, tiled=True)]
    ppermute x2 -> x0, waiting for transfers between devices: 35.5 us -> none  [from_behind(): lax.ppermute(shard, axis, [(i, (i + by) % length) for i in range(length)])]
  transfers between devices with their start and end apart: 7 -> 3, of which waited for: 5 -> 3; matrix products, arithmetic and copies ran while one was open for 13% -> 2% of each run, Pallas kernels for 0% -> 0%
where the time goes in v1:
time: 236 us; the launch traced here: 234 us
  waiting for transfers between devices  106 us (45%)
  blocking collectives  54 us (23%)
  Pallas kernels  44.9 us (19%)
  between operations  13.5 us (6%)
  local copies, waits for them, and re-layouts  10.3 us (4%)
  starting transfers between devices  4.54 us (2%)
    all_gather x1, waiting for transfers between devices, body(): samples = lax.all_gather(got, 'z', axis=0, tiled=False)  60.1 us
    all_to_all x2, blocking collectives, body(): lax.all_to_all(part, ('x', 'core'), split_axis=0, concat_axis=0, tiled=True)  39.2 us
    pallas_call x2, Pallas kernels, grid_chunk(): pl.pallas_call(lambda *refs: grid_kernel(blocks, *refs), grid=(blocks,),...  39.1 us
    reduce_scatter x1, waiting for transfers between devices, body(): lax.psum_scatter(partial, ('y', 'core'), scatter_dimension=1, tiled=True)  34.9 us
    all_to_all x1, blocking collectives, body(): lax.all_to_all(packed, ('x', 'core'), split_axis=0, concat_axis=0, tiled=...  14.8 us
    all_to_all x1, waiting for transfers between devices, body(): lax.all_to_all(part, ('x', 'core'), split_axis=0, concat_axis=0, tiled=True)  10.5 us
    pallas_call x1, Pallas kernels, combine(): pl.pallas_call(combine_kernel, grid=(4,), in_specs=[pl.BlockSpec((GROUPS,...  5.46 us
  transfers between devices with their start and end apart: 3, of which 3 were waited for; matrix products, arithmetic and copies ran while one was open for 2% of the time, Pallas kernels for 0%

profile of v1, /device:TPU:1, one launch (start us, length us, event | category | flops | bytes accessed | tf_op | source)
XLA Modules:
  0.0 234.5 jit_solution(13762395865866171523)
XLA Ops:
  6.5 0.0 copy-start
  6.5 0.0 all-gather.2.cloned.1.call-start
  6.5 0.8 broadcast_compare_fusion
  7.3 0.8 fusion.1
  8.1 0.8 reshape.16
  8.9 0.1 pad.2.clone
  9.0 0.1 maximum_select_fusion
  9.1 0.1 maximum_maximum_fusion
  9.2 14.8 %all_to_all.20 = bf16[8,8,512]{2,1,0:T(8,128)(2,1)S(1)} all-to-all(bf16[8,8,512]{2,1,0:T(8,128)(2,1)S(1)} %bitcast.8), channel_id=1, replica_groups=mesh['z'=16,'x'=4,'y'=4,'core'=2] {'x','core'}, dimensions={0} | all-to-all | bytes 131072 | tf_op jit(solution)/shard_map/all_to_all | solution.py:305
  24.0 0.1 reshape.18
  24.2 0.1 copy.11
  24.3 0.8 all_gather_reshape.3
  25.1 0.0 all-gather.2.cloned.1.call-update
  25.1 0.7 dynamic-slice_bitcast_fusion.refs_1_
  25.8 60.1 %all-gather.2.cloned.1.call-done = bf16[16,8,16,256]{3,2,1,0:T(8,128)(2,1)} async-done(((bf16[1,8,16,256]{3,2,1,0:T(8,128)(2,1)}), bf16[16,8,16,256]{3,2,1,0:T(8,128)(2,1)}) %all-gather.2.cloned.1.call-update) | async-done | bytes 1048592 | tf_op jit(solution)/shard_map/all_gather | solution.py:307
  85.9 1.3 fusion.7
  87.2 0.0 copy-done
  87.2 19.1 %grid_chunk.2 = (bf16[8,2,2,16,1024]{4,3,2,1,0:T(8,128)(2,1)S(1)}, f32[4,128,256]{2,1,0:T(8,128)S(1)}) custom-call(bf16[16,4,16,256]{3,2,1,0:T(8,128)(2,1)S(1)} %get-tuple-element.14.refs_0_, bf16[32,256]{1,0:T(8,128)(2,1)S(1)} %dynamic-slice_bitcast_fusion.refs_1_, bf16[512,512]{1,0:T(8,128)(2,1)S(1)} %copy-done, f32[4,128,256]{2,1,0:T(8,128)S(1)} %broadcast_in_dim.22.refs_3_), custom_call_target="tpu_custom_call" | custom-call | tf_op jit(solution)/shard_map/grid_chunk/pallas_call | solution.py:205
  106.3 20.0 %grid_chunk.3 = (bf16[8,2,2,16,1024]{4,3,2,1,0:T(8,128)(2,1)}, f32[4,128,256]{2,1,0:T(8,128)S(1)}) custom-call(bf16[16,4,16,256]{3,2,1,0:T(8,128)(2,1)S(1)} %get-tuple-element.13.refs_0_, bf16[32,256]{1,0:T(8,128)(2,1)S(1)} %dynamic-slice_bitcast_fusion.refs_1_, bf16[512,512]{1,0:T(8,128)(2,1)S(1)} %copy-done, f32[4,128,256]{2,1,0:T(8,128)S(1)} %get-tuple-element.10.refs_3_), custom_call_target="tpu_custom_call" | custom-call | tf_op jit(solution)/shard_map/grid_chunk/pallas_call | solution.py:205
  126.3 0.4 halo_rows.1
  126.7 20.7 %all_to_all.21.halo_ref = bf16[8,16,1024]{2,1,0:T(8,128)(2,1)S(1)} all-to-all(bf16[8,16,1024]{2,1,0:T(8,128)(2,1)S(1)} %halo_rows.1), channel_id=1, replica_groups=mesh['z'=16,'x'=4,'y'=4,'core'=2] {'x','core'}, dimensions={0} | all-to-all | bytes 524288 | tf_op jit(solution)/shard_map/all_to_all | solution.py:317
  147.4 18.5 %all_to_all.22.first_ref = bf16[8,2,2,16,1024]{4,3,2,1,0:T(8,128)(2,1)S(1)} all-to-all(bf16[8,2,2,16,1024]{4,3,2,1,0:T(8,128)(2,1)S(1)} %get-tuple-element.9), channel_id=1, replica_groups=mesh['z'=16,'x'=4,'y'=4,'core'=2] {'x','core'}, dimensions={0} | all-to-all | bytes 2097152 | tf_op jit(solution)/shard_map/all_to_all | solution.py:317
  165.9 4.5 %all-to-all-start.2 = ((bf16[8,2,2,16,1024]{4,3,2,1,0:T(8,128)(2,1)}), bf16[8,2,2,16,1024]{4,3,2,1,0:T(8,128)(2,1)S(1)}, u32[]{:S(2)}, u32[]{:S(2)}) async-start(bf16[8,2,2,16,1024]{4,3,2,1,0:T(8,128)(2,1)} %get-tuple-element.11), calls=%async_computation.2 | async-start | bytes 2097152 | tf_op jit(solution)/shard_map/all_to_all | solution.py:317
  170.4 0.0 copy-start.1
  170.4 0.0 copy-start.2
  170.4 0.0 reduce-scatter.2.cloned.1.call-start
  170.5 4.5 %reshape.19.maps_ref = bf16[2,2,256,1024]{3,2,1,0:T(8,128)(2,1)} reshape(bf16[2,2,256,4,256]{4,3,2,1,0:T(4,128)(2,1)} %param.13) | data formatting | bytes 4194304 | tf_op jit(solution)/shard_map/reshape | solution.py:320
  175.0 10.5 %all-to-all-done.2.second_ref = bf16[8,2,2,16,1024]{4,3,2,1,0:T(8,128)(2,1)S(1)} async-done(((bf16[8,2,2,16,1024]{4,3,2,1,0:T(8,128)(2,1)}), bf16[8,2,2,16,1024]{4,3,2,1,0:T(8,128)(2,1)S(1)}, u32[]{:S(2)}, u32[]{:S(2)}) %all-to-all-start.2) | async-done | bytes 1048608 | tf_op jit(solution)/shard_map/all_to_all | solution.py:317
  185.5 0.0 copy-done.1
  185.5 0.0 copy-done.2
  185.5 5.5 %combine.1 = f32[2,256,1024]{2,1,0:T(8,128)} custom-call(bf16[8,2,2,16,1024]{4,3,2,1,0:T(8,128)(2,1)S(1)} %all_to_all.22.first_ref, bf16[8,2,2,16,1024]{4,3,2,1,0:T(8,128)(2,1)S(1)} %all-to-all-done.2.second_ref, bf16[8,16,1024]{2,1,0:T(8,128)(2,1)S(1)} %all_to_all.21.halo_ref, bf16[2,512,256]{2,1,0:T(8,128)(2,1)S(1)} %copy-done.1, ...), custom_call_target="tpu_custom_call" | custom-call | tf_op jit(solution)/shard_map/combine/pallas_call | solution.py:276
  191.0 0.0 reduce-scatter.2.cloned.1.call-update
  191.0 34.9 %reduce-scatter.2.cloned.1.call-done = f32[2,32,1024]{2,1,0:T(8,128)} async-done(((f32[2,256,1024]{2,1,0:T(8,128)}), f32[2,32,1024]{2,1,0:T(8,128)}) %reduce-scatter.2.cloned.1.call-update) | async-done | bytes 262160 | tf_op jit(solution)/shard_map/reduce_scatter | solution.py:322
  225.9 1.8 reshape.20
  (5 shorter events, 0.1 us)
Async XLA Ops:
  6.5 80.7 %copy-start = (bf16[512,512]{1,0:T(8,128)(2,1)S(1)}, bf16[512,512]{1,0:T(8,128)(2,1)}, u32[]{:S(2)}) copy-start(bf16[512,512]{1,0:T(8,128)(2,1)} %constant.75.clone.refs_2_.z_ref) | copy-start | bytes 1572868
  6.5 79.3 %all-gather.2.cloned.1.call-start = ((), (), s32[]{:S(2)}) async-start(), calls=%async_computation.5 | async-start | bytes 1114112 | tf_op jit(solution)/shard_map/all_gather | solution.py:307
  165.9 19.6 %all-to-all-start.2 = ((bf16[8,2,2,16,1024]{4,3,2,1,0:T(8,128)(2,1)}), bf16[8,2,2,16,1024]{4,3,2,1,0:T(8,128)(2,1)S(1)}, u32[]{:S(2)}, u32[]{:S(2)}) async-start(bf16[8,2,2,16,1024]{4,3,2,1,0:T(8,128)(2,1)} %get-tuple-element.11), calls=%async_computation.2 | async-start | bytes 2097152 | tf_op jit(solution)/shard_map/all_to_all | solution.py:317
  170.4 15.1 %copy-start.1 = (bf16[2,512,256]{2,1,0:T(8,128)(2,1)S(1)}, bf16[2,512,256]{2,1,0:T(8,128)(2,1)}, u32[]{:S(2)}) copy-start(bf16[2,512,256]{2,1,0:T(8,128)(2,1)} %constant.76.clone.main_ref) | copy-start | bytes 1572868
  170.4 15.1 %copy-start.2 = (bf16[2,512,128]{2,1,0:T(8,128)(2,1)S(1)}, bf16[2,512,128]{2,1,0:T(8,128)(2,1)}, u32[]{:S(2)}) copy-start(bf16[2,512,128]{2,1,0:T(8,128)(2,1)} %constant.77.clone.edge_ref) | copy-start | bytes 786436
  170.4 55.5 %reduce-scatter.2.cloned.1.call-start = ((), (), s32[]{:S(2)}) async-start(), calls=%async_computation.6 | async-start | bytes 2359296 | tf_op jit(solution)/shard_map/reduce_scatter | solution.py:322
Sparse Core Ops, SparseCore 0:
  25.2 60.6 all-gather.1
  191.1 34.6 reduce-scatter.1

commit v2 on v1

v2 whole, which is shorter than its diff:
```python
import math

import jax
import jax.numpy as jnp
import ml_dtypes
import numpy as np
from jax import lax
from jax.experimental import pallas as pl
from jax.experimental.pallas import tpu as pltpu
from jax.sharding import Mesh
from jax.sharding import PartitionSpec as P

GX = 256
GY = 256
GZ = 256
SLOTS = 4096
CAP = 64

BETA = 9.0
TERMS = 31

ZH = 8
GROUPS = 16
BLOCKS = 4
CHUNKS = 2
LANES = 512
STEP = 2
COILS = 4
ROWS = 32
TAPS = 4
SPAN = 7
PAIR = 2 * COILS * ROWS
HALF = PAIR // 2
PLANES = 8
HALO = 4


def series():
    quarter = 0.25 * BETA * BETA
    terms = [quarter**k / float(math.factorial(k)) ** 2 for k in range(TERMS)]
    total = math.fsum(terms)
    return [float(np.float32(t / total)) for t in terms]


def waves():
    counter = np.arange(256)
    phase = (counter[:, None] * counter[None, :] % 256).astype(np.float32) * np.float32(
        2.0 * math.pi / 256
    )
    scale = np.float32(1.0 / 16.0)
    both = np.stack([np.cos(phase) * scale, np.sin(phase) * scale], 0)
    return both.astype(ml_dtypes.bfloat16).astype(np.float32)


def z_table():
    cosine, sine = waves()
    return np.block([[cosine, sine], [-sine, cosine]]).astype(ml_dtypes.bfloat16)


def y_table():
    both = waves().reshape(2, ZH, ROWS, 256)
    return both.transpose(1, 0, 2, 3).reshape(ZH, 2 * ROWS, 256).astype(ml_dtypes.bfloat16)


def x_columns(planes, part):
    cosine, sine = waves()
    if part == 0:
        return np.concatenate([cosine[:, planes], sine[:, planes]], 0)
    return np.concatenate([-sine[:, planes], cosine[:, planes]], 0)


def x_tables():
    main = []
    for chunk in range(CHUNKS):
        cols = []
        for group in range(GROUPS):
            planes = (16 * group + PLANES * chunk + np.arange(PLANES) - 1) % GX
            cols += [x_columns(planes, 0), x_columns(planes, 1)]
        main.append(np.concatenate(cols, 1))
    halo = []
    for coil in range(2):
        cols = []
        for group in range(GROUPS):
            planes = (16 * group + 16 + np.arange(HALO) - 1) % GX
            real = np.arange(HALO) < 3
            for other in range(2):
                keep = real & (other == coil)
                cols += [x_columns(planes, part) * keep for part in range(2)]
        halo.append(np.concatenate(cols, 1))
    return np.stack(main).astype(ml_dtypes.bfloat16), np.stack(halo).astype(ml_dtypes.bfloat16)


def tap_rows(first, second, lanes):
    row = lax.broadcasted_iota(jnp.int32, (8, lanes), 0)
    offset = jnp.where(row < TAPS, first, second)
    distance = offset + (1.0 - (row % TAPS).astype(jnp.float32))
    inner = jnp.maximum(1.0 - 0.25 * distance * distance, 0.0)
    coefficients = series()
    total = jnp.full((8, lanes), coefficients[-1], jnp.float32)
    for value in coefficients[-2::-1]:
        total = total * inner + value
    return total


def dense_rows(weights, base, lanes):
    high = base // 16
    low = base % 16
    row = lax.broadcasted_iota(jnp.int32, (16, lanes), 0)
    pattern = jnp.zeros((16, lanes), jnp.float32)
    for tap in range(TAPS):
        pattern = jnp.where(row == (low + tap) % 16, weights[tap], pattern)
    place = jnp.where(row < low, (high + 1) % 16, high).astype(jnp.float32)
    pattern = pattern.astype(jnp.bfloat16)
    place = place.astype(jnp.bfloat16)
    zero = jnp.zeros((16, lanes), jnp.bfloat16)
    return [
        jnp.where(place == jnp.bfloat16(block), pattern, zero) for block in range(16)
    ]


def build(packed, y_tab, pair_ref, dense_ref, at, lanes):
    taps_xy = tap_rows(packed[4:5], packed[5:6], lanes)
    taps_z = tap_rows(packed[6:7], packed[6:7], lanes)
    cell = packed.astype(jnp.int32)
    base_x = cell[12:13]
    base_y = (cell[13:14] + 255) % 256
    base_z = (cell[14:15] + 255) % 256
    z_blocks = dense_rows([taps_z[t : t + 1] for t in range(TAPS)], base_z, lanes)
    for block in range(16):
        dense_ref[block * 16 : (block + 1) * 16, at : at + lanes] = z_blocks[block]
    y_blocks = dense_rows([taps_xy[4 + t : 5 + t] for t in range(TAPS)], base_y, lanes)
    turn = jnp.dot(y_tab, jnp.concatenate(y_blocks, 0), preferred_element_type=jnp.float32)
    turn_re, turn_im = turn[:ROWS], turn[ROWS:]
    real, imag = [], []
    for coil in range(COILS):
        row = (coil // 2) * 8 + (coil % 2) * 2
        value_re, value_im = packed[row : row + 1], packed[row + 1 : row + 2]
        real.append((value_re * turn_re - value_im * turn_im).astype(jnp.bfloat16))
        imag.append((value_re * turn_im + value_im * turn_re).astype(jnp.bfloat16))
    values = real + imag
    row = lax.broadcasted_iota(jnp.int32, (8, lanes), 0)
    dense_x = jnp.zeros((8, lanes), jnp.float32)
    for tap in range(TAPS):
        dense_x = jnp.where(row == base_x + tap, taps_xy[tap : tap + 1], dense_x)
    for plane in range(SPAN):
        weight = jnp.broadcast_to(dense_x[plane : plane + 1], (ROWS, lanes)).astype(jnp.bfloat16)
        for part in range(2 * COILS):
            start = plane * PAIR + part * ROWS
            pair_ref[start : start + ROWS, at : at + lanes] = values[part] * weight


def transform_z(grid_planes, z_tab):
    planes = grid_planes.shape[0]
    grid = grid_planes.astype(jnp.bfloat16)
    joined = jnp.concatenate([grid[:, :HALF], grid[:, HALF:]], axis=2)
    along = jnp.dot(
        joined.reshape(planes * HALF, 2 * GZ), z_tab, preferred_element_type=jnp.float32
    )
    return jnp.swapaxes(along.reshape(planes, HALF, 2 * GZ), 0, 1)


def grid_kernel(last, samples_ref, y_ref, z_ref, carry_ref, out_ref, carried_ref, pair_ref, dense_ref, acc_ref):
    q = pl.program_id(0)

    @pl.when(q == 0)
    def _():
        acc_ref[0:HALO] = carry_ref[...]
        acc_ref[HALO:] = jnp.zeros((PLANES, PAIR, GZ), jnp.float32)

    y_tab = y_ref[...]

    def step(index, _):
        for part in range(STEP):
            packed = samples_ref[index * STEP + part, 0].astype(jnp.float32)
            build(packed, y_tab, pair_ref, dense_ref, part * LANES, LANES)
        product = lax.dot_general(
            pair_ref[...], dense_ref[...], (((1,), (1,)), ((), ())), preferred_element_type=jnp.float32
        )
        here = pl.ds(4 * q, SPAN)
        acc_ref[here] = acc_ref[here] + product.reshape(SPAN, PAIR, GZ)
        return 0

    lax.fori_loop(0, ZH // STEP, step, 0)

    @pl.when(q == BLOCKS // CHUNKS - 1)
    def _():
        z_tab = z_ref[...]
        lines = transform_z(acc_ref[0:PLANES], z_tab)
        for coil in range(COILS):
            for row in range(ROWS):
                line = lines[coil * ROWS + row]
                both = jnp.concatenate([line[:, :GZ], line[:, GZ:]], 0).astype(jnp.bfloat16)
                out_ref[
                    (row // 4) * 2 + coil // 2, coil % 2, :, (row % 4) * GZ : (row % 4 + 1) * GZ
                ] = both
        if last:
            edge = transform_z(acc_ref[PLANES:], z_tab)
            for coil in range(0, COILS, 2):
                for row in range(ROWS):
                    pieces = []
                    for inner in range(2):
                        line = edge[(coil + inner) * ROWS + row]
                        pieces += [line[:, :GZ], line[:, GZ:]]
                    out_ref[
                        (row // 4) * 2 + coil // 2, 2, :, (row % 4) * GZ : (row % 4 + 1) * GZ
                    ] = jnp.concatenate(pieces, 0).astype(jnp.bfloat16)
        else:
            carried_ref[...] = acc_ref[PLANES:]


def grid_chunk(samples, y_tab, z_tab, carry, chunk):
    blocks = BLOCKS // CHUNKS
    last = chunk == CHUNKS - 1
    tiles = 3 if last else 2
    flops = 2 * SPAN * PAIR * GZ * ZH * LANES * blocks + 2 * PLANES * PAIR * GZ * 2 * GZ
    return pl.pallas_call(
        lambda *refs: grid_kernel(last, *refs),
        grid=(blocks,),
        in_specs=[
            pl.BlockSpec((ZH, 1, 16, LANES), lambda q: (0, q + chunk * blocks, 0, 0)),
            pl.BlockSpec((2 * ROWS, GY), lambda q: (0, 0)),
            pl.BlockSpec((2 * GZ, 2 * GZ), lambda q: (0, 0)),
            pl.BlockSpec((HALO, PAIR, GZ), lambda q: (0, 0, 0)),
        ],
        out_specs=[
            pl.BlockSpec((GROUPS, tiles, 16, 4 * GZ), lambda q: (0, 0, 0, 0)),
            pl.BlockSpec((HALO, PAIR, GZ), lambda q: (0, 0, 0)),
        ],
        out_shape=[
            jax.ShapeDtypeStruct((GROUPS, tiles, 16, 4 * GZ), jnp.bfloat16),
            jax.ShapeDtypeStruct((HALO, PAIR, GZ), jnp.float32),
        ],
        scratch_shapes=[
            pltpu.VMEM((SPAN * PAIR, STEP * LANES), jnp.bfloat16),
            pltpu.VMEM((GZ, STEP * LANES), jnp.bfloat16),
            pltpu.VMEM((PLANES + HALO, PAIR, GZ), jnp.float32),
        ],
        compiler_params=pltpu.CompilerParams(vmem_limit_bytes=48 * 2**20),
        cost_estimate=pl.CostEstimate(
            flops=flops, bytes_accessed=4 * 2**20, transcendentals=0
        ),
        name="grid_chunk",
    )(samples, y_tab, z_tab, carry)


def combine_kernel(first_ref, second_ref, main_ref, edge_ref, maps_ref, out_ref):
    total = [None, None]
    depth = GROUPS * 16
    edge_rows = second_ref[:, 2].reshape(depth, GZ)
    for coil in range(2):
        image = jnp.dot(edge_ref[coil], edge_rows, preferred_element_type=jnp.float32)
        for chunk, ref in enumerate((first_ref, second_ref)):
            rows = ref[:, coil].reshape(depth, GZ)
            image = image + jnp.dot(main_ref[chunk], rows, preferred_element_type=jnp.float32)
        image_re, image_im = image[:GX], image[GX:]
        map_re = maps_ref[coil, 0].astype(jnp.float32)
        map_im = maps_ref[coil, 1].astype(jnp.float32)
        real = map_re * image_re + map_im * image_im
        imag = map_re * image_im - map_im * image_re
        total = [real, imag] if coil == 0 else [total[0] + real, total[1] + imag]
    for part in range(2):
        out_ref[:, part] = total[part].astype(jnp.bfloat16).reshape(8, GX // 8, GZ)


def combine(first, second, maps):
    main_tab, edge_tab = x_tables()
    depth = GROUPS * 16
    return pl.pallas_call(
        combine_kernel,
        grid=(4,),
        in_specs=[
            pl.BlockSpec((GROUPS, 2, 16, GZ), lambda y: (0, 0, 0, y)),
            pl.BlockSpec((GROUPS, 3, 16, GZ), lambda y: (0, 0, 0, y)),
            pl.BlockSpec((CHUNKS, 2 * GX, depth), lambda y: (0, 0, 0)),
            pl.BlockSpec((2, 2 * GX, depth), lambda y: (0, 0, 0)),
            pl.BlockSpec((2, 2, GX, GZ), lambda y: (0, 0, 0, y)),
        ],
        out_specs=pl.BlockSpec((8, 2, GX // 8, GZ), lambda y: (0, 0, 0, y)),
        out_shape=jax.ShapeDtypeStruct((8, 2, GX // 8, 4 * GZ), jnp.bfloat16),
        compiler_params=pltpu.CompilerParams(vmem_limit_bytes=48 * 2**20),
        cost_estimate=pl.CostEstimate(
            flops=2 * 2 * 2 * GX * 3 * depth * 4 * GZ, bytes_accessed=8 * 2**20, transcendentals=0
        ),
        name="combine",
    )(first, second, jnp.asarray(main_tab), jnp.asarray(edge_tab), maps)


def pack(values, offsets, cells, slots):
    used = slots < SLOTS
    kept = jnp.where(used[None, :], values.reshape(4, SLOTS), jnp.zeros((), jnp.bfloat16))
    spots = jnp.stack([cells // (GY * GZ), cells // GZ % GY, cells % GZ], 0).astype(jnp.bfloat16)
    about = jnp.where(lax.axis_index("core") == 0, offsets, spots)
    rows = jnp.concatenate([kept, about, jnp.zeros((1, SLOTS), jnp.bfloat16)], 0)
    return rows.reshape(8, GROUPS, BLOCKS * CAP).swapaxes(0, 1)


def turn(array, axes):
    return lax.all_to_all(array, axes, split_axis=0, concat_axis=0, tiled=True)


def body(sample_values, sample_offsets, sample_cells, sample_slots, sensitivity):
    packed = pack(sample_values, sample_offsets, sample_cells, sample_slots)
    planes = ("zl", "x", "core")
    got = turn(packed, planes)
    got = got.reshape(8, 2, 8, BLOCKS, CAP).transpose(3, 1, 2, 0, 4).reshape(BLOCKS, 16, LANES)
    samples = turn(jnp.broadcast_to(got[None], (ZH,) + got.shape), "zh")
    y_tab = lax.dynamic_index_in_dim(
        jnp.asarray(y_table()), lax.axis_index("zh"), 0, keepdims=False
    )
    z_tab = jnp.asarray(z_table())
    carry = jnp.zeros((HALO, PAIR, GZ), jnp.float32)
    turned = []
    for chunk in range(CHUNKS):
        part, carry = grid_chunk(samples, y_tab, z_tab, carry, chunk)
        turned.append(turn(part, planes))
    maps = sensitivity.reshape(2, 2, GX, 4 * GZ)
    partial = turn(combine(*turned, maps), ("y", "core"))
    image = jnp.sum(partial.astype(jnp.float32), axis=0)
    return image.reshape(2, GX // 8, 4, GZ)


def solution(mesh):
    fine = Mesh(mesh.devices.reshape(8, 2, 4, 4, 2), ("zh", "zl", "x", "y", "core"))
    space, coil = ("zh", "zl", "x"), ("y", "core")
    placed = (
        P(coil, None, space),
        P(None, space),
        P(space),
        P(space),
        P(coil, None, None, space, None),
    )
    return jax.shard_map(
        body, mesh=fine, in_specs=placed, out_specs=P(None, coil, space, None), check_vma=False
    )
```

time: 236 us -> 154 us (0.65)
  waiting for transfers between devices: 106 us -> 46.3 us
  starting transfers between devices: 4.54 us -> 22.8 us
  blocking collectives: 54 us -> 36.1 us
  between operations: 13.5 us -> 0.11 us
  Pallas kernels: 44.9 us -> 35.3 us
    all_gather x1 -> x0, waiting for transfers between devices: 60.1 us -> none  [body(): samples = lax.all_gather(got, 'z', axis=0, tiled=False)]
    all_to_all x1 -> x3, waiting for transfers between devices: 10.5 us -> 46.3 us  [turn(): return lax.all_to_all(array, axes, split_axis=0, concat_axis=0, tiled=True)]
    reduce_scatter x1 -> x0, waiting for transfers between devices: 34.9 us -> none  [body(): lax.psum_scatter(partial, ('y', 'core'), scatter_dimension=1, tiled=True)]
    all_to_all x1 -> x3, starting transfers between devices: 4.5 us -> 22.8 us  [turn(): return lax.all_to_all(array, axes, split_axis=0, concat_axis=0, tiled=True)]
    all_to_all x3 -> x2, blocking collectives: 54 us -> 36.1 us  [turn(): return lax.all_to_all(array, axes, split_axis=0, concat_axis=0, tiled=True)]
    pallas_call x3 -> x2, Pallas kernels: 39.5 us -> 30.7 us  [grid_chunk(): pl.pallas_call(lambda *refs: grid_kernel(last, *refs), grid=(blocks,), in...]
  transfers between devices with their start and end apart: 3 -> 3, of which waited for: 3 -> 2; matrix products, arithmetic and copies ran while one was open for 2% -> 3% of each run, Pallas kernels for 0% -> 10%
where the time goes in v2:
time: 154 us; the launch traced here: 153 us
  waiting for transfers between devices  46.3 us (30%)
  blocking collectives  36.1 us (23%)
  Pallas kernels  35.3 us (23%)
  starting transfers between devices  22.8 us (15%)
  local copies, waits for them, and re-layouts  10.5 us (7%)
  other arithmetic  1.9 us (1%)
    all_to_all x3, waiting for transfers between devices, turn(): return lax.all_to_all(array, axes, split_axis=0, concat_axis=0, tiled=True)  46.3 us
    all_to_all x2, blocking collectives, turn(): return lax.all_to_all(array, axes, split_axis=0, concat_axis=0, tiled=True)  36.1 us
    pallas_call x2, Pallas kernels, grid_chunk(): pl.pallas_call(lambda *refs: grid_kernel(last, *refs), grid=(blocks,), in...  30.7 us
    all_to_all x3, starting transfers between devices, turn(): return lax.all_to_all(array, axes, split_axis=0, concat_axis=0, tiled=True)  22.8 us
    pallas_call x1, Pallas kernels, combine(): pl.pallas_call(combine_kernel, grid=(4,), in_specs=[pl.BlockSpec((GROUPS,...  4.59 us
    reshape x1, local copies, waits for them, and re-layouts, body(): maps = sensitivity.reshape(2, 2, GX, 4 * GZ)  4.49 us
  transfers between devices with their start and end apart: 3, of which 2 were waited for; matrix products, arithmetic and copies ran while one was open for 3% of the time, Pallas kernels for 10%

profile of v2, /device:TPU:1, one launch (start us, length us, event | category | flops | bytes accessed | tf_op | source)
XLA Modules:
  0.0 153.0 jit_solution(11094636805031054301)
XLA Ops:
  0.0 0.0 copy-start.3
  0.0 0.8 broadcast_compare_fusion
  0.8 0.8 fusion.1
  1.6 0.8 reshape.17
  2.4 0.1 pad.2.clone
  2.5 0.1 maximum_select_fusion
  2.6 0.1 maximum_maximum_fusion
  2.7 15.9 %all_to_all.25 = bf16[16,8,256]{2,1,0:T(8,128)(2,1)S(1)} all-to-all(bf16[16,8,256]{2,1,0:T(8,128)(2,1)S(1)} %bitcast.10), channel_id=1, replica_groups=mesh['zh'=8,'zl'=2,'x'=4,'y'=4,'core'=2] {'zl','x','core'}, dimensions={0} | all-to-all | bytes 131072 | tf_op jit(solution)/shard_map/all_to_all | solution.py:298
  18.6 0.1 reshape.19
  18.7 0.1 copy.10
  18.8 0.1 broadcast_in_dim.29
  18.9 0.9 broadcast_in_dim.30
  19.8 11.5 %all-to-all-start.1 = ((bf16[8,4,16,512]{3,2,1,0:T(8,128)(2,1)}), bf16[8,4,16,512]{3,2,1,0:T(8,128)(2,1)S(1)}, u32[]{:S(2)}, u32[]{:S(2)}) async-start(bf16[8,4,16,512]{3,2,1,0:T(8,128)(2,1)} %broadcast_in_dim.30), calls=%async_computation.1 | async-start | bytes 1048576 | tf_op jit(solution)/shard_map/all_to_all | solution.py:298
  31.3 0.8 dynamic-slice_bitcast_fusion.refs_1_
  32.1 29.0 %all-to-all-done.1.refs_0_ = bf16[8,4,16,512]{3,2,1,0:T(8,128)(2,1)S(1)} async-done(((bf16[8,4,16,512]{3,2,1,0:T(8,128)(2,1)}), bf16[8,4,16,512]{3,2,1,0:T(8,128)(2,1)S(1)}, u32[]{:S(2)}, u32[]{:S(2)}) %all-to-all-start.1) | async-done | bytes 524320 | tf_op jit(solution)/shard_map/all_to_all | solution.py:298
  61.1 0.1 broadcast_in_dim.31.refs_3_
  61.2 0.0 copy-done.3
  61.2 15.1 %grid_chunk.2 = (bf16[16,2,16,1024]{3,2,1,0:T(8,128)(2,1)}, f32[4,256,256]{2,1,0:T(8,128)S(1)}) custom-call(bf16[8,4,16,512]{3,2,1,0:T(8,128)(2,1)S(1)} %all-to-all-done.1.refs_0_, bf16[64,256]{1,0:T(8,128)(2,1)S(1)} %dynamic-slice_bitcast_fusion.refs_1_, bf16[512,512]{1,0:T(8,128)(2,1)S(1)} %copy-done.3, f32[4,256,256]{2,1,0:T(8,128)S(1)} %broadcast_in_dim.31.refs_3_), custom_call_target="tpu_custom_call" | custom-call | flops 8053063680 | bytes 4194304 | tf_op jit(solution)/shard_map/grid_chunk/pallas_call | solution.py:216
  76.3 5.5 %all-to-all-start.2 = ((bf16[16,2,16,1024]{3,2,1,0:T(8,128)(2,1)}), bf16[16,2,16,1024]{3,2,1,0:T(8,128)(2,1)S(1)}, u32[]{:S(2)}, u32[]{:S(2)}) async-start(bf16[16,2,16,1024]{3,2,1,0:T(8,128)(2,1)} %get-tuple-element.8), calls=%async_computation.2 | async-start | bytes 2097152 | tf_op jit(solution)/shard_map/all_to_all | solution.py:298
  81.8 15.6 %grid_chunk.3 = (bf16[16,3,16,1024]{3,2,1,0:T(8,128)(2,1)S(1)}, f32[4,256,256]{2,1,0:T(8,128)}) custom-call(bf16[8,4,16,512]{3,2,1,0:T(8,128)(2,1)S(1)} %all-to-all-done.1.refs_0_, bf16[64,256]{1,0:T(8,128)(2,1)S(1)} %dynamic-slice_bitcast_fusion.refs_1_, bf16[512,512]{1,0:T(8,128)(2,1)S(1)} %copy-done.3, f32[4,256,256]{2,1,0:T(8,128)S(1)} %get-tuple-element.9.refs_3_), custom_call_target="tpu_custom_call" | custom-call | flops 8053063680 | bytes 4194304 | tf_op jit(solution)/shard_map/grid_chunk/pallas_call | solution.py:216
  97.4 0.0 copy-start
  97.4 1.2 copy-done
  98.5 0.0 all-to-all-done.2.first_ref
  98.5 5.8 %all-to-all-start.3 = ((bf16[16,3,16,1024]{3,2,1,0:T(8,128)(2,1)}), bf16[16,3,16,1024]{3,2,1,0:T(8,128)(2,1)S(1)}, u32[]{:S(2)}, u32[]{:S(2)}) async-start(bf16[16,3,16,1024]{3,2,1,0:T(8,128)(2,1)} %copy-done), calls=%async_computation.3 | async-start | bytes 3145728 | tf_op jit(solution)/shard_map/all_to_all | solution.py:298
  104.3 0.0 copy-start.1
  104.3 4.5 %reshape.20.maps_ref = bf16[2,2,256,1024]{3,2,1,0:T(8,128)(2,1)} reshape(bf16[2,2,256,4,256]{4,3,2,1,0:T(4,128)(2,1)} %param.13) | data formatting | bytes 4194304 | tf_op jit(solution)/shard_map/reshape | solution.py:316
  108.8 17.3 %all-to-all-done.3.second_ref = bf16[16,3,16,1024]{3,2,1,0:T(8,128)(2,1)S(1)} async-done(((bf16[16,3,16,1024]{3,2,1,0:T(8,128)(2,1)}), bf16[16,3,16,1024]{3,2,1,0:T(8,128)(2,1)S(1)}, u32[]{:S(2)}, u32[]{:S(2)}) %all-to-all-start.3) | async-done | bytes 1572896 | tf_op jit(solution)/shard_map/all_to_all | solution.py:298
  126.1 0.0 copy-done.1
  126.1 0.0 copy-start.2
  126.1 1.0 copy-done.2
  127.2 4.6 %combine.1 = bf16[8,2,32,1024]{3,2,1,0:T(8,128)(2,1)S(1)} custom-call(bf16[16,2,16,1024]{3,2,1,0:T(8,128)(2,1)S(1)} %all-to-all-done.2.first_ref, bf16[16,3,16,1024]{3,2,1,0:T(8,128)(2,1)S(1)} %all-to-all-done.3.second_ref, bf16[2,512,256]{2,1,0:T(8,128)(2,1)S(1)} %copy-done.2, bf16[2,512,256]{2,1,0:T(8,128)(2,1)S(1)} %copy-done.1, ...), custom_call_target="tpu_custom_call" | custom-call | flops 1610612736 | bytes 8388608 | tf_op jit(solution)/shard_map/combine/pallas_call | solution.py:268
  131.8 20.2 %all_to_all.26 = bf16[8,2,32,1024]{3,2,1,0:T(8,128)(2,1)S(1)} all-to-all(bf16[8,2,32,1024]{3,2,1,0:T(8,128)(2,1)S(1)} %combine.1), channel_id=1, replica_groups=mesh['zh'=8,'zl'=2,'x'=4,'y'=4,'core'=2] {'y','core'}, dimensions={0} | all-to-all | bytes 2097152 | tf_op jit(solution)/shard_map/all_to_all | solution.py:298
  152.0 0.2 convert_reduce_fusion
  152.2 0.8 reshape.21
  (4 shorter events, 0.1 us)
Async XLA Ops:
  0.0 61.2 %copy-start.3 = (bf16[512,512]{1,0:T(8,128)(2,1)S(1)}, bf16[512,512]{1,0:T(8,128)(2,1)}, u32[]{:S(2)}) copy-start(bf16[512,512]{1,0:T(8,128)(2,1)} %constant.76.clone.refs_2_) | copy-start | bytes 1572868
  19.8 41.3 %all-to-all-start.1 = ((bf16[8,4,16,512]{3,2,1,0:T(8,128)(2,1)}), bf16[8,4,16,512]{3,2,1,0:T(8,128)(2,1)S(1)}, u32[]{:S(2)}, u32[]{:S(2)}) async-start(bf16[8,4,16,512]{3,2,1,0:T(8,128)(2,1)} %broadcast_in_dim.30), calls=%async_computation.1 | async-start | bytes 1048576 | tf_op jit(solution)/shard_map/all_to_all | solution.py:298
  76.3 22.3 %all-to-all-start.2 = ((bf16[16,2,16,1024]{3,2,1,0:T(8,128)(2,1)}), bf16[16,2,16,1024]{3,2,1,0:T(8,128)(2,1)S(1)}, u32[]{:S(2)}, u32[]{:S(2)}) async-start(bf16[16,2,16,1024]{3,2,1,0:T(8,128)(2,1)} %get-tuple-element.8), calls=%async_computation.2 | async-start | bytes 2097152 | tf_op jit(solution)/shard_map/all_to_all | solution.py:298
  97.4 1.2 copy-start
  98.5 27.6 %all-to-all-start.3 = ((bf16[16,3,16,1024]{3,2,1,0:T(8,128)(2,1)}), bf16[16,3,16,1024]{3,2,1,0:T(8,128)(2,1)S(1)}, u32[]{:S(2)}, u32[]{:S(2)}) async-start(bf16[16,3,16,1024]{3,2,1,0:T(8,128)(2,1)} %copy-done), calls=%async_computation.3 | async-start | bytes 3145728 | tf_op jit(solution)/shard_map/all_to_all | solution.py:298
  104.3 21.8 %copy-start.1 = (bf16[2,512,256]{2,1,0:T(8,128)(2,1)S(1)}, bf16[2,512,256]{2,1,0:T(8,128)(2,1)}, u32[]{:S(2)}) copy-start(bf16[2,512,256]{2,1,0:T(8,128)(2,1)} %constant.78.clone.edge_ref) | copy-start | bytes 1572868
  126.1 1.0 copy-start.2

commit v3 on v2

--- a/solution.py
+++ b/solution.py
@@ -23,15 +23,15 @@
 GROUPS = 16
 BLOCKS = 4
 CHUNKS = 2
+QS = BLOCKS // CHUNKS
+SOURCES = 64
 LANES = 512
 STEP = 2
 COILS = 4
 ROWS = 32
 TAPS = 4
 SPAN = 7
-PAIR = 2 * COILS * ROWS
-HALF = PAIR // 2
-PLANES = 8
+PLANES = 4 * QS
 HALO = 4
 
 
@@ -57,9 +57,14 @@
     return np.block([[cosine, sine], [-sine, cosine]]).astype(ml_dtypes.bfloat16)
 
 
-def y_table():
-    both = waves().reshape(2, ZH, ROWS, 256)
-    return both.transpose(1, 0, 2, 3).reshape(ZH, 2 * ROWS, 256).astype(ml_dtypes.bfloat16)
+def row_order(part):
+    rows = [4 * owner + 2 * half + e for half in range(2) for owner in range(8) for e in range(2)]
+    return rows if part is None else rows[16 * part : 16 * part + 16]
+
+
+def y_table(part):
+    both = waves().reshape(2, ZH, ROWS, 256)[:, :, row_order(part)]
+    return both.transpose(1, 0, 2, 3).reshape(ZH, -1, 256).astype(ml_dtypes.bfloat16)
 
 
 def x_columns(planes, part):
@@ -118,7 +123,20 @@
     ]
 
 
+def gather(samples_ref, start, q):
+    lane = lax.broadcasted_iota(jnp.int32, (16, 2 * CAP), 1)
+    pieces = []
+    for pair in range(LANES // (2 * CAP)):
+        first = samples_ref[start + 2 * pair].astype(jnp.float32)
+        second = samples_ref[start + 2 * pair + 1].astype(jnp.float32)
+        first = jnp.where(q == 0, first, pltpu.roll(first, CAP, 1))
+        second = jnp.where(q == 0, pltpu.roll(second, CAP, 1), second)
+        pieces.append(jnp.where(lane < CAP, first, second))
+    return jnp.concatenate(pieces, 1)
+
+
 def build(packed, y_tab, pair_ref, dense_ref, at, lanes):
+    rows = y_tab.shape[0] // 2
     taps_xy = tap_rows(packed[4:5], packed[5:6], lanes)
     taps_z = tap_rows(packed[6:7], packed[6:7], lanes)
     cell = packed.astype(jnp.int32)
@@ -130,7 +148,7 @@
         dense_ref[block * 16 : (block + 1) * 16, at : at + lanes] = z_blocks[block]
     y_blocks = dense_rows([taps_xy[4 + t : 5 + t] for t in range(TAPS)], base_y, lanes)
     turn = jnp.dot(y_tab, jnp.concatenate(y_blocks, 0), preferred_element_type=jnp.float32)
-    turn_re, turn_im = turn[:ROWS], turn[ROWS:]
+    turn_re, turn_im = turn[:rows], turn[rows:]
     real, imag = [], []
     for coil in range(COILS):
         row = (coil // 2) * 8 + (coil % 2) * 2
@@ -143,104 +161,121 @@
     for tap in range(TAPS):
         dense_x = jnp.where(row == base_x + tap, taps_xy[tap : tap + 1], dense_x)
     for plane in range(SPAN):
-        weight = jnp.broadcast_to(dense_x[plane : plane + 1], (ROWS, lanes)).astype(jnp.bfloat16)
+        weight = jnp.broadcast_to(dense_x[plane : plane + 1], (rows, lanes)).astype(jnp.bfloat16)
         for part in range(2 * COILS):
-            start = plane * PAIR + part * ROWS
-            pair_ref[start : start + ROWS, at : at + lanes] = values[part] * weight
+            start = (plane * 2 * COILS + part) * rows
+            pair_ref[start : start + rows, at : at + lanes] = values[part] * weight
 
 
 def transform_z(grid_planes, z_tab):
-    planes = grid_planes.shape[0]
+    planes, _, rows, _ = grid_planes.shape
+    half = COILS * rows
     grid = grid_planes.astype(jnp.bfloat16)
-    joined = jnp.concatenate([grid[:, :HALF], grid[:, HALF:]], axis=2)
-    along = jnp.dot(
-        joined.reshape(planes * HALF, 2 * GZ), z_tab, preferred_element_type=jnp.float32
+    joined = jnp.concatenate(
+        [
+            grid[:, :COILS].reshape(planes * half, GZ),
+            grid[:, COILS:].reshape(planes * half, GZ),
+        ],
+        axis=1,
     )
-    return jnp.swapaxes(along.reshape(planes, HALF, 2 * GZ), 0, 1)
-
-
-def grid_kernel(last, samples_ref, y_ref, z_ref, carry_ref, out_ref, carried_ref, pair_ref, dense_ref, acc_ref):
+    along = jnp.dot(joined, z_tab, preferred_element_type=jnp.float32)
+    return jnp.swapaxes(along.reshape(planes, half, 2 * GZ), 0, 1)
+
+
+def grid_kernel(last, samples_ref, y_ref, z_ref, *refs):
+    if last:
+        carry_ref, out_ref, pair_ref, dense_ref, acc_ref = refs
+    else:
+        out_ref, carried_ref, pair_ref, dense_ref, acc_ref = refs
     q = pl.program_id(0)
+    rows = y_ref.shape[0] // 2
 
     @pl.when(q == 0)
     def _():
-        acc_ref[0:HALO] = carry_ref[...]
-        acc_ref[HALO:] = jnp.zeros((PLANES, PAIR, GZ), jnp.float32)
+        if last:
+            acc_ref[0:HALO] = carry_ref[...]
+            acc_ref[HALO:] = jnp.zeros((PLANES, 2 * COILS, rows, GZ), jnp.float32)
+        else:
+            acc_ref[...] = jnp.zeros((PLANES + HALO, 2 * COILS, rows, GZ), jnp.float32)
 
     y_tab = y_ref[...]
 
     def step(index, _):
         for part in range(STEP):
-            packed = samples_ref[index * STEP + part, 0].astype(jnp.float32)
+            packed = gather(samples_ref, (index * STEP + part) * (LANES // CAP), q)
             build(packed, y_tab, pair_ref, dense_ref, part * LANES, LANES)
         product = lax.dot_general(
             pair_ref[...], dense_ref[...], (((1,), (1,)), ((), ())), preferred_element_type=jnp.float32
         )
         here = pl.ds(4 * q, SPAN)
-        acc_ref[here] = acc_ref[here] + product.reshape(SPAN, PAIR, GZ)
+        acc_ref[here] = acc_ref[here] + product.reshape(SPAN, 2 * COILS, rows, GZ)
         return 0
 
-    lax.fori_loop(0, ZH // STEP, step, 0)
-
-    @pl.when(q == BLOCKS // CHUNKS - 1)
+    lax.fori_loop(0, SOURCES * CAP // (STEP * LANES), step, 0)
+
+    @pl.when(q == QS - 1)
     def _():
         z_tab = z_ref[...]
         lines = transform_z(acc_ref[0:PLANES], z_tab)
-        for coil in range(COILS):
-            for row in range(ROWS):
-                line = lines[coil * ROWS + row]
-                both = jnp.concatenate([line[:, :GZ], line[:, GZ:]], 0).astype(jnp.bfloat16)
-                out_ref[
-                    (row // 4) * 2 + coil // 2, coil % 2, :, (row % 4) * GZ : (row % 4 + 1) * GZ
-                ] = both
         if last:
             edge = transform_z(acc_ref[PLANES:], z_tab)
-            for coil in range(0, COILS, 2):
-                for row in range(ROWS):
-                    pieces = []
-                    for inner in range(2):
-                        line = edge[(coil + inner) * ROWS + row]
-                        pieces += [line[:, :GZ], line[:, GZ:]]
-                    out_ref[
-                        (row // 4) * 2 + coil // 2, 2, :, (row % 4) * GZ : (row % 4 + 1) * GZ
-                    ] = jnp.concatenate(pieces, 0).astype(jnp.bfloat16)
-        else:
+        for row in range(rows):
+            half, owner, e = row // 16, row % 16 // 2, row % 2
+            here = slice((2 * half + e) * GZ, (2 * half + e + 1) * GZ)
+            for coil in range(COILS):
+                line = lines[coil * rows + row]
+                out_ref[owner * 2 + coil // 2, coil % 2, :, here] = jnp.concatenate(
+                    [line[:, :GZ], line[:, GZ:]], 0
+                ).astype(jnp.bfloat16)
+            for coil in range(0, COILS, 2) if last else ():
+                pieces = []
+                for inner in range(2):
+                    line = edge[(coil + inner) * rows + row]
+                    pieces += [line[:, :GZ], line[:, GZ:]]
+                out_ref[owner * 2 + coil // 2, 2, :, here] = jnp.concatenate(pieces, 0).astype(
+                    jnp.bfloat16
+                )
+        if not last:
             carried_ref[...] = acc_ref[PLANES:]
 
 
-def grid_chunk(samples, y_tab, z_tab, carry, chunk):
-    blocks = BLOCKS // CHUNKS
-    last = chunk == CHUNKS - 1
-    tiles = 3 if last else 2
-    flops = 2 * SPAN * PAIR * GZ * ZH * LANES * blocks + 2 * PLANES * PAIR * GZ * 2 * GZ
+def grid_chunk(samples, y_tab, z_tab, carry=None, part=0):
+    last = carry is not None
+    rows = y_tab.shape[0] // 2
+    tiles, lanes = (3, rows // 8 * GZ) if last else (2, rows // 8 * GZ)
+    size = SPAN * 2 * COILS * rows
+    flops = 2 * size * GZ * SOURCES * CAP * QS + 2 * PLANES * COILS * rows * 4 * GZ * GZ
+    in_specs = [
+        pl.BlockSpec((SOURCES, 16, 2 * CAP), lambda q: (0, 0, 0)),
+        pl.BlockSpec((2 * rows, GY), lambda q: (0, 0)),
+        pl.BlockSpec((2 * GZ, 2 * GZ), lambda q: (0, 0)),
+    ]
+    out_specs = [pl.BlockSpec((GROUPS, tiles, 16, lanes), lambda q: (0, 0, 0, 0))]
+    out_shape = [jax.ShapeDtypeStruct((GROUPS, tiles, 16, lanes), jnp.bfloat16)]
+    operands = [samples, y_tab, z_tab]
+    if last:
+        in_specs.append(pl.BlockSpec((HALO, 2 * COILS, rows, GZ), lambda q: (0, 0, part, 0)))
+        operands.append(carry)
+    else:
+        out_specs.append(pl.BlockSpec((HALO, 2 * COILS, rows, GZ), lambda q: (0, 0, 0, 0)))
+        out_shape.append(jax.ShapeDtypeStruct((HALO, 2 * COILS, rows, GZ), jnp.float32))
     return pl.pallas_call(
         lambda *refs: grid_kernel(last, *refs),
-        grid=(blocks,),
-        in_specs=[
-            pl.BlockSpec((ZH, 1, 16, LANES), lambda q: (0, q + chunk * blocks, 0, 0)),
-            pl.BlockSpec((2 * ROWS, GY), lambda q: (0, 0)),
-            pl.BlockSpec((2 * GZ, 2 * GZ), lambda q: (0, 0)),
-            pl.BlockSpec((HALO, PAIR, GZ), lambda q: (0, 0, 0)),
-        ],
-        out_specs=[
-            pl.BlockSpec((GROUPS, tiles, 16, 4 * GZ), lambda q: (0, 0, 0, 0)),
-            pl.BlockSpec((HALO, PAIR, GZ), lambda q: (0, 0, 0)),
-        ],
-        out_shape=[
-            jax.ShapeDtypeStruct((GROUPS, tiles, 16, 4 * GZ), jnp.bfloat16),
-            jax.ShapeDtypeStruct((HALO, PAIR, GZ), jnp.float32),
-        ],
+        grid=(QS,),
+        in_specs=in_specs,
+        out_specs=out_specs,
+        out_shape=out_shape,
         scratch_shapes=[
-            pltpu.VMEM((SPAN * PAIR, STEP * LANES), jnp.bfloat16),
+            pltpu.VMEM((size, STEP * LANES), jnp.bfloat16),
             pltpu.VMEM((GZ, STEP * LANES), jnp.bfloat16),
-            pltpu.VMEM((PLANES + HALO, PAIR, GZ), jnp.float32),
+            pltpu.VMEM((PLANES + HALO, 2 * COILS, rows, GZ), jnp.float32),
         ],
         compiler_params=pltpu.CompilerParams(vmem_limit_bytes=48 * 2**20),
         cost_estimate=pl.CostEstimate(
-            flops=flops, bytes_accessed=4 * 2**20, transcendentals=0
+            flops=2 * flops, bytes_accessed=4 * 2**20, transcendentals=0
         ),
         name="grid_chunk",
-    )(samples, y_tab, z_tab, carry)
+    )(*operands)
 
 
 def combine_kernel(first_ref, second_ref, main_ref, edge_ref, maps_ref, out_ref):
@@ -262,24 +297,24 @@
         out_ref[:, part] = total[part].astype(jnp.bfloat16).reshape(8, GX // 8, GZ)
 
 
-def combine(first, second, maps):
+def combine(first, second, maps, half):
     main_tab, edge_tab = x_tables()
     depth = GROUPS * 16
     return pl.pallas_call(
         combine_kernel,
-        grid=(4,),
+        grid=(2,),
         in_specs=[
-            pl.BlockSpec((GROUPS, 2, 16, GZ), lambda y: (0, 0, 0, y)),
+            pl.BlockSpec((GROUPS, 2, 16, GZ), lambda y: (0, 0, 0, y + 2 * half)),
             pl.BlockSpec((GROUPS, 3, 16, GZ), lambda y: (0, 0, 0, y)),
             pl.BlockSpec((CHUNKS, 2 * GX, depth), lambda y: (0, 0, 0)),
             pl.BlockSpec((2, 2 * GX, depth), lambda y: (0, 0, 0)),
-            pl.BlockSpec((2, 2, GX, GZ), lambda y: (0, 0, 0, y)),
+            pl.BlockSpec((2, 2, GX, GZ), lambda y: (0, 0, 0, y + 2 * half)),
         ],
         out_specs=pl.BlockSpec((8, 2, GX // 8, GZ), lambda y: (0, 0, 0, y)),
-        out_shape=jax.ShapeDtypeStruct((8, 2, GX // 8, 4 * GZ), jnp.bfloat16),
+        out_shape=jax.ShapeDtypeStruct((8, 2, GX // 8, 2 * GZ), jnp.bfloat16),
         compiler_params=pltpu.CompilerParams(vmem_limit_bytes=48 * 2**20),
         cost_estimate=pl.CostEstimate(
-            flops=2 * 2 * 2 * GX * 3 * depth * 4 * GZ, bytes_accessed=8 * 2**20, transcendentals=0
+            flops=2 * 2 * 2 * GX * 3 * depth * 2 * GZ, bytes_accessed=4 * 2**20, transcendentals=0
         ),
         name="combine",
     )(first, second, jnp.asarray(main_tab), jnp.asarray(edge_tab), maps)
@@ -291,7 +326,7 @@
     spots = jnp.stack([cells // (GY * GZ), cells // GZ % GY, cells % GZ], 0).astype(jnp.bfloat16)
     about = jnp.where(lax.axis_index("core") == 0, offsets, spots)
     rows = jnp.concatenate([kept, about, jnp.zeros((1, SLOTS), jnp.bfloat16)], 0)
-    return rows.reshape(8, GROUPS, BLOCKS * CAP).swapaxes(0, 1)
+    return rows.reshape(8, GROUPS, CHUNKS, QS * CAP).transpose(2, 1, 0, 3)
 
 
 def turn(array, axes):
@@ -301,22 +336,26 @@
 def body(sample_values, sample_offsets, sample_cells, sample_slots, sensitivity):
     packed = pack(sample_values, sample_offsets, sample_cells, sample_slots)
     planes = ("zl", "x", "core")
-    got = turn(packed, planes)
-    got = got.reshape(8, 2, 8, BLOCKS, CAP).transpose(3, 1, 2, 0, 4).reshape(BLOCKS, 16, LANES)
-    samples = turn(jnp.broadcast_to(got[None], (ZH,) + got.shape), "zh")
-    y_tab = lax.dynamic_index_in_dim(
-        jnp.asarray(y_table()), lax.axis_index("zh"), 0, keepdims=False
-    )
+    samples = []
+    for chunk in range(CHUNKS):
+        copies = jnp.broadcast_to(packed[chunk][None], (ZH,) + packed.shape[1:])
+        got = turn(copies.reshape(ZH * GROUPS, 8, QS * CAP), ("zh",) + planes)
+        samples.append(got.reshape(SOURCES, 16, QS * CAP))
+    here = lax.axis_index("zh")
+
+    def rows(part):
+        return lax.dynamic_index_in_dim(jnp.asarray(y_table(part)), here, 0, keepdims=False)
+
     z_tab = jnp.asarray(z_table())
-    carry = jnp.zeros((HALO, PAIR, GZ), jnp.float32)
-    turned = []
-    for chunk in range(CHUNKS):
-        part, carry = grid_chunk(samples, y_tab, z_tab, carry, chunk)
-        turned.append(turn(part, planes))
+    first, carry = grid_chunk(samples[0], rows(None), z_tab)
+    first = turn(first, planes)
     maps = sensitivity.reshape(2, 2, GX, 4 * GZ)
-    partial = turn(combine(*turned, maps), ("y", "core"))
-    image = jnp.sum(partial.astype(jnp.float32), axis=0)
-    return image.reshape(2, GX // 8, 4, GZ)
+    images = []
+    for half in range(2):
+        (second,) = grid_chunk(samples[1], rows(half), z_tab, carry, half)
+        partial = combine(first, turn(second, planes), maps, half)
+        images.append(jnp.sum(turn(partial, ("y", "core")).astype(jnp.float32), axis=0))
+    return jnp.concatenate(images, 2).reshape(2, GX // 8, 4, GZ)
 
 
 def solution(mesh):

time: 154 us -> 174 us (1.13)
  starting transfers between devices: 22.8 us -> 48.4 us
  blocking collectives: 36.1 us -> 18.7 us
  Pallas kernels: 35.3 us -> 44.6 us
  local copies, waits for them, and re-layouts: 10.5 us -> 15.5 us
  waiting for transfers between devices: 46.3 us -> 42.2 us
    all_to_all x3 -> x6, starting transfers between devices: 22.8 us -> 48.4 us  [turn(): return lax.all_to_all(array, axes, split_axis=0, concat_axis=0, tiled=True)]
    all_to_all x2 -> x1, blocking collectives: 36.1 us -> 18.7 us  [turn(): return lax.all_to_all(array, axes, split_axis=0, concat_axis=0, tiled=True)]
    pallas_call x3 -> x5, Pallas kernels: 35.3 us -> 44.6 us  [the longest x3 40.3 us: grid_chunk(): pl.pallas_call(lambda *refs: grid_kernel(last, *refs), grid=(QS,), in_spe...]
    unnamed x8 -> x16, local copies, waits for them, and re-layouts: 2.22 us -> 6.87 us
    all_to_all x3 -> x6, waiting for transfers between devices: 46.3 us -> 42.2 us  [turn(): return lax.all_to_all(array, axes, split_axis=0, concat_axis=0, tiled=True)]
  transfers between devices with their start and end apart: 3 -> 6, of which waited for: 2 -> 6; matrix products, arithmetic and copies ran while one was open for 3% -> 4% of each run, Pallas kernels for 10% -> 19%
where the time goes in v3:
time: 174 us; the launch traced here: 172 us
  starting transfers between devices  48.4 us (28%)
  Pallas kernels  44.6 us (26%)
  waiting for transfers between devices  42.2 us (24%)
  blocking collectives  18.7 us (11%)
  local copies, waits for them, and re-layouts  15.5 us (9%)
  other arithmetic  2.94 us (2%)
    all_to_all x6, starting transfers between devices, turn(): return lax.all_to_all(array, axes, split_axis=0, concat_axis=0, tiled=True)  48.4 us
    all_to_all x6, waiting for transfers between devices, turn(): return lax.all_to_all(array, axes, split_axis=0, concat_axis=0, tiled=True)  42.2 us
    pallas_call x3, Pallas kernels, grid_chunk(): pl.pallas_call(lambda *refs: grid_kernel(last, *refs), grid=(QS,), in_spe...  40.3 us
    all_to_all x1, blocking collectives, turn(): return lax.all_to_all(array, axes, split_axis=0, concat_axis=0, tiled=True)  18.7 us
    unnamed x16, local copies, waits for them, and re-layouts  6.87 us
    pallas_call x2, Pallas kernels, combine(): pl.pallas_call(combine_kernel, grid=(2,), in_specs=[pl.BlockSpec((GROUPS,...  4.24 us
  transfers between devices with their start and end apart: 6, of which 6 were waited for; matrix products, arithmetic and copies ran while one was open for 4% of the time, Pallas kernels for 19%

profile of v3, /device:TPU:1, one launch (start us, length us, event | category | flops | bytes accessed | tf_op | source)
XLA Modules:
  0.0 172.5 jit_solution(1569919193079776673)
XLA Ops:
  0.0 0.0 copy-start.7
  0.0 0.8 broadcast_compare_fusion
  0.8 0.8 fusion.1
  1.6 0.8 reshape.25
  2.4 0.1 pad.4.clone
  2.5 0.1 maximum_select_fusion
  2.6 0.1 maximum_maximum_fusion
  2.7 0.7 broadcast_in_dim.34
  3.4 21.1 %all-to-all-start = ((bf16[128,8,128]{2,1,0:T(8,128)(2,1)}), bf16[128,8,128]{2,1,0:T(8,128)(2,1)S(1)}, u32[]{:S(2)}, u32[]{:S(2)}) async-start(bf16[128,8,128]{2,1,0:T(8,128)(2,1)} %bitcast.3), calls=%async_computation | async-start | bytes 524288 | tf_op jit(solution)/shard_map/all_to_all | solution.py:333
  24.6 0.7 dynamic-slice_bitcast_fusion.2.refs_1_
  25.3 0.8 dynamic-slice_bitcast_fusion.refs_1_
  26.1 19.0 %all-to-all-done = bf16[128,8,128]{2,1,0:T(8,128)(2,1)S(1)} async-done(((bf16[128,8,128]{2,1,0:T(8,128)(2,1)}), bf16[128,8,128]{2,1,0:T(8,128)(2,1)S(1)}, u32[]{:S(2)}, u32[]{:S(2)}) %all-to-all-start) | async-done | bytes 262176 | tf_op jit(solution)/shard_map/all_to_all | solution.py:333
  45.0 0.7 broadcast_in_dim.36
  45.8 8.3 %all-to-all-start.2 = ((bf16[128,8,128]{2,1,0:T(8,128)(2,1)}), bf16[128,8,128]{2,1,0:T(8,128)(2,1)S(1)}, u32[]{:S(2)}, u32[]{:S(2)}) async-start(bf16[128,8,128]{2,1,0:T(8,128)(2,1)} %bitcast.8), calls=%async_computation.2 | async-start | bytes 524288 | tf_op jit(solution)/shard_map/all_to_all | solution.py:333
  54.1 0.0 copy-done.7
  54.1 17.0 %grid_chunk.3 = (bf16[16,2,16,1024]{3,2,1,0:T(8,128)(2,1)}, f32[4,8,32,256]{3,2,1,0:T(8,128)S(1)}) custom-call(bf16[64,16,128]{2,1,0:T(8,128)(2,1)S(1)} %bitcast.18, bf16[64,256]{1,0:T(8,128)(2,1)S(1)} %dynamic-slice_bitcast_fusion.refs_1_, bf16[512,512]{1,0:T(8,128)(2,1)S(1)} %copy-done.7), custom_call_target="tpu_custom_call" | custom-call | flops 16106127360 | bytes 4194304 | tf_op jit(solution)/shard_map/grid_chunk/pallas_call | solution.py:262
  71.1 3.5 %all-to-all-done.2 = bf16[128,8,128]{2,1,0:T(8,128)(2,1)S(1)} async-done(((bf16[128,8,128]{2,1,0:T(8,128)(2,1)}), bf16[128,8,128]{2,1,0:T(8,128)(2,1)S(1)}, u32[]{:S(2)}, u32[]{:S(2)}) %all-to-all-start.2) | async-done | bytes 262176 | tf_op jit(solution)/shard_map/all_to_all | solution.py:333
  74.6 11.2 %grid_chunk.4 = bf16[16,3,16,512]{3,2,1,0:T(8,128)(2,1)S(1)} custom-call(bf16[64,16,128]{2,1,0:T(8,128)(2,1)S(1)} %bitcast.19, bf16[32,256]{1,0:T(8,128)(2,1)S(1)} %dynamic-slice_bitcast_fusion.2.refs_1_, bf16[512,512]{1,0:T(8,128)(2,1)S(1)} %copy-done.7, f32[4,8,32,256]{3,2,1,0:T(8,128)S(1)} %get-tuple-element.8.refs_3_), custom_call_target="tpu_custom_call" | custom-call | flops 8053063680 | bytes 4194304 | tf_op jit(solution)/shard_map/grid_chunk/pallas_call | solution.py:262
  85.8 18.7 %all_to_all.35.second_ref = bf16[16,3,16,512]{3,2,1,0:T(8,128)(2,1)} all-to-all(bf16[16,3,16,512]{3,2,1,0:T(8,128)(2,1)S(1)} %grid_chunk.4), channel_id=1, replica_groups=mesh['zh'=8,'zl'=2,'x'=4,'y'=4,'core'=2] {'zl','x','core'}, dimensions={0} | all-to-all | bytes 1572864 | tf_op jit(solution)/shard_map/all_to_all | solution.py:333
  104.4 4.4 %all-to-all-start.1 = ((bf16[16,2,16,1024]{3,2,1,0:T(8,128)(2,1)}), bf16[16,2,16,1024]{3,2,1,0:T(8,128)(2,1)S(1)}, u32[]{:S(2)}, u32[]{:S(2)}) async-start(bf16[16,2,16,1024]{3,2,1,0:T(8,128)(2,1)} %get-tuple-element.7), calls=%async_computation.1 | async-start | bytes 2097152 | tf_op jit(solution)/shard_map/all_to_all | solution.py:333
  108.9 0.7 dynamic-slice_bitcast_fusion.1.refs_1_
  109.6 12.1 %grid_chunk.5 = bf16[16,3,16,512]{3,2,1,0:T(8,128)(2,1)} custom-call(bf16[64,16,128]{2,1,0:T(8,128)(2,1)S(1)} %bitcast.20, bf16[32,256]{1,0:T(8,128)(2,1)S(1)} %dynamic-slice_bitcast_fusion.1.refs_1_, bf16[512,512]{1,0:T(8,128)(2,1)S(1)} %copy-done.7, f32[4,8,32,256]{3,2,1,0:T(8,128)S(1)} %get-tuple-element.8.refs_3_), custom_call_target="tpu_custom_call" | custom-call | flops 8053063680 | bytes 4194304 | tf_op jit(solution)/shard_map/grid_chunk/pallas_call | solution.py:262
  121.7 3.1 %all-to-all-done.1.first_ref = bf16[16,2,16,1024]{3,2,1,0:T(8,128)(2,1)S(1)} async-done(((bf16[16,2,16,1024]{3,2,1,0:T(8,128)(2,1)}), bf16[16,2,16,1024]{3,2,1,0:T(8,128)(2,1)S(1)}, u32[]{:S(2)}, u32[]{:S(2)}) %all-to-all-start.1) | async-done | bytes 1048608 | tf_op jit(solution)/shard_map/all_to_all | solution.py:333
  124.8 4.9 %all-to-all-start.5 = ((bf16[16,3,16,512]{3,2,1,0:T(8,128)(2,1)}), bf16[16,3,16,512]{3,2,1,0:T(8,128)(2,1)}, u32[]{:S(2)}, u32[]{:S(2)}) async-start(bf16[16,3,16,512]{3,2,1,0:T(8,128)(2,1)} %grid_chunk.5), calls=%async_computation.5 | async-start | bytes 1572864 | tf_op jit(solution)/shard_map/all_to_all | solution.py:333
  129.7 3.2 %reshape.31.maps_ref = bf16[2,2,256,1024]{3,2,1,0:T(8,128)(2,1)S(1)} reshape(bf16[2,2,256,4,256]{4,3,2,1,0:T(4,128)(2,1)} %param.17) | data formatting | bytes 4194304 | tf_op jit(solution)/shard_map/reshape | solution.py:352
  132.9 0.0 copy-start
  132.9 1.1 copy-done
  134.0 0.0 copy-start.3
  134.1 1.0 copy-done.3
  135.1 0.0 copy-start.5
  135.1 1.0 copy-done.5
  136.1 1.7 %combine.2 = bf16[8,2,32,512]{3,2,1,0:T(8,128)(2,1)S(1)} custom-call(bf16[16,2,16,1024]{3,2,1,0:T(8,128)(2,1)S(1)} %all-to-all-done.1.first_ref, bf16[16,3,16,512]{3,2,1,0:T(8,128)(2,1)S(1)} %copy-done, bf16[2,512,256]{2,1,0:T(8,128)(2,1)S(1)} %copy-done.5, bf16[2,512,256]{2,1,0:T(8,128)(2,1)S(1)} %copy-done.3, bf16[2,2,256,1024]{3,2,1,0:T(8,128)(2,1)S(1)} %reshape.31.maps_ref), custom_call_target="tpu_custom_call" | custom-call | flops 805306368 | bytes 4194304 | tf_op jit(solution)/shard_map/combine/pallas_call | solution.py:303
  137.9 0.0 copy-start.1
  137.9 0.8 copy-done.1
  138.7 4.2 %all-to-all-done.5.second_ref = bf16[16,3,16,512]{3,2,1,0:T(8,128)(2,1)} async-done(((bf16[16,3,16,512]{3,2,1,0:T(8,128)(2,1)}), bf16[16,3,16,512]{3,2,1,0:T(8,128)(2,1)}, u32[]{:S(2)}, u32[]{:S(2)}) %all-to-all-start.5) | async-done | bytes 786464 | tf_op jit(solution)/shard_map/all_to_all | solution.py:333
  142.8 5.3 %all-to-all-start.4 = ((bf16[8,2,32,512]{3,2,1,0:T(8,128)(2,1)}), bf16[8,2,32,512]{3,2,1,0:T(8,128)(2,1)}, u32[]{:S(2)}, u32[]{:S(2)}) async-start(bf16[8,2,32,512]{3,2,1,0:T(8,128)(2,1)} %copy-done.1), calls=%async_computation.4 | async-start | bytes 1048576 | tf_op jit(solution)/shard_map/all_to_all | solution.py:333
  148.2 0.0 copy-start.4
  148.2 1.0 copy-done.4
  149.2 0.0 copy-start.6
  149.2 1.0 copy-done.6
  150.3 2.5 %combine.3 = bf16[8,2,32,512]{3,2,1,0:T(8,128)(2,1)S(1)} custom-call(bf16[16,2,16,1024]{3,2,1,0:T(8,128)(2,1)S(1)} %all-to-all-done.1.first_ref, bf16[16,3,16,512]{3,2,1,0:T(8,128)(2,1)} %all-to-all-done.5.second_ref, bf16[2,512,256]{2,1,0:T(8,128)(2,1)S(1)} %copy-done.6, bf16[2,512,256]{2,1,0:T(8,128)(2,1)S(1)} %copy-done.4, ...), custom_call_target="tpu_custom_call" | custom-call | flops 805306368 | bytes 4194304 | tf_op jit(solution)/shard_map/combine/pallas_call | solution.py:303
  152.8 0.0 copy-start.2
  152.8 0.8 copy-done.2
  153.6 4.2 %all-to-all-done.4 = bf16[8,2,32,512]{3,2,1,0:T(8,128)(2,1)} async-done(((bf16[8,2,32,512]{3,2,1,0:T(8,128)(2,1)}), bf16[8,2,32,512]{3,2,1,0:T(8,128)(2,1)}, u32[]{:S(2)}, u32[]{:S(2)}) %all-to-all-start.4) | async-done | bytes 524320 | tf_op jit(solution)/shard_map/all_to_all | solution.py:333
  157.8 4.3 %all-to-all-start.6 = ((bf16[8,2,32,512]{3,2,1,0:T(8,128)(2,1)}), bf16[8,2,32,512]{3,2,1,0:T(8,128)(2,1)S(1)}, u32[]{:S(2)}, u32[]{:S(2)}) async-start(bf16[8,2,32,512]{3,2,1,0:T(8,128)(2,1)} %copy-done.2), calls=%async_computation.6 | async-start | bytes 1048576 | tf_op jit(solution)/shard_map/all_to_all | solution.py:333
  162.0 1.1 convert_reduce_fusion.1
  163.2 8.4 %all-to-all-done.6 = bf16[8,2,32,512]{3,2,1,0:T(8,128)(2,1)S(1)} async-done(((bf16[8,2,32,512]{3,2,1,0:T(8,128)(2,1)}), bf16[8,2,32,512]{3,2,1,0:T(8,128)(2,1)S(1)}, u32[]{:S(2)}, u32[]{:S(2)}) %all-to-all-start.6) | async-done | bytes 524320 | tf_op jit(solution)/shard_map/all_to_all | solution.py:333
  171.5 0.1 convert_reduce_fusion
  171.6 0.8 reshape.32
  (6 shorter events, 0.1 us)
Async XLA Ops:
  0.0 54.1 %copy-start.7 = (bf16[512,512]{1,0:T(8,128)(2,1)S(1)}, bf16[512,512]{1,0:T(8,128)(2,1)}, u32[]{:S(2)}) copy-start(bf16[512,512]{1,0:T(8,128)(2,1)} %constant.84.clone.refs_2_) | copy-start | bytes 1572868
  3.4 41.6 %all-to-all-start = ((bf16[128,8,128]{2,1,0:T(8,128)(2,1)}), bf16[128,8,128]{2,1,0:T(8,128)(2,1)S(1)}, u32[]{:S(2)}, u32[]{:S(2)}) async-start(bf16[128,8,128]{2,1,0:T(8,128)(2,1)} %bitcast.3), calls=%async_computation | async-start | bytes 524288 | tf_op jit(solution)/shard_map/all_to_all | solution.py:333
  45.8 28.8 %all-to-all-start.2 = ((bf16[128,8,128]{2,1,0:T(8,128)(2,1)}), bf16[128,8,128]{2,1,0:T(8,128)(2,1)S(1)}, u32[]{:S(2)}, u32[]{:S(2)}) async-start(bf16[128,8,128]{2,1,0:T(8,128)(2,1)} %bitcast.8), calls=%async_computation.2 | async-start | bytes 524288 | tf_op jit(solution)/shard_map/all_to_all | solution.py:333
  104.4 20.3 %all-to-all-start.1 = ((bf16[16,2,16,1024]{3,2,1,0:T(8,128)(2,1)}), bf16[16,2,16,1024]{3,2,1,0:T(8,128)(2,1)S(1)}, u32[]{:S(2)}, u32[]{:S(2)}) async-start(bf16[16,2,16,1024]{3,2,1,0:T(8,128)(2,1)} %get-tuple-element.7), calls=%async_computation.1 | async-start | bytes 2097152 | tf_op jit(solution)/shard_map/all_to_all | solution.py:333
  124.8 18.1 %all-to-all-start.5 = ((bf16[16,3,16,512]{3,2,1,0:T(8,128)(2,1)}), bf16[16,3,16,512]{3,2,1,0:T(8,128)(2,1)}, u32[]{:S(2)}, u32[]{:S(2)}) async-start(bf16[16,3,16,512]{3,2,1,0:T(8,128)(2,1)} %grid_chunk.5), calls=%async_computation.5 | async-start | bytes 1572864 | tf_op jit(solution)/shard_map/all_to_all | solution.py:333
  132.9 1.1 copy-start
  134.0 1.0 copy-start.3
  135.1 1.0 copy-start.5
  137.9 0.8 copy-start.1
  142.8 14.9 %all-to-all-start.4 = ((bf16[8,2,32,512]{3,2,1,0:T(8,128)(2,1)}), bf16[8,2,32,512]{3,2,1,0:T(8,128)(2,1)}, u32[]{:S(2)}, u32[]{:S(2)}) async-start(bf16[8,2,32,512]{3,2,1,0:T(8,128)(2,1)} %copy-done.1), calls=%async_computation.4 | async-start | bytes 1048576 | tf_op jit(solution)/shard_map/all_to_all | solution.py:333
  148.2 1.0 copy-start.4
  149.2 1.0 copy-start.6
  152.8 0.8 copy-start.2
  157.8 13.8 %all-to-all-start.6 = ((bf16[8,2,32,512]{3,2,1,0:T(8,128)(2,1)}), bf16[8,2,32,512]{3,2,1,0:T(8,128)(2,1)S(1)}, u32[]{:S(2)}, u32[]{:S(2)}) async-start(bf16[8,2,32,512]{3,2,1,0:T(8,128)(2,1)} %copy-done.2), calls=%async_computation.6 | async-start | bytes 1048576 | tf_op jit(solution)/shard_map/all_to_all | solution.py:333

commit v4 on v2

--- a/solution.py
+++ b/solution.py
@@ -20,6 +20,8 @@
 TERMS = 31
 
 ZH = 8
+SOURCES = 64
+UNIT = 16
 GROUPS = 16
 BLOCKS = 4
 CHUNKS = 2
@@ -159,6 +161,29 @@
     return jnp.swapaxes(along.reshape(planes, HALF, 2 * GZ), 0, 1)
 
 
+def gather(samples_ref, start, offset):
+    per = 128 // UNIT
+    lane = lax.broadcasted_iota(jnp.int32, (16, 128), 1) // UNIT
+    pieces = []
+    for piece in range(LANES // 128):
+        joined = None
+        for k in range(per):
+            rows = samples_ref[start + piece * per + k].astype(jnp.float32)
+            rows = pltpu.roll(rows, (128 + UNIT * k - offset) % 128, 1)
+            joined = rows if joined is None else jnp.where(lane == k, rows, joined)
+        pieces.append(joined)
+    return jnp.concatenate(pieces, 1)
+
+
+def largest(samples_ref):
+    def step(index, seen):
+        return jnp.maximum(seen, jnp.abs(samples_ref[index].astype(jnp.float32)))
+
+    seen = lax.fori_loop(0, SOURCES, step, jnp.zeros((16, 128), jnp.float32), unroll=8)
+    row = lax.broadcasted_iota(jnp.int32, (16, 128), 0)
+    return jnp.max(jnp.where(row % 8 < 4, seen, 0.0), axis=0, keepdims=True)
+
+
 def grid_kernel(last, samples_ref, y_ref, z_ref, carry_ref, out_ref, carried_ref, pair_ref, dense_ref, acc_ref):
     q = pl.program_id(0)
 
@@ -168,19 +193,29 @@
         acc_ref[HALO:] = jnp.zeros((PLANES, PAIR, GZ), jnp.float32)
 
     y_tab = y_ref[...]
+    seen = largest(samples_ref)
+    unit = lax.broadcasted_iota(jnp.int32, (1, 128), 1) // UNIT
 
     def step(index, _):
-        for part in range(STEP):
-            packed = samples_ref[index * STEP + part, 0].astype(jnp.float32)
-            build(packed, y_tab, pair_ref, dense_ref, part * LANES, LANES)
-        product = lax.dot_general(
-            pair_ref[...], dense_ref[...], (((1,), (1,)), ((), ())), preferred_element_type=jnp.float32
-        )
-        here = pl.ds(4 * q, SPAN)
-        acc_ref[here] = acc_ref[here] + product.reshape(SPAN, PAIR, GZ)
+        place = q * (CAP // UNIT) + index
+
+        @pl.when(jnp.max(jnp.where(unit == place, seen, 0.0)) > 0.0)
+        def _():
+            for part in range(STEP):
+                packed = gather(samples_ref, part * (LANES // UNIT), place * UNIT)
+                build(packed, y_tab, pair_ref, dense_ref, part * LANES, LANES)
+            product = lax.dot_general(
+                pair_ref[...],
+                dense_ref[...],
+                (((1,), (1,)), ((), ())),
+                preferred_element_type=jnp.float32,
+            )
+            here = pl.ds(4 * q, SPAN)
+            acc_ref[here] = acc_ref[here] + product.reshape(SPAN, PAIR, GZ)
+
         return 0
 
-    lax.fori_loop(0, ZH // STEP, step, 0)
+    lax.fori_loop(0, CAP // UNIT, step, 0)
 
     @pl.when(q == BLOCKS // CHUNKS - 1)
     def _():
@@ -212,12 +247,12 @@
     blocks = BLOCKS // CHUNKS
     last = chunk == CHUNKS - 1
     tiles = 3 if last else 2
-    flops = 2 * SPAN * PAIR * GZ * ZH * LANES * blocks + 2 * PLANES * PAIR * GZ * 2 * GZ
+    flops = 2 * SPAN * PAIR * GZ * SOURCES * CAP * blocks + 2 * PLANES * PAIR * GZ * 2 * GZ
     return pl.pallas_call(
         lambda *refs: grid_kernel(last, *refs),
         grid=(blocks,),
         in_specs=[
-            pl.BlockSpec((ZH, 1, 16, LANES), lambda q: (0, q + chunk * blocks, 0, 0)),
+            pl.BlockSpec((SOURCES, 16, blocks * CAP), lambda q: (0, 0, chunk)),
             pl.BlockSpec((2 * ROWS, GY), lambda q: (0, 0)),
             pl.BlockSpec((2 * GZ, 2 * GZ), lambda q: (0, 0)),
             pl.BlockSpec((HALO, PAIR, GZ), lambda q: (0, 0, 0)),
@@ -285,13 +320,31 @@
     )(first, second, jnp.asarray(main_tab), jnp.asarray(edge_tab), maps)
 
 
+def pack_kernel(values_ref, offsets_ref, cells_ref, slots_ref, out_ref):
+    used = slots_ref[...] < SLOTS
+    cells = cells_ref[...]
+    rows = [jnp.where(used, values_ref[r : r + 1].astype(jnp.float32), 0.0) for r in range(4)]
+    spots = (cells // (GY * GZ), cells // GZ % GY, cells % GZ)
+    first = lax.axis_index("core") == 0
+    for axis in range(3):
+        offset = offsets_ref[axis : axis + 1].astype(jnp.float32)
+        rows.append(jnp.where(first, offset, spots[axis].astype(jnp.float32)))
+    rows.append(jnp.zeros((1, SLOTS), jnp.float32))
+    packed = jnp.concatenate(rows, 0).astype(jnp.bfloat16)
+    width = BLOCKS * CAP
+    for group in range(GROUPS):
+        part = packed[:, group * width : (group + 1) * width]
+        for copy in range(ZH):
+            out_ref[copy * GROUPS + group] = part
+
+
 def pack(values, offsets, cells, slots):
-    used = slots < SLOTS
-    kept = jnp.where(used[None, :], values.reshape(4, SLOTS), jnp.zeros((), jnp.bfloat16))
-    spots = jnp.stack([cells // (GY * GZ), cells // GZ % GY, cells % GZ], 0).astype(jnp.bfloat16)
-    about = jnp.where(lax.axis_index("core") == 0, offsets, spots)
-    rows = jnp.concatenate([kept, about, jnp.zeros((1, SLOTS), jnp.bfloat16)], 0)
-    return rows.reshape(8, GROUPS, BLOCKS * CAP).swapaxes(0, 1)
+    return pl.pallas_call(
+        pack_kernel,
+        out_shape=jax.ShapeDtypeStruct((ZH * GROUPS, 8, BLOCKS * CAP), jnp.bfloat16),
+        compiler_params=pltpu.CompilerParams(vmem_limit_bytes=16 * 2**20),
+        name="pack",
+    )(values.reshape(4, SLOTS), offsets, cells.reshape(1, SLOTS), slots.reshape(1, SLOTS))
 
 
 def turn(array, axes):
@@ -301,9 +354,8 @@
 def body(sample_values, sample_offsets, sample_cells, sample_slots, sensitivity):
     packed = pack(sample_values, sample_offsets, sample_cells, sample_slots)
     planes = ("zl", "x", "core")
-    got = turn(packed, planes)
-    got = got.reshape(8, 2, 8, BLOCKS, CAP).transpose(3, 1, 2, 0, 4).reshape(BLOCKS, 16, LANES)
-    samples = turn(jnp.broadcast_to(got[None], (ZH,) + got.shape), "zh")
+    got = turn(packed, ("zh",) + planes)
+    samples = got.reshape(SOURCES, 16, BLOCKS * CAP)
     y_tab = lax.dynamic_index_in_dim(
         jnp.asarray(y_table()), lax.axis_index("zh"), 0, keepdims=False
     )

time: 154 us -> 145 us (0.942)
  blocking collectives: 36.1 us -> 20.2 us
  starting transfers between devices: 22.8 us -> 33.9 us
  Pallas kernels: 35.3 us -> 27.7 us
  waiting for transfers between devices: 46.3 us -> 50.8 us
  other arithmetic: 1.9 us -> 0.17 us
    all_to_all x2 -> x1, blocking collectives: 36.1 us -> 20.2 us  [turn(): return lax.all_to_all(array, axes, split_axis=0, concat_axis=0, tiled=True)]
    all_to_all x3, starting transfers between devices: 22.8 us -> 33.9 us  [turn(): return lax.all_to_all(array, axes, split_axis=0, concat_axis=0, tiled=True)]
    pallas_call x2, Pallas kernels: 30.7 us -> 22.2 us  [grid_chunk(): pl.pallas_call(lambda *refs: grid_kernel(last, *refs), grid=(blocks,), in...]
    all_to_all x3, waiting for transfers between devices: 46.3 us -> 50.8 us  [turn(): return lax.all_to_all(array, axes, split_axis=0, concat_axis=0, tiled=True)]
    unnamed x8 -> x14, local copies, waits for them, and re-layouts: 2.22 us -> 4.39 us
  transfers between devices with their start and end apart: 3 -> 3, of which waited for: 2 -> 3; matrix products, arithmetic and copies ran while one was open for 3% -> 4% of each run, Pallas kernels for 10% -> 8%
where the time goes in v4:
time: 145 us; the launch traced here: 144 us
  waiting for transfers between devices  50.8 us (35%)
  starting transfers between devices  33.9 us (23%)
  Pallas kernels  27.7 us (19%)
  blocking collectives  20.2 us (14%)
  local copies, waits for them, and re-layouts  11.3 us (8%)
    all_to_all x3, waiting for transfers between devices, turn(): return lax.all_to_all(array, axes, split_axis=0, concat_axis=0, tiled=True)  50.8 us
    all_to_all x3, starting transfers between devices, turn(): return lax.all_to_all(array, axes, split_axis=0, concat_axis=0, tiled=True)  33.9 us
    pallas_call x2, Pallas kernels, grid_chunk(): pl.pallas_call(lambda *refs: grid_kernel(last, *refs), grid=(blocks,), in...  22.2 us
    all_to_all x1, blocking collectives, turn(): return lax.all_to_all(array, axes, split_axis=0, concat_axis=0, tiled=True)  20.2 us
    pallas_call x1, Pallas kernels, combine(): pl.pallas_call(combine_kernel, grid=(4,), in_specs=[pl.BlockSpec((GROUPS,...  4.59 us
    reshape x1, local copies, waits for them, and re-layouts, body(): maps = sensitivity.reshape(2, 2, GX, 4 * GZ)  4.51 us
    unnamed x14, local copies, waits for them, and re-layouts  4.39 us
  transfers between devices with their start and end apart: 3, of which 3 were waited for; matrix products, arithmetic and copies ran while one was open for 4% of the time, Pallas kernels for 8%

profile of v4, /device:TPU:1, one launch (start us, length us, event | category | flops | bytes accessed | tf_op | source)
XLA Modules:
  0.0 144.2 jit_solution(16844436693133225638)
XLA Ops:
  0.0 0.8 reshape.18.values_ref
  0.8 0.0 copy-start.3
  0.8 0.7 copy-done.3
  1.5 0.0 copy-start.4
  1.5 0.7 copy-done.4
  2.3 0.0 copy-start.5
  2.3 0.7 copy-done.5
  3.0 0.0 copy-start.6
  3.0 0.9 pack.1
  3.9 20.4 %all-to-all-start = ((bf16[128,8,256]{2,1,0:T(8,128)(2,1)}), bf16[128,8,256]{2,1,0:T(8,128)(2,1)S(1)}, u32[]{:S(2)}, u32[]{:S(2)}) async-start(bf16[128,8,256]{2,1,0:T(8,128)(2,1)} %pack.1), calls=%async_computation | async-start | bytes 1048576 | tf_op jit(solution)/shard_map/all_to_all | solution.py:351
  24.3 0.8 dynamic-slice_bitcast_fusion.refs_1_
  25.1 30.1 %all-to-all-done = bf16[128,8,256]{2,1,0:T(8,128)(2,1)S(1)} async-done(((bf16[128,8,256]{2,1,0:T(8,128)(2,1)}), bf16[128,8,256]{2,1,0:T(8,128)(2,1)S(1)}, u32[]{:S(2)}, u32[]{:S(2)}) %all-to-all-start) | async-done | bytes 524320 | tf_op jit(solution)/shard_map/all_to_all | solution.py:351
  55.1 0.1 broadcast_in_dim.3.refs_3_
  55.2 0.0 copy-done.6
  55.2 10.8 %grid_chunk.2 = (bf16[16,2,16,1024]{3,2,1,0:T(8,128)(2,1)}, f32[4,256,256]{2,1,0:T(8,128)S(1)}) custom-call(bf16[64,16,256]{2,1,0:T(8,128)(2,1)S(1)} %bitcast.5, bf16[64,256]{1,0:T(8,128)(2,1)S(1)} %dynamic-slice_bitcast_fusion.refs_1_, bf16[512,512]{1,0:T(8,128)(2,1)S(1)} %copy-done.6, f32[4,256,256]{2,1,0:T(8,128)S(1)} %broadcast_in_dim.3.refs_3_), custom_call_target="tpu_custom_call" | custom-call | flops 8053063680 | bytes 4194304 | tf_op jit(solution)/shard_map/grid_chunk/pallas_call | solution.py:251
  66.1 9.2 %all-to-all-start.1 = ((bf16[16,2,16,1024]{3,2,1,0:T(8,128)(2,1)}), bf16[16,2,16,1024]{3,2,1,0:T(8,128)(2,1)S(1)}, u32[]{:S(2)}, u32[]{:S(2)}) async-start(bf16[16,2,16,1024]{3,2,1,0:T(8,128)(2,1)} %get-tuple-element.8), calls=%async_computation.1 | async-start | bytes 2097152 | tf_op jit(solution)/shard_map/all_to_all | solution.py:351
  75.2 11.3 %grid_chunk.3 = (bf16[16,3,16,1024]{3,2,1,0:T(8,128)(2,1)S(1)}, f32[4,256,256]{2,1,0:T(8,128)}) custom-call(bf16[64,16,256]{2,1,0:T(8,128)(2,1)S(1)} %bitcast.6, bf16[64,256]{1,0:T(8,128)(2,1)S(1)} %dynamic-slice_bitcast_fusion.refs_1_, bf16[512,512]{1,0:T(8,128)(2,1)S(1)} %copy-done.6, f32[4,256,256]{2,1,0:T(8,128)S(1)} %get-tuple-element.9.refs_3_), custom_call_target="tpu_custom_call" | custom-call | flops 8053063680 | bytes 4194304 | tf_op jit(solution)/shard_map/grid_chunk/pallas_call | solution.py:251
  86.6 0.0 copy-start
  86.6 1.2 copy-done
  87.7 3.4 %all-to-all-done.1.first_ref = bf16[16,2,16,1024]{3,2,1,0:T(8,128)(2,1)S(1)} async-done(((bf16[16,2,16,1024]{3,2,1,0:T(8,128)(2,1)}), bf16[16,2,16,1024]{3,2,1,0:T(8,128)(2,1)S(1)}, u32[]{:S(2)}, u32[]{:S(2)}) %all-to-all-start.1) | async-done | bytes 1048608 | tf_op jit(solution)/shard_map/all_to_all | solution.py:351
  91.1 4.4 %all-to-all-start.2 = ((bf16[16,3,16,1024]{3,2,1,0:T(8,128)(2,1)}), bf16[16,3,16,1024]{3,2,1,0:T(8,128)(2,1)S(1)}, u32[]{:S(2)}, u32[]{:S(2)}) async-start(bf16[16,3,16,1024]{3,2,1,0:T(8,128)(2,1)} %copy-done), calls=%async_computation.2 | async-start | bytes 3145728 | tf_op jit(solution)/shard_map/all_to_all | solution.py:351
  95.4 0.0 copy-start.1
  95.5 4.5 %reshape.22.maps_ref = bf16[2,2,256,1024]{3,2,1,0:T(8,128)(2,1)} reshape(bf16[2,2,256,4,256]{4,3,2,1,0:T(4,128)(2,1)} %param.13) | data formatting | bytes 4194304 | tf_op jit(solution)/shard_map/reshape | solution.py:368
  100.0 17.4 %all-to-all-done.2.second_ref = bf16[16,3,16,1024]{3,2,1,0:T(8,128)(2,1)S(1)} async-done(((bf16[16,3,16,1024]{3,2,1,0:T(8,128)(2,1)}), bf16[16,3,16,1024]{3,2,1,0:T(8,128)(2,1)S(1)}, u32[]{:S(2)}, u32[]{:S(2)}) %all-to-all-start.2) | async-done | bytes 1572896 | tf_op jit(solution)/shard_map/all_to_all | solution.py:351
  117.3 0.0 copy-done.1
  117.3 0.0 copy-start.2
  117.3 1.0 copy-done.2
  118.4 4.6 %combine.1 = bf16[8,2,32,1024]{3,2,1,0:T(8,128)(2,1)S(1)} custom-call(bf16[16,2,16,1024]{3,2,1,0:T(8,128)(2,1)S(1)} %all-to-all-done.1.first_ref, bf16[16,3,16,1024]{3,2,1,0:T(8,128)(2,1)S(1)} %all-to-all-done.2.second_ref, bf16[2,512,256]{2,1,0:T(8,128)(2,1)S(1)} %copy-done.2, bf16[2,512,256]{2,1,0:T(8,128)(2,1)S(1)} %copy-done.1, ...), custom_call_target="tpu_custom_call" | custom-call | flops 1610612736 | bytes 8388608 | tf_op jit(solution)/shard_map/combine/pallas_call | solution.py:303
  123.0 20.2 %all_to_all.20 = bf16[8,2,32,1024]{3,2,1,0:T(8,128)(2,1)S(1)} all-to-all(bf16[8,2,32,1024]{3,2,1,0:T(8,128)(2,1)S(1)} %combine.1), channel_id=1, replica_groups=mesh['zh'=8,'zl'=2,'x'=4,'y'=4,'core'=2] {'y','core'}, dimensions={0} | all-to-all | bytes 2097152 | tf_op jit(solution)/shard_map/all_to_all | solution.py:351
  143.2 0.2 convert_reduce_fusion
  143.4 0.8 reshape.23
Async XLA Ops:
  0.8 0.8 copy-start.3
  1.5 0.7 copy-start.4
  2.3 0.7 copy-start.5
  3.0 52.2 %copy-start.6 = (bf16[512,512]{1,0:T(8,128)(2,1)S(1)}, bf16[512,512]{1,0:T(8,128)(2,1)}, u32[]{:S(2)}) copy-start(bf16[512,512]{1,0:T(8,128)(2,1)} %constant.24.clone.refs_2_) | copy-start | bytes 1572868
  3.9 51.2 %all-to-all-start = ((bf16[128,8,256]{2,1,0:T(8,128)(2,1)}), bf16[128,8,256]{2,1,0:T(8,128)(2,1)S(1)}, u32[]{:S(2)}, u32[]{:S(2)}) async-start(bf16[128,8,256]{2,1,0:T(8,128)(2,1)} %pack.1), calls=%async_computation | async-start | bytes 1048576 | tf_op jit(solution)/shard_map/all_to_all | solution.py:351
  66.1 25.0 %all-to-all-start.1 = ((bf16[16,2,16,1024]{3,2,1,0:T(8,128)(2,1)}), bf16[16,2,16,1024]{3,2,1,0:T(8,128)(2,1)S(1)}, u32[]{:S(2)}, u32[]{:S(2)}) async-start(bf16[16,2,16,1024]{3,2,1,0:T(8,128)(2,1)} %get-tuple-element.8), calls=%async_computation.1 | async-start | bytes 2097152 | tf_op jit(solution)/shard_map/all_to_all | solution.py:351
  86.6 1.2 copy-start
  91.1 26.3 %all-to-all-start.2 = ((bf16[16,3,16,1024]{3,2,1,0:T(8,128)(2,1)}), bf16[16,3,16,1024]{3,2,1,0:T(8,128)(2,1)S(1)}, u32[]{:S(2)}, u32[]{:S(2)}) async-start(bf16[16,3,16,1024]{3,2,1,0:T(8,128)(2,1)} %copy-done), calls=%async_computation.2 | async-start | bytes 3145728 | tf_op jit(solution)/shard_map/all_to_all | solution.py:351
  95.4 21.9 %copy-start.1 = (bf16[2,512,256]{2,1,0:T(8,128)(2,1)S(1)}, bf16[2,512,256]{2,1,0:T(8,128)(2,1)}, u32[]{:S(2)}) copy-start(bf16[2,512,256]{2,1,0:T(8,128)(2,1)} %constant.26.clone.edge_ref) | copy-start | bytes 1572868
  117.3 1.0 copy-start.2

commit v5 on v4

--- a/solution.py
+++ b/solution.py
@@ -24,16 +24,15 @@
 UNIT = 16
 GROUPS = 16
 BLOCKS = 4
-CHUNKS = 2
-LANES = 512
-STEP = 2
+LANES = 256
+STEP = 4
 COILS = 4
 ROWS = 32
 TAPS = 4
 SPAN = 7
 PAIR = 2 * COILS * ROWS
 HALF = PAIR // 2
-PLANES = 8
+PLANES = 16
 HALO = 4
 
 
@@ -73,23 +72,21 @@
 
 def x_tables():
     main = []
-    for chunk in range(CHUNKS):
-        cols = []
-        for group in range(GROUPS):
-            planes = (16 * group + PLANES * chunk + np.arange(PLANES) - 1) % GX
-            cols += [x_columns(planes, 0), x_columns(planes, 1)]
-        main.append(np.concatenate(cols, 1))
+    for group in range(GROUPS):
+        for half in range(2):
+            planes = (PLANES * group + 8 * half + np.arange(8) - 1) % GX
+            main += [x_columns(planes, 0), x_columns(planes, 1)]
     halo = []
     for coil in range(2):
         cols = []
         for group in range(GROUPS):
-            planes = (16 * group + 16 + np.arange(HALO) - 1) % GX
+            planes = (PLANES * group + PLANES + np.arange(HALO) - 1) % GX
             real = np.arange(HALO) < 3
             for other in range(2):
                 keep = real & (other == coil)
                 cols += [x_columns(planes, part) * keep for part in range(2)]
         halo.append(np.concatenate(cols, 1))
-    return np.stack(main).astype(ml_dtypes.bfloat16), np.stack(halo).astype(ml_dtypes.bfloat16)
+    return np.concatenate(main, 1).astype(ml_dtypes.bfloat16), np.stack(halo).astype(ml_dtypes.bfloat16)
 
 
 def tap_rows(first, second, lanes):
@@ -161,132 +158,113 @@
     return jnp.swapaxes(along.reshape(planes, HALF, 2 * GZ), 0, 1)
 
 
-def gather(samples_ref, start, offset):
+def gather(samples_ref, start, half, offset):
     per = 128 // UNIT
     lane = lax.broadcasted_iota(jnp.int32, (16, 128), 1) // UNIT
     pieces = []
     for piece in range(LANES // 128):
         joined = None
         for k in range(per):
-            rows = samples_ref[start + piece * per + k].astype(jnp.float32)
+            rows = samples_ref[half, start + piece * per + k].astype(jnp.float32)
             rows = pltpu.roll(rows, (128 + UNIT * k - offset) % 128, 1)
             joined = rows if joined is None else jnp.where(lane == k, rows, joined)
         pieces.append(joined)
     return jnp.concatenate(pieces, 1)
 
 
-def largest(samples_ref):
+def largest(samples_ref, half):
     def step(index, seen):
-        return jnp.maximum(seen, jnp.abs(samples_ref[index].astype(jnp.float32)))
+        return jnp.maximum(seen, jnp.abs(samples_ref[half, index].astype(jnp.float32)))
 
     seen = lax.fori_loop(0, SOURCES, step, jnp.zeros((16, 128), jnp.float32), unroll=8)
     row = lax.broadcasted_iota(jnp.int32, (16, 128), 0)
     return jnp.max(jnp.where(row % 8 < 4, seen, 0.0), axis=0, keepdims=True)
 
 
-def grid_kernel(last, samples_ref, y_ref, z_ref, carry_ref, out_ref, carried_ref, pair_ref, dense_ref, acc_ref):
-    q = pl.program_id(0)
-
-    @pl.when(q == 0)
-    def _():
-        acc_ref[0:HALO] = carry_ref[...]
-        acc_ref[HALO:] = jnp.zeros((PLANES, PAIR, GZ), jnp.float32)
-
+def grid_kernel(source_ref, y_ref, z_ref, out_ref, samples_ref, pair_ref, dense_ref, acc_ref, list_ref):
+    for half in range(2):
+        samples_ref[half] = source_ref[:, :, half * 128 : (half + 1) * 128]
+    units = 128 // UNIT
+    unit = lax.broadcasted_iota(jnp.int32, (1, 128), 1) // UNIT
+    count = jnp.int32(0)
+    for half in range(2):
+        seen = largest(samples_ref, half)
+        for place in range(units):
+            list_ref[count] = half * units + place
+            some = jnp.max(jnp.where(unit == place, seen, 0.0)) > 0.0
+            count = count + some.astype(jnp.int32)
+    acc_ref[...] = jnp.zeros(acc_ref.shape, jnp.float32)
     y_tab = y_ref[...]
-    seen = largest(samples_ref)
-    unit = lax.broadcasted_iota(jnp.int32, (1, 128), 1) // UNIT
 
     def step(index, _):
-        place = q * (CAP // UNIT) + index
-
-        @pl.when(jnp.max(jnp.where(unit == place, seen, 0.0)) > 0.0)
-        def _():
-            for part in range(STEP):
-                packed = gather(samples_ref, part * (LANES // UNIT), place * UNIT)
-                build(packed, y_tab, pair_ref, dense_ref, part * LANES, LANES)
-            product = lax.dot_general(
-                pair_ref[...],
-                dense_ref[...],
-                (((1,), (1,)), ((), ())),
-                preferred_element_type=jnp.float32,
-            )
-            here = pl.ds(4 * q, SPAN)
-            acc_ref[here] = acc_ref[here] + product.reshape(SPAN, PAIR, GZ)
-
+        block = list_ref[index]
+        for part in range(STEP):
+            start = part * (LANES // UNIT)
+            packed = gather(samples_ref, start, block // units, block % units * UNIT)
+            build(packed, y_tab, pair_ref, dense_ref, part * LANES, LANES)
+        here = pl.ds(4 * (block // (CAP // UNIT)), SPAN)
+        product = lax.dot_general(
+            pair_ref[...], dense_ref[...], (((1,), (1,)), ((), ())), preferred_element_type=jnp.float32
+        )
+        acc_ref[here] = acc_ref[here] + product.reshape(SPAN, PAIR, GZ)
         return 0
 
-    lax.fori_loop(0, CAP // UNIT, step, 0)
-
-    @pl.when(q == BLOCKS // CHUNKS - 1)
-    def _():
-        z_tab = z_ref[...]
-        lines = transform_z(acc_ref[0:PLANES], z_tab)
+    lax.fori_loop(0, count, step, 0)
+
+    z_tab = z_ref[...]
+    for first in range(0, PLANES, 8):
+        lines = transform_z(acc_ref[first : first + 8], z_tab)
         for coil in range(COILS):
             for row in range(ROWS):
                 line = lines[coil * ROWS + row]
-                both = jnp.concatenate([line[:, :GZ], line[:, GZ:]], 0).astype(jnp.bfloat16)
-                out_ref[
-                    (row // 4) * 2 + coil // 2, coil % 2, :, (row % 4) * GZ : (row % 4 + 1) * GZ
-                ] = both
-        if last:
-            edge = transform_z(acc_ref[PLANES:], z_tab)
-            for coil in range(0, COILS, 2):
-                for row in range(ROWS):
-                    pieces = []
-                    for inner in range(2):
-                        line = edge[(coil + inner) * ROWS + row]
-                        pieces += [line[:, :GZ], line[:, GZ:]]
+                for part in range(2):
                     out_ref[
-                        (row // 4) * 2 + coil // 2, 2, :, (row % 4) * GZ : (row % 4 + 1) * GZ
-                    ] = jnp.concatenate(pieces, 0).astype(jnp.bfloat16)
-        else:
-            carried_ref[...] = acc_ref[PLANES:]
-
-
-def grid_chunk(samples, y_tab, z_tab, carry, chunk):
-    blocks = BLOCKS // CHUNKS
-    last = chunk == CHUNKS - 1
-    tiles = 3 if last else 2
-    flops = 2 * SPAN * PAIR * GZ * SOURCES * CAP * blocks + 2 * PLANES * PAIR * GZ * 2 * GZ
+                        (row // 4) * 2 + coil // 2,
+                        (coil % 2) * 2 + first // 8,
+                        part * 8 : part * 8 + 8,
+                        (row % 4) * GZ : (row % 4 + 1) * GZ,
+                    ] = line[:, part * GZ : (part + 1) * GZ].astype(jnp.bfloat16)
+    edge = transform_z(acc_ref[PLANES:], z_tab)
+    for coil in range(0, COILS, 2):
+        for row in range(ROWS):
+            pieces = []
+            for inner in range(2):
+                line = edge[(coil + inner) * ROWS + row]
+                pieces += [line[:, :GZ], line[:, GZ:]]
+            out_ref[
+                (row // 4) * 2 + coil // 2, 4, :, (row % 4) * GZ : (row % 4 + 1) * GZ
+            ] = jnp.concatenate(pieces, 0).astype(jnp.bfloat16)
+
+
+def grid_all(samples, y_tab, z_tab):
+    flops = 2 * SPAN * PAIR * GZ * SOURCES * CAP * BLOCKS
     return pl.pallas_call(
-        lambda *refs: grid_kernel(last, *refs),
-        grid=(blocks,),
-        in_specs=[
-            pl.BlockSpec((SOURCES, 16, blocks * CAP), lambda q: (0, 0, chunk)),
-            pl.BlockSpec((2 * ROWS, GY), lambda q: (0, 0)),
-            pl.BlockSpec((2 * GZ, 2 * GZ), lambda q: (0, 0)),
-            pl.BlockSpec((HALO, PAIR, GZ), lambda q: (0, 0, 0)),
-        ],
-        out_specs=[
-            pl.BlockSpec((GROUPS, tiles, 16, 4 * GZ), lambda q: (0, 0, 0, 0)),
-            pl.BlockSpec((HALO, PAIR, GZ), lambda q: (0, 0, 0)),
-        ],
-        out_shape=[
-            jax.ShapeDtypeStruct((GROUPS, tiles, 16, 4 * GZ), jnp.bfloat16),
-            jax.ShapeDtypeStruct((HALO, PAIR, GZ), jnp.float32),
-        ],
+        grid_kernel,
+        out_shape=jax.ShapeDtypeStruct((GROUPS, 5, 16, 4 * GZ), jnp.bfloat16),
         scratch_shapes=[
+            pltpu.VMEM((2, SOURCES, 16, 128), jnp.bfloat16),
             pltpu.VMEM((SPAN * PAIR, STEP * LANES), jnp.bfloat16),
             pltpu.VMEM((GZ, STEP * LANES), jnp.bfloat16),
             pltpu.VMEM((PLANES + HALO, PAIR, GZ), jnp.float32),
+            pltpu.SMEM((17,), jnp.int32),
         ],
-        compiler_params=pltpu.CompilerParams(vmem_limit_bytes=48 * 2**20),
+        compiler_params=pltpu.CompilerParams(vmem_limit_bytes=56 * 2**20),
         cost_estimate=pl.CostEstimate(
             flops=flops, bytes_accessed=4 * 2**20, transcendentals=0
         ),
-        name="grid_chunk",
-    )(samples, y_tab, z_tab, carry)
-
-
-def combine_kernel(first_ref, second_ref, main_ref, edge_ref, maps_ref, out_ref):
+        name="grid_all",
+    )(samples, y_tab, z_tab)
+
+
+def combine_kernel(turned_ref, main_ref, edge_ref, maps_ref, out_ref):
     total = [None, None]
     depth = GROUPS * 16
-    edge_rows = second_ref[:, 2].reshape(depth, GZ)
+    edge_rows = turned_ref[:, 4].reshape(depth, GZ)
     for coil in range(2):
-        image = jnp.dot(edge_ref[coil], edge_rows, preferred_element_type=jnp.float32)
-        for chunk, ref in enumerate((first_ref, second_ref)):
-            rows = ref[:, coil].reshape(depth, GZ)
-            image = image + jnp.dot(main_ref[chunk], rows, preferred_element_type=jnp.float32)
+        rows = turned_ref[:, 2 * coil : 2 * coil + 2].reshape(2 * depth, GZ)
+        image = jnp.dot(main_ref[...], rows, preferred_element_type=jnp.float32) + jnp.dot(
+            edge_ref[coil], edge_rows, preferred_element_type=jnp.float32
+        )
         image_re, image_im = image[:GX], image[GX:]
         map_re = maps_ref[coil, 0].astype(jnp.float32)
         map_im = maps_ref[coil, 1].astype(jnp.float32)
@@ -297,33 +275,33 @@
         out_ref[:, part] = total[part].astype(jnp.bfloat16).reshape(8, GX // 8, GZ)
 
 
-def combine(first, second, maps):
+def combine(turned, maps):
     main_tab, edge_tab = x_tables()
     depth = GROUPS * 16
     return pl.pallas_call(
         combine_kernel,
         grid=(4,),
         in_specs=[
-            pl.BlockSpec((GROUPS, 2, 16, GZ), lambda y: (0, 0, 0, y)),
-            pl.BlockSpec((GROUPS, 3, 16, GZ), lambda y: (0, 0, 0, y)),
-            pl.BlockSpec((CHUNKS, 2 * GX, depth), lambda y: (0, 0, 0)),
+            pl.BlockSpec((GROUPS, 5, 16, GZ), lambda y: (0, 0, 0, y)),
+            pl.BlockSpec((2 * GX, 2 * depth), lambda y: (0, 0)),
             pl.BlockSpec((2, 2 * GX, depth), lambda y: (0, 0, 0)),
             pl.BlockSpec((2, 2, GX, GZ), lambda y: (0, 0, 0, y)),
         ],
         out_specs=pl.BlockSpec((8, 2, GX // 8, GZ), lambda y: (0, 0, 0, y)),
         out_shape=jax.ShapeDtypeStruct((8, 2, GX // 8, 4 * GZ), jnp.bfloat16),
-        compiler_params=pltpu.CompilerParams(vmem_limit_bytes=48 * 2**20),
+        compiler_params=pltpu.CompilerParams(vmem_limit_bytes=56 * 2**20),
         cost_estimate=pl.CostEstimate(
             flops=2 * 2 * 2 * GX * 3 * depth * 4 * GZ, bytes_accessed=8 * 2**20, transcendentals=0
         ),
         name="combine",
-    )(first, second, jnp.asarray(main_tab), jnp.asarray(edge_tab), maps)
+    )(turned, jnp.asarray(main_tab), jnp.asarray(edge_tab), maps)
 
 
 def pack_kernel(values_ref, offsets_ref, cells_ref, slots_ref, out_ref):
     used = slots_ref[...] < SLOTS
     cells = cells_ref[...]
-    rows = [jnp.where(used, values_ref[r : r + 1].astype(jnp.float32), 0.0) for r in range(4)]
+    values = [values_ref[coil].astype(jnp.float32) for coil in range(2)]
+    rows = [jnp.where(used, values[r // 2][r % 2 : r % 2 + 1], 0.0) for r in range(4)]
     spots = (cells // (GY * GZ), cells // GZ % GY, cells % GZ)
     first = lax.axis_index("core") == 0
     for axis in range(3):
@@ -342,9 +320,9 @@
     return pl.pallas_call(
         pack_kernel,
         out_shape=jax.ShapeDtypeStruct((ZH * GROUPS, 8, BLOCKS * CAP), jnp.bfloat16),
-        compiler_params=pltpu.CompilerParams(vmem_limit_bytes=16 * 2**20),
+        compiler_params=pltpu.CompilerParams(vmem_limit_bytes=56 * 2**20),
         name="pack",
-    )(values.reshape(4, SLOTS), offsets, cells.reshape(1, SLOTS), slots.reshape(1, SLOTS))
+    )(values, offsets, cells.reshape(1, SLOTS), slots.reshape(1, SLOTS))
 
 
 def turn(array, axes):
@@ -360,13 +338,9 @@
         jnp.asarray(y_table()), lax.axis_index("zh"), 0, keepdims=False
     )
     z_tab = jnp.asarray(z_table())
-    carry = jnp.zeros((HALO, PAIR, GZ), jnp.float32)
-    turned = []
-    for chunk in range(CHUNKS):
-        part, carry = grid_chunk(samples, y_tab, z_tab, carry, chunk)
-        turned.append(turn(part, planes))
+    turned = turn(grid_all(samples, y_tab, z_tab), planes)
     maps = sensitivity.reshape(2, 2, GX, 4 * GZ)
-    partial = turn(combine(*turned, maps), ("y", "core"))
+    partial = turn(combine(turned, maps), ("y", "core"))
     image = jnp.sum(partial.astype(jnp.float32), axis=0)
     return image.reshape(2, GX // 8, 4, GZ)
 

time: 145 us -> 149 us (1.028); the launches traced: 144 us -> 146 us
  waiting for transfers between devices: 50.8 us -> 58.6 us
  starting transfers between devices: 33.9 us -> 29.6 us
  local copies, waits for them, and re-layouts: 11.3 us -> 8.97 us
    all_to_all x3 -> x2, waiting for transfers between devices: 50.8 us -> 58.6 us  [turn(): return lax.all_to_all(array, axes, split_axis=0, concat_axis=0, tiled=True)]
    all_to_all x3 -> x2, starting transfers between devices: 33.9 us -> 29.6 us  [turn(): return lax.all_to_all(array, axes, split_axis=0, concat_axis=0, tiled=True)]
    unnamed x14 -> x4, local copies, waits for them, and re-layouts: 4.39 us -> 2.31 us
    pallas_call x2 -> x1, Pallas kernels: 22.2 us -> 20.7 us  [grid_all(): pl.pallas_call(grid_kernel, out_shape=jax.ShapeDtypeStruct((GROUPS, 5, 16...]
  transfers between devices with their start and end apart: 3 -> 2, of which waited for: 3 -> 2; matrix products, arithmetic and copies ran while one was open for 4% -> 4% of each run, Pallas kernels for 8% -> 0%
where the time goes in v5:
time: 149 us; the launch traced here: 146 us
  waiting for transfers between devices  58.6 us (39%)
  starting transfers between devices  29.6 us (20%)
  Pallas kernels  28.3 us (19%)
  blocking collectives  20.4 us (14%)
  local copies, waits for them, and re-layouts  8.97 us (6%)
    all_to_all x2, waiting for transfers between devices, turn(): return lax.all_to_all(array, axes, split_axis=0, concat_axis=0, tiled=True)  58.6 us
    all_to_all x2, starting transfers between devices, turn(): return lax.all_to_all(array, axes, split_axis=0, concat_axis=0, tiled=True)  29.6 us
    pallas_call x1, Pallas kernels, grid_all(): pl.pallas_call(grid_kernel, out_shape=jax.ShapeDtypeStruct((GROUPS, 5, 16...  20.7 us
    all_to_all x1, blocking collectives, turn(): return lax.all_to_all(array, axes, split_axis=0, concat_axis=0, tiled=True)  20.4 us
    pallas_call x1, Pallas kernels, combine(): pl.pallas_call(combine_kernel, grid=(4,), in_specs=[pl.BlockSpec((GROUPS,...  5.92 us
    reshape x1, local copies, waits for them, and re-layouts, body(): maps = sensitivity.reshape(2, 2, GX, 4 * GZ)  4.46 us
  transfers between devices with their start and end apart: 2, of which 2 were waited for; matrix products, arithmetic and copies ran while one was open for 4% of the time, Pallas kernels for 0%

profile of v5, /device:TPU:1, one launch (start us, length us, event | category | flops | bytes accessed | tf_op | source)
XLA Modules:
  0.0 146.0 jit_solution(385123115372654051)
XLA Ops:
  0.0 1.7 %pack.1 = bf16[128,8,256]{2,1,0:T(8,128)(2,1)} custom-call(bf16[2,2,4096]{2,1,0:T(2,128)(2,1)} %values_ref.1, bf16[3,4096]{1,0:T(4,128)(2,1)} %offsets_ref.1, s32[1,4096]{1,0:T(1,128)} %bitcast.6, s32[1,4096]{1,0:T(1,128)} %bitcast.7), custom_call_target="tpu_custom_call" | custom-call | tf_op jit(solution)/shard_map/pack/pallas_call | solution.py:320
  1.7 20.4 %all-to-all-start = ((bf16[128,8,256]{2,1,0:T(8,128)(2,1)}), bf16[128,8,256]{2,1,0:T(8,128)(2,1)S(1)}, u32[]{:S(2)}, u32[]{:S(2)}) async-start(bf16[128,8,256]{2,1,0:T(8,128)(2,1)} %pack.1), calls=%async_computation | async-start | bytes 1048576 | tf_op jit(solution)/shard_map/all_to_all | solution.py:329
  22.1 1.4 dynamic-slice_bitcast_fusion.y_ref
  23.5 29.4 %all-to-all-done = bf16[128,8,256]{2,1,0:T(8,128)(2,1)S(1)} async-done(((bf16[128,8,256]{2,1,0:T(8,128)(2,1)}), bf16[128,8,256]{2,1,0:T(8,128)(2,1)S(1)}, u32[]{:S(2)}, u32[]{:S(2)}) %all-to-all-start) | async-done | bytes 524320 | tf_op jit(solution)/shard_map/all_to_all | solution.py:329
  52.9 0.0 copy-start.1
  52.9 0.8 copy-done.1
  53.7 20.7 %grid_all.1 = bf16[16,5,16,1024]{3,2,1,0:T(8,128)(2,1)} custom-call(bf16[64,16,256]{2,1,0:T(8,128)(2,1)} %bitcast.5, bf16[64,256]{1,0:T(8,128)(2,1)} %dynamic-slice_bitcast_fusion.y_ref, bf16[512,512]{1,0:T(8,128)(2,1)} %constant.23.clone.z_ref), custom_call_target="tpu_custom_call" | custom-call | flops 15032385536 | bytes 4194304 | tf_op jit(solution)/shard_map/grid_all/pallas_call | solution.py:241
  74.4 9.2 %all-to-all-start.1 = ((bf16[16,5,16,1024]{3,2,1,0:T(8,128)(2,1)}), bf16[16,5,16,1024]{3,2,1,0:T(8,128)(2,1)S(1)}, u32[]{:S(2)}, u32[]{:S(2)}) async-start(bf16[16,5,16,1024]{3,2,1,0:T(8,128)(2,1)} %grid_all.1), calls=%async_computation.1 | async-start | bytes 5242880 | tf_op jit(solution)/shard_map/all_to_all | solution.py:329
  83.6 4.5 %reshape.18.maps_ref = bf16[2,2,256,1024]{3,2,1,0:T(8,128)(2,1)} reshape(bf16[2,2,256,4,256]{4,3,2,1,0:T(4,128)(2,1)} %param.13) | data formatting | bytes 4194304 | tf_op jit(solution)/shard_map/reshape | solution.py:342
  88.0 29.2 %all-to-all-done.1.turned_ref = bf16[16,5,16,1024]{3,2,1,0:T(8,128)(2,1)S(1)} async-done(((bf16[16,5,16,1024]{3,2,1,0:T(8,128)(2,1)}), bf16[16,5,16,1024]{3,2,1,0:T(8,128)(2,1)S(1)}, u32[]{:S(2)}, u32[]{:S(2)}) %all-to-all-start.1) | async-done | bytes 2621472 | tf_op jit(solution)/shard_map/all_to_all | solution.py:329
  117.2 0.0 copy-start
  117.2 1.5 %copy-done = bf16[16,5,16,1024]{3,2,1,0:T(8,128)(2,1)} copy-done((bf16[16,5,16,1024]{3,2,1,0:T(8,128)(2,1)}, bf16[16,5,16,1024]{3,2,1,0:T(8,128)(2,1)S(1)}, u32[]{:S(2)}) %copy-start) | copy-done | bytes 2621464
  118.7 5.9 %combine.1 = bf16[8,2,32,1024]{3,2,1,0:T(8,128)(2,1)} custom-call(bf16[16,5,16,1024]{3,2,1,0:T(8,128)(2,1)} %copy-done, bf16[512,512]{1,0:T(8,128)(2,1)} %constant.24.clone.main_ref, bf16[2,512,256]{2,1,0:T(8,128)(2,1)} %constant.25.clone.edge_ref, bf16[2,2,256,1024]{3,2,1,0:T(8,128)(2,1)} %reshape.18.maps_ref), custom_call_target="tpu_custom_call" | custom-call | flops 1610612736 | bytes 8388608 | tf_op jit(solution)/shard_map/combine/pallas_call | solution.py:281
  124.6 20.4 %all_to_all.15 = bf16[8,2,32,1024]{3,2,1,0:T(8,128)(2,1)S(1)} all-to-all(bf16[8,2,32,1024]{3,2,1,0:T(8,128)(2,1)} %combine.1), channel_id=1, replica_groups=mesh['zh'=8,'zl'=2,'x'=4,'y'=4,'core'=2] {'y','core'}, dimensions={0} | all-to-all | bytes 2097152 | tf_op jit(solution)/shard_map/all_to_all | solution.py:329
  145.0 0.2 convert_reduce_fusion
  145.2 0.8 reshape.19
Async XLA Ops:
  1.7 51.2 %all-to-all-start = ((bf16[128,8,256]{2,1,0:T(8,128)(2,1)}), bf16[128,8,256]{2,1,0:T(8,128)(2,1)S(1)}, u32[]{:S(2)}, u32[]{:S(2)}) async-start(bf16[128,8,256]{2,1,0:T(8,128)(2,1)} %pack.1), calls=%async_computation | async-start | bytes 1048576 | tf_op jit(solution)/shard_map/all_to_all | solution.py:329
  52.9 0.8 copy-start.1
  74.4 42.8 %all-to-all-start.1 = ((bf16[16,5,16,1024]{3,2,1,0:T(8,128)(2,1)}), bf16[16,5,16,1024]{3,2,1,0:T(8,128)(2,1)S(1)}, u32[]{:S(2)}, u32[]{:S(2)}) async-start(bf16[16,5,16,1024]{3,2,1,0:T(8,128)(2,1)} %grid_all.1), calls=%async_computation.1 | async-start | bytes 5242880 | tf_op jit(solution)/shard_map/all_to_all | solution.py:329
  117.2 1.5 %copy-start = (bf16[16,5,16,1024]{3,2,1,0:T(8,128)(2,1)}, bf16[16,5,16,1024]{3,2,1,0:T(8,128)(2,1)S(1)}, u32[]{:S(2)}) copy-start(bf16[16,5,16,1024]{3,2,1,0:T(8,128)(2,1)S(1)} %all-to-all-done.1.turned_ref) | copy-start | bytes 7864324

commit v6 on v5

--- a/solution.py
+++ b/solution.py
@@ -32,7 +32,8 @@
 SPAN = 7
 PAIR = 2 * COILS * ROWS
 HALF = PAIR // 2
-PLANES = 16
+CHUNKS = 2
+PLANES = 8
 HALO = 4
 
 
@@ -72,21 +73,23 @@
 
 def x_tables():
     main = []
-    for group in range(GROUPS):
-        for half in range(2):
-            planes = (PLANES * group + 8 * half + np.arange(8) - 1) % GX
-            main += [x_columns(planes, 0), x_columns(planes, 1)]
+    for chunk in range(CHUNKS):
+        cols = []
+        for group in range(GROUPS):
+            planes = (16 * group + PLANES * chunk + np.arange(PLANES) - 1) % GX
+            cols += [x_columns(planes, 0), x_columns(planes, 1)]
+        main.append(np.concatenate(cols, 1))
     halo = []
     for coil in range(2):
         cols = []
         for group in range(GROUPS):
-            planes = (PLANES * group + PLANES + np.arange(HALO) - 1) % GX
+            planes = (16 * group + 16 + np.arange(HALO) - 1) % GX
             real = np.arange(HALO) < 3
             for other in range(2):
                 keep = real & (other == coil)
                 cols += [x_columns(planes, part) * keep for part in range(2)]
         halo.append(np.concatenate(cols, 1))
-    return np.concatenate(main, 1).astype(ml_dtypes.bfloat16), np.stack(halo).astype(ml_dtypes.bfloat16)
+    return np.stack(main).astype(ml_dtypes.bfloat16), np.stack(halo).astype(ml_dtypes.bfloat16)
 
 
 def tap_rows(first, second, lanes):
@@ -158,49 +161,57 @@
     return jnp.swapaxes(along.reshape(planes, HALF, 2 * GZ), 0, 1)
 
 
-def gather(samples_ref, start, half, offset):
+def gather(samples_ref, start, offset):
     per = 128 // UNIT
     lane = lax.broadcasted_iota(jnp.int32, (16, 128), 1) // UNIT
     pieces = []
     for piece in range(LANES // 128):
         joined = None
         for k in range(per):
-            rows = samples_ref[half, start + piece * per + k].astype(jnp.float32)
+            rows = samples_ref[start + piece * per + k].astype(jnp.float32)
             rows = pltpu.roll(rows, (128 + UNIT * k - offset) % 128, 1)
             joined = rows if joined is None else jnp.where(lane == k, rows, joined)
         pieces.append(joined)
     return jnp.concatenate(pieces, 1)
 
 
-def largest(samples_ref, half):
+def filled(samples_ref):
     def step(index, seen):
-        return jnp.maximum(seen, jnp.abs(samples_ref[half, index].astype(jnp.float32)))
+        return jnp.maximum(seen, jnp.abs(samples_ref[index].astype(jnp.float32)))
 
     seen = lax.fori_loop(0, SOURCES, step, jnp.zeros((16, 128), jnp.float32), unroll=8)
     row = lax.broadcasted_iota(jnp.int32, (16, 128), 0)
-    return jnp.max(jnp.where(row % 8 < 4, seen, 0.0), axis=0, keepdims=True)
-
-
-def grid_kernel(source_ref, y_ref, z_ref, out_ref, samples_ref, pair_ref, dense_ref, acc_ref, list_ref):
-    for half in range(2):
-        samples_ref[half] = source_ref[:, :, half * 128 : (half + 1) * 128]
-    units = 128 // UNIT
-    unit = lax.broadcasted_iota(jnp.int32, (1, 128), 1) // UNIT
+    seen = jnp.max(jnp.where(row % 8 < 4, seen, 0.0), axis=0, keepdims=True)
+    seen = jnp.broadcast_to(seen, (8, 128))
+    for shift in (8, 4, 2, 1):
+        seen = jnp.maximum(seen, pltpu.roll(seen, shift, 1))
+    lane = lax.broadcasted_iota(jnp.int32, (8, 128), 1)
+    place = lax.broadcasted_iota(jnp.int32, (8, 128), 0)
+    hit = (seen > 0.0) & (lane == place * UNIT + UNIT - 1)
+    return jnp.sum(jnp.where(hit, (1 << place).astype(jnp.float32), 0.0)).astype(jnp.int32)
+
+
+def grid_kernel(last, samples_ref, y_ref, z_ref, *refs):
+    if last:
+        carry_ref, out_ref, pair_ref, dense_ref, acc_ref, list_ref = refs
+    else:
+        out_ref, carried_ref, pair_ref, dense_ref, acc_ref, list_ref = refs
+    bits = filled(samples_ref)
     count = jnp.int32(0)
-    for half in range(2):
-        seen = largest(samples_ref, half)
-        for place in range(units):
-            list_ref[count] = half * units + place
-            some = jnp.max(jnp.where(unit == place, seen, 0.0)) > 0.0
-            count = count + some.astype(jnp.int32)
-    acc_ref[...] = jnp.zeros(acc_ref.shape, jnp.float32)
+    for place in range(128 // UNIT):
+        list_ref[count] = place
+        count = count + ((bits >> place) & 1)
+    if last:
+        acc_ref[0:HALO] = carry_ref[...]
+        acc_ref[HALO:] = jnp.zeros((PLANES, PAIR, GZ), jnp.float32)
+    else:
+        acc_ref[...] = jnp.zeros((PLANES + HALO, PAIR, GZ), jnp.float32)
     y_tab = y_ref[...]
 
     def step(index, _):
         block = list_ref[index]
         for part in range(STEP):
-            start = part * (LANES // UNIT)
-            packed = gather(samples_ref, start, block // units, block % units * UNIT)
+            packed = gather(samples_ref, part * (LANES // UNIT), block * UNIT)
             build(packed, y_tab, pair_ref, dense_ref, part * LANES, LANES)
         here = pl.ds(4 * (block // (CAP // UNIT)), SPAN)
         product = lax.dot_general(
@@ -212,89 +223,108 @@
     lax.fori_loop(0, count, step, 0)
 
     z_tab = z_ref[...]
-    for first in range(0, PLANES, 8):
-        lines = transform_z(acc_ref[first : first + 8], z_tab)
+    lines = transform_z(acc_ref[0:PLANES], z_tab)
+    if last:
+        edge = transform_z(acc_ref[PLANES:], z_tab)
+    else:
+        carried_ref[...] = acc_ref[PLANES:]
+    for row in range(ROWS):
+        owner = (row // 4) * 2 + row % 4 // 2
+        here = slice(row % 2 * GZ, (row % 2 + 1) * GZ)
         for coil in range(COILS):
-            for row in range(ROWS):
-                line = lines[coil * ROWS + row]
-                for part in range(2):
-                    out_ref[
-                        (row // 4) * 2 + coil // 2,
-                        (coil % 2) * 2 + first // 8,
-                        part * 8 : part * 8 + 8,
-                        (row % 4) * GZ : (row % 4 + 1) * GZ,
-                    ] = line[:, part * GZ : (part + 1) * GZ].astype(jnp.bfloat16)
-    edge = transform_z(acc_ref[PLANES:], z_tab)
-    for coil in range(0, COILS, 2):
-        for row in range(ROWS):
+            line = lines[coil * ROWS + row]
+            out_ref[owner, coil, :, here] = jnp.concatenate([line[:, :GZ], line[:, GZ:]], 0).astype(
+                jnp.bfloat16
+            )
+        for pair in range(COILS // 2) if last else ():
             pieces = []
             for inner in range(2):
-                line = edge[(coil + inner) * ROWS + row]
+                line = edge[(2 * pair + inner) * ROWS + row]
                 pieces += [line[:, :GZ], line[:, GZ:]]
-            out_ref[
-                (row // 4) * 2 + coil // 2, 4, :, (row % 4) * GZ : (row % 4 + 1) * GZ
-            ] = jnp.concatenate(pieces, 0).astype(jnp.bfloat16)
-
-
-def grid_all(samples, y_tab, z_tab):
-    flops = 2 * SPAN * PAIR * GZ * SOURCES * CAP * BLOCKS
+            out_ref[owner, COILS + pair, :, here] = jnp.concatenate(pieces, 0).astype(jnp.bfloat16)
+
+
+def grid_chunk(samples, y_tab, z_tab, chunk, carry=None):
+    last = carry is not None
+    tiles = COILS + (COILS // 2 if last else 0)
+    flops = 2 * SPAN * PAIR * GZ * SOURCES * CAP * BLOCKS // CHUNKS
+    edges = (HALO, PAIR, GZ)
+    in_specs = [
+        pl.BlockSpec((SOURCES, 16, 128), lambda q: (0, 0, chunk)),
+        pl.BlockSpec((2 * ROWS, GY), lambda q: (0, 0)),
+        pl.BlockSpec((2 * GZ, 2 * GZ), lambda q: (0, 0)),
+    ]
+    out_specs = [pl.BlockSpec((GROUPS, tiles, 16, 2 * GZ), lambda q: (0, 0, 0, 0))]
+    out_shape = [jax.ShapeDtypeStruct((GROUPS, tiles, 16, 2 * GZ), jnp.bfloat16)]
+    operands = [samples, y_tab, z_tab]
+    if last:
+        in_specs.append(pl.BlockSpec(edges, lambda q: (0, 0, 0)))
+        operands.append(carry)
+    else:
+        out_specs.append(pl.BlockSpec(edges, lambda q: (0, 0, 0)))
+        out_shape.append(jax.ShapeDtypeStruct(edges, jnp.float32))
     return pl.pallas_call(
-        grid_kernel,
-        out_shape=jax.ShapeDtypeStruct((GROUPS, 5, 16, 4 * GZ), jnp.bfloat16),
+        lambda *refs: grid_kernel(last, *refs),
+        grid=(1,),
+        in_specs=in_specs,
+        out_specs=out_specs,
+        out_shape=out_shape,
         scratch_shapes=[
-            pltpu.VMEM((2, SOURCES, 16, 128), jnp.bfloat16),
             pltpu.VMEM((SPAN * PAIR, STEP * LANES), jnp.bfloat16),
             pltpu.VMEM((GZ, STEP * LANES), jnp.bfloat16),
             pltpu.VMEM((PLANES + HALO, PAIR, GZ), jnp.float32),
-            pltpu.SMEM((17,), jnp.int32),
+            pltpu.SMEM((9,), jnp.int32),
         ],
-        compiler_params=pltpu.CompilerParams(vmem_limit_bytes=56 * 2**20),
-        cost_estimate=pl.CostEstimate(
-            flops=flops, bytes_accessed=4 * 2**20, transcendentals=0
-        ),
-        name="grid_all",
-    )(samples, y_tab, z_tab)
-
-
-def combine_kernel(turned_ref, main_ref, edge_ref, maps_ref, out_ref):
+        compiler_params=pltpu.CompilerParams(vmem_limit_bytes=36 * 2**20),
+        cost_estimate=pl.CostEstimate(flops=flops, bytes_accessed=4 * 2**20, transcendentals=0),
+        name="grid_chunk",
+    )(*operands)
+
+
+def combine_kernel(first_ref, second_ref, main_ref, edge_ref, own_ref, other_ref, out_ref):
+    core = lax.axis_index("core")
     total = [None, None]
     depth = GROUPS * 16
-    edge_rows = turned_ref[:, 4].reshape(depth, GZ)
-    for coil in range(2):
-        rows = turned_ref[:, 2 * coil : 2 * coil + 2].reshape(2 * depth, GZ)
-        image = jnp.dot(main_ref[...], rows, preferred_element_type=jnp.float32) + jnp.dot(
-            edge_ref[coil], edge_rows, preferred_element_type=jnp.float32
-        )
-        image_re, image_im = image[:GX], image[GX:]
-        map_re = maps_ref[coil, 0].astype(jnp.float32)
-        map_im = maps_ref[coil, 1].astype(jnp.float32)
-        real = map_re * image_re + map_im * image_im
-        imag = map_re * image_im - map_im * image_re
-        total = [real, imag] if coil == 0 else [total[0] + real, total[1] + imag]
+    for maps_ref, pair in ((own_ref, core), (other_ref, 1 - core)):
+        edge_rows = second_ref[:, COILS + pair].reshape(depth, GZ)
+        for coil in range(2):
+            image = jnp.dot(edge_ref[coil], edge_rows, preferred_element_type=jnp.float32)
+            for chunk, ref in enumerate((first_ref, second_ref)):
+                rows = ref[:, 2 * pair + coil].reshape(depth, GZ)
+                image = image + jnp.dot(main_ref[chunk], rows, preferred_element_type=jnp.float32)
+            image_re, image_im = image[:GX], image[GX:]
+            map_re = maps_ref[coil, 0].astype(jnp.float32)
+            map_im = maps_ref[coil, 1].astype(jnp.float32)
+            real = map_re * image_re + map_im * image_im
+            imag = map_re * image_im - map_im * image_re
+            total = [real, imag] if total[0] is None else [total[0] + real, total[1] + imag]
     for part in range(2):
         out_ref[:, part] = total[part].astype(jnp.bfloat16).reshape(8, GX // 8, GZ)
 
 
-def combine(turned, maps):
+def combine(first, second, own, other):
     main_tab, edge_tab = x_tables()
     depth = GROUPS * 16
+    maps = pl.BlockSpec((2, 2, GX, GZ), lambda y: (0, 0, 0, y))
     return pl.pallas_call(
         combine_kernel,
-        grid=(4,),
+        grid=(2,),
         in_specs=[
-            pl.BlockSpec((GROUPS, 5, 16, GZ), lambda y: (0, 0, 0, y)),
-            pl.BlockSpec((2 * GX, 2 * depth), lambda y: (0, 0)),
+            pl.BlockSpec((GROUPS, COILS, 16, GZ), lambda y: (0, 0, 0, y)),
+            pl.BlockSpec((GROUPS, COILS + 2, 16, GZ), lambda y: (0, 0, 0, y)),
+            pl.BlockSpec((CHUNKS, 2 * GX, depth), lambda y: (0, 0, 0)),
             pl.BlockSpec((2, 2 * GX, depth), lambda y: (0, 0, 0)),
-            pl.BlockSpec((2, 2, GX, GZ), lambda y: (0, 0, 0, y)),
+            maps,
+            maps,
         ],
         out_specs=pl.BlockSpec((8, 2, GX // 8, GZ), lambda y: (0, 0, 0, y)),
-        out_shape=jax.ShapeDtypeStruct((8, 2, GX // 8, 4 * GZ), jnp.bfloat16),
-        compiler_params=pltpu.CompilerParams(vmem_limit_bytes=56 * 2**20),
+        out_shape=jax.ShapeDtypeStruct((8, 2, GX // 8, 2 * GZ), jnp.bfloat16),
+        compiler_params=pltpu.CompilerParams(vmem_limit_bytes=36 * 2**20),
         cost_estimate=pl.CostEstimate(
-            flops=2 * 2 * 2 * GX * 3 * depth * 4 * GZ, bytes_accessed=8 * 2**20, transcendentals=0
+            flops=2 * 4 * 2 * GX * 3 * depth * 2 * GZ, bytes_accessed=8 * 2**20, transcendentals=0
         ),
         name="combine",
-    )(turned, jnp.asarray(main_tab), jnp.asarray(edge_tab), maps)
+    )(first, second, jnp.asarray(main_tab), jnp.asarray(edge_tab), own, other)
 
 
 def pack_kernel(values_ref, offsets_ref, cells_ref, slots_ref, out_ref):
@@ -331,6 +361,7 @@
 
 def body(sample_values, sample_offsets, sample_cells, sample_slots, sensitivity):
     packed = pack(sample_values, sample_offsets, sample_cells, sample_slots)
+    packed, sensitivity = lax.optimization_barrier((packed, sensitivity))
     planes = ("zl", "x", "core")
     got = turn(packed, ("zh",) + planes)
     samples = got.reshape(SOURCES, 16, BLOCKS * CAP)
@@ -338,11 +369,20 @@
         jnp.asarray(y_table()), lax.axis_index("zh"), 0, keepdims=False
     )
     z_tab = jnp.asarray(z_table())
-    turned = turn(grid_all(samples, y_tab, z_tab), planes)
-    maps = sensitivity.reshape(2, 2, GX, 4 * GZ)
-    partial = turn(combine(turned, maps), ("y", "core"))
-    image = jnp.sum(partial.astype(jnp.float32), axis=0)
-    return image.reshape(2, GX // 8, 4, GZ)
+    core = lax.axis_index("core")
+
+    def maps(half):
+        rows = lax.dynamic_slice_in_dim(sensitivity, 2 * half, 2, 3)
+        return rows.reshape(2, 2, GX, 2 * GZ)
+
+    other = lax.ppermute(maps(1 - core), "core", [(0, 1), (1, 0)])
+    first, carry = grid_chunk(samples, y_tab, z_tab, 0)
+    first = turn(first, planes)
+    (second,) = grid_chunk(samples, y_tab, z_tab, 1, carry)
+    partial = combine(first, turn(second, planes), maps(core), other)
+    parts = turn(partial, ("y", "core")).reshape(4, 2, 2, GX // 8, 2, GZ)
+    image = jnp.sum(parts.astype(jnp.float32), axis=0)
+    return image.transpose(1, 2, 0, 3, 4).reshape(2, GX // 8, 4, GZ)
 
 
 def solution(mesh):

time: 149 us -> 139 us (0.933); the launches traced: 146 us -> 138 us
  waiting for transfers between devices: 58.6 us -> 43 us
  local copies, waits for them, and re-layouts: 8.97 us -> 18.8 us
  starting transfers between devices: 29.6 us -> 36.2 us
  blocking collectives: 20.4 us -> 14.5 us
  Pallas kernels: 28.3 us -> 24.8 us
    all_to_all x2 -> x3, waiting for transfers between devices: 58.6 us -> 42.6 us  [turn(): return lax.all_to_all(array, axes, split_axis=0, concat_axis=0, tiled=True)]
    all_to_all x1, blocking collectives: 20.4 us -> 14.5 us  [turn(): return lax.all_to_all(array, axes, split_axis=0, concat_axis=0, tiled=True)]
    all_to_all x2 -> x3, starting transfers between devices: 29.6 us -> 34.1 us  [turn(): return lax.all_to_all(array, axes, split_axis=0, concat_axis=0, tiled=True)]
    optimization_barrier x0 -> x1, local copies, waits for them, and re-layouts: none -> 4.29 us  [body(): packed, sensitivity = lax.optimization_barrier((packed, sensitivity))]
    pallas_call x2 -> x3, Pallas kernels: 26.6 us -> 23.1 us  [the longest x2 19.4 us: grid_chunk(): pl.pallas_call(lambda *refs: grid_kernel(last, *refs), grid=(1,), in_spec...]
    dynamic_slice x0 -> x1, local copies, waits for them, and re-layouts: none -> 3.05 us  [maps(): rows = lax.dynamic_slice_in_dim(sensitivity, 2 * half, 2, 3)]
    unnamed x4 -> x12, local copies, waits for them, and re-layouts: 2.31 us -> 4.47 us
    ppermute x0 -> x1, starting transfers between devices: none -> 2.13 us  [body(): other = lax.ppermute(maps(1 - core), 'core', [(0, 1), (1, 0)])]
  transfers between devices with their start and end apart: 2 -> 4, of which waited for: 2 -> 4; matrix products, arithmetic and copies ran while one was open for 4% -> 9% of each run, Pallas kernels for 0% -> 7%
where the time goes in v6:
time: 139 us; the launch traced here: 138 us
  waiting for transfers between devices  43 us (31%)
  starting transfers between devices  36.2 us (26%)
  Pallas kernels  24.8 us (18%)
  local copies, waits for them, and re-layouts  18.8 us (14%)
  blocking collectives  14.5 us (10%)
    all_to_all x3, waiting for transfers between devices, turn(): return lax.all_to_all(array, axes, split_axis=0, concat_axis=0, tiled=True)  42.6 us
    all_to_all x3, starting transfers between devices, turn(): return lax.all_to_all(array, axes, split_axis=0, concat_axis=0, tiled=True)  34.1 us
    pallas_call x2, Pallas kernels, grid_chunk(): pl.pallas_call(lambda *refs: grid_kernel(last, *refs), grid=(1,), in_spec...  19.4 us
    all_to_all x1, blocking collectives, turn(): return lax.all_to_all(array, axes, split_axis=0, concat_axis=0, tiled=True)  14.5 us
    reshape x2, local copies, waits for them, and re-layouts, maps(): return rows.reshape(2, 2, GX, 2 * GZ)  4.67 us
    unnamed x12, local copies, waits for them, and re-layouts  4.47 us
    optimization_barrier x1, local copies, waits for them, and re-layouts, body(): packed, sensitivity = lax.optimization_barrier((packed, sensitivity))  4.29 us
    pallas_call x1, Pallas kernels, combine(): pl.pallas_call(combine_kernel, grid=(2,), in_specs=[pl.BlockSpec((GROUPS,...  3.73 us
  transfers between devices with their start and end apart: 4, of which 4 were waited for; matrix products, arithmetic and copies ran while one was open for 9% of the time, Pallas kernels for 7%

profile of v6, /device:TPU:1, one launch (start us, length us, event | category | flops | bytes accessed | tf_op | source)
XLA Modules:
  0.0 138.0 jit_solution(11269022724125270236)
XLA Ops:
  0.0 1.7 %pack.1 = bf16[128,8,256]{2,1,0:T(8,128)(2,1)} custom-call(bf16[2,2,4096]{2,1,0:T(2,128)(2,1)} %values_ref.1, bf16[3,4096]{1,0:T(4,128)(2,1)} %offsets_ref.1, s32[1,4096]{1,0:T(1,128)} %bitcast.17, s32[1,4096]{1,0:T(1,128)} %bitcast.18), custom_call_target="tpu_custom_call" | custom-call | tf_op jit(solution)/shard_map/pack/pallas_call | solution.py:350
  1.7 20.4 %all-to-all-start = ((bf16[128,8,256]{2,1,0:T(8,128)(2,1)}), bf16[128,8,256]{2,1,0:T(8,128)(2,1)S(1)}, u32[]{:S(2)}, u32[]{:S(2)}) async-start(bf16[128,8,256]{2,1,0:T(8,128)(2,1)} %pack.1), calls=%async_computation | async-start | bytes 1048576 | tf_op jit(solution)/shard_map/all_to_all | solution.py:359
  22.1 0.8 dynamic-slice_bitcast_fusion.refs_1_
  22.9 30.0 %all-to-all-done = bf16[128,8,256]{2,1,0:T(8,128)(2,1)S(1)} async-done(((bf16[128,8,256]{2,1,0:T(8,128)(2,1)}), bf16[128,8,256]{2,1,0:T(8,128)(2,1)S(1)}, u32[]{:S(2)}, u32[]{:S(2)}) %all-to-all-start) | async-done | bytes 524320 | tf_op jit(solution)/shard_map/all_to_all | solution.py:359
  52.9 0.0 copy-start.4
  52.9 1.0 copy-done.4
  54.0 10.0 %grid_chunk.2 = (bf16[16,4,16,512]{3,2,1,0:T(8,128)(2,1)}, f32[4,256,256]{2,1,0:T(8,128)S(1)}) custom-call(bf16[64,16,256]{2,1,0:T(8,128)(2,1)S(1)} %bitcast.11, bf16[64,256]{1,0:T(8,128)(2,1)S(1)} %dynamic-slice_bitcast_fusion.refs_1_, bf16[512,512]{1,0:T(8,128)(2,1)S(1)} %copy-done.4), custom_call_target="tpu_custom_call" | custom-call | flops 7516192768 | bytes 4194304 | tf_op jit(solution)/shard_map/grid_chunk/pallas_call | solution.py:266
  63.9 0.0 copy-start.5
  63.9 9.3 %all-to-all-start.1 = ((bf16[16,4,16,512]{3,2,1,0:T(8,128)(2,1)}), bf16[16,4,16,512]{3,2,1,0:T(8,128)(2,1)S(1)}, u32[]{:S(2)}, u32[]{:S(2)}) async-start(bf16[16,4,16,512]{3,2,1,0:T(8,128)(2,1)} %get-tuple-element.10), calls=%async_computation.1 | async-start | bytes 2097152 | tf_op jit(solution)/shard_map/all_to_all | solution.py:359
  73.2 0.0 copy-done.5
  73.2 9.4 %grid_chunk.3 = bf16[16,6,16,512]{3,2,1,0:T(8,128)(2,1)S(1)} custom-call(bf16[64,16,256]{2,1,0:T(8,128)(2,1)S(1)} %bitcast.12, bf16[64,256]{1,0:T(8,128)(2,1)S(1)} %dynamic-slice_bitcast_fusion.refs_1_, bf16[512,512]{1,0:T(8,128)(2,1)S(1)} %copy-done.5, f32[4,256,256]{2,1,0:T(8,128)S(1)} %get-tuple-element.11.refs_3_), custom_call_target="tpu_custom_call" | custom-call | flops 7516192768 | bytes 4194304 | tf_op jit(solution)/shard_map/grid_chunk/pallas_call | solution.py:266
  82.7 0.0 copy-start.1
  82.7 1.1 copy-done.1
  83.8 5.2 %all-to-all-done.1.first_ref = bf16[16,4,16,512]{3,2,1,0:T(8,128)(2,1)S(1)} async-done(((bf16[16,4,16,512]{3,2,1,0:T(8,128)(2,1)}), bf16[16,4,16,512]{3,2,1,0:T(8,128)(2,1)S(1)}, u32[]{:S(2)}, u32[]{:S(2)}) %all-to-all-start.1) | async-done | bytes 1048608 | tf_op jit(solution)/shard_map/all_to_all | solution.py:359
  89.1 4.4 %all-to-all-start.2 = ((bf16[16,6,16,512]{3,2,1,0:T(8,128)(2,1)}), bf16[16,6,16,512]{3,2,1,0:T(8,128)(2,1)S(1)}, u32[]{:S(2)}, u32[]{:S(2)}) async-start(bf16[16,6,16,512]{3,2,1,0:T(8,128)(2,1)} %copy-done.1), calls=%async_computation.2 | async-start | bytes 3145728 | tf_op jit(solution)/shard_map/all_to_all | solution.py:359
  93.4 4.3 %copy.18 = bf16[2,2,256,4,256]{2,4,3,1,0:T(8,128)(2,1)} copy(bf16[2,2,256,4,256]{4,3,2,1,0:T(4,128)(2,1)} %param.13) | data formatting | bytes 4194304 | tf_op jit(solution)/shard_map/optimization_barrier | solution.py:364
  97.7 3.1 %constant_dynamic-slice_fusion = (bf16[2,2,256,2,256]{2,4,3,1,0:T(8,128)(2,1)}, bf16[2,2,256,2,256]{2,4,3,1,0:T(8,128)(2,1)}) fusion(bf16[2,2,256,4,256]{2,4,3,1,0:T(8,128)(2,1)} %copy.18, s32[]{:T(128)S(6)} %select_n.12, s32[]{:T(128)S(6)} %select_n.11), kind=kLoop, calls=%fused_computation.1 | loop fusion | bytes 4194312 | tf_op jit(solution)/shard_map/dynamic_slice | solution.py:375
  100.8 0.0 copy-start.2
  100.8 2.3 %copy.20 = bf16[2,2,256,512]{3,2,1,0:T(8,128)(2,1)} copy(bf16[2,2,256,512]{2,3,1,0:T(8,128)(2,1)} %bitcast.14) | data formatting | bytes 2097152 | tf_op jit(solution)/shard_map/reshape | solution.py:376
  103.1 2.1 %collective-permute-start = (bf16[2,2,256,512]{3,2,1,0:T(8,128)(2,1)}, bf16[2,2,256,512]{3,2,1,0:T(8,128)(2,1)}, u32[]{:S(2)}, u32[]{:S(2)}) collective-permute-start(bf16[2,2,256,512]{3,2,1,0:T(8,128)(2,1)} %copy.20), channel_id=1, source_target_pairs={{0,1},{1,0},{2,3},{3,2},{4,5},{5,4},{6,7},{7,6},{8,9},{9,8},{10,11... | collective-permute-start | bytes 3145736 | tf_op jit(solution)/shard_map/ppermute | solution.py:378
  105.3 2.3 %copy.21.own_ref = bf16[2,2,256,512]{3,2,1,0:T(8,128)(2,1)} copy(bf16[2,2,256,512]{2,3,1,0:T(8,128)(2,1)} %bitcast.13) | data formatting | bytes 2097152 | tf_op jit(solution)/shard_map/reshape | solution.py:376
  107.6 0.4 collective-permute-done.other_ref
  108.0 7.3 %all-to-all-done.2.second_ref = bf16[16,6,16,512]{3,2,1,0:T(8,128)(2,1)S(1)} async-done(((bf16[16,6,16,512]{3,2,1,0:T(8,128)(2,1)}), bf16[16,6,16,512]{3,2,1,0:T(8,128)(2,1)S(1)}, u32[]{:S(2)}, u32[]{:S(2)}) %all-to-all-start.2) | async-done | bytes 1572896 | tf_op jit(solution)/shard_map/all_to_all | solution.py:359
  115.3 0.0 copy-done.2
  115.3 0.0 copy-start
  115.3 1.2 copy-done
  116.6 0.0 copy-start.3
  116.6 1.0 copy-done.3
  117.6 3.7 %combine.1 = bf16[8,2,32,512]{3,2,1,0:T(8,128)(2,1)S(1)} custom-call(bf16[16,4,16,512]{3,2,1,0:T(8,128)(2,1)S(1)} %all-to-all-done.1.first_ref, bf16[16,6,16,512]{3,2,1,0:T(8,128)(2,1)S(1)} %all-to-all-done.2.second_ref, bf16[2,512,256]{2,1,0:T(8,128)(2,1)S(1)} %copy-done.3, bf16[2,512,256]{2,1,0:T(8,128)(2,1)S(1)} %copy-done.2, ...), custom_call_target="tpu_custom_call" | custom-call | flops 1610612736 | bytes 8388608 | tf_op jit(solution)/shard_map/combine/pallas_call | solution.py:309
  121.3 14.5 %all_to_all.20 = bf16[8,2,32,512]{3,2,1,0:T(8,128)(2,1)S(1)} all-to-all(bf16[8,2,32,512]{3,2,1,0:T(8,128)(2,1)S(1)} %combine.1), channel_id=1, replica_groups=mesh['zh'=8,'zl'=2,'x'=4,'y'=4,'core'=2] {'y','core'}, dimensions={0} | all-to-all | bytes 1048576 | tf_op jit(solution)/shard_map/all_to_all | solution.py:359
  135.9 0.6 reshape.27
  136.5 0.6 reduce_sum.9
  137.1 0.9 copy.23
  (1 shorter events, 0.0 us)
Async XLA Ops:
  1.7 51.2 %all-to-all-start = ((bf16[128,8,256]{2,1,0:T(8,128)(2,1)}), bf16[128,8,256]{2,1,0:T(8,128)(2,1)S(1)}, u32[]{:S(2)}, u32[]{:S(2)}) async-start(bf16[128,8,256]{2,1,0:T(8,128)(2,1)} %pack.1), calls=%async_computation | async-start | bytes 1048576 | tf_op jit(solution)/shard_map/all_to_all | solution.py:359
  52.9 1.0 copy-start.4
  63.9 9.3 %copy-start.5 = (bf16[512,512]{1,0:T(8,128)(2,1)S(1)}, bf16[512,512]{1,0:T(8,128)(2,1)}, u32[]{:S(2)}) copy-start(bf16[512,512]{1,0:T(8,128)(2,1)} %constant.34.clone.refs_2_) | copy-start | bytes 1572868
  63.9 25.1 %all-to-all-start.1 = ((bf16[16,4,16,512]{3,2,1,0:T(8,128)(2,1)}), bf16[16,4,16,512]{3,2,1,0:T(8,128)(2,1)S(1)}, u32[]{:S(2)}, u32[]{:S(2)}) async-start(bf16[16,4,16,512]{3,2,1,0:T(8,128)(2,1)} %get-tuple-element.10), calls=%async_computation.1 | async-start | bytes 2097152 | tf_op jit(solution)/shard_map/all_to_all | solution.py:359
  82.7 1.2 copy-start.1
  89.1 26.3 %all-to-all-start.2 = ((bf16[16,6,16,512]{3,2,1,0:T(8,128)(2,1)}), bf16[16,6,16,512]{3,2,1,0:T(8,128)(2,1)S(1)}, u32[]{:S(2)}, u32[]{:S(2)}) async-start(bf16[16,6,16,512]{3,2,1,0:T(8,128)(2,1)} %copy-done.1), calls=%async_computation.2 | async-start | bytes 3145728 | tf_op jit(solution)/shard_map/all_to_all | solution.py:359
  100.8 14.6 %copy-start.2 = (bf16[2,512,256]{2,1,0:T(8,128)(2,1)S(1)}, bf16[2,512,256]{2,1,0:T(8,128)(2,1)}, u32[]{:S(2)}) copy-start(bf16[2,512,256]{2,1,0:T(8,128)(2,1)} %constant.36.clone.edge_ref) | copy-start | bytes 1572868
  103.1 4.9 %collective-permute-start = (bf16[2,2,256,512]{3,2,1,0:T(8,128)(2,1)}, bf16[2,2,256,512]{3,2,1,0:T(8,128)(2,1)}, u32[]{:S(2)}, u32[]{:S(2)}) collective-permute-start(bf16[2,2,256,512]{3,2,1,0:T(8,128)(2,1)} %copy.20), channel_id=1, source_target_pairs={{0,1},{1,0},{2,3},{3,2},{4,5},{5,4},{6,7},{7,6},{8,9},{9,8},{10,11... | collective-permute-start | bytes 3145736 | tf_op jit(solution)/shard_map/ppermute | solution.py:378
  115.3 1.2 copy-start
  116.6 1.0 copy-start.3

commit v7 on v6

--- a/solution.py
+++ b/solution.py
@@ -62,6 +62,12 @@
 def y_table():
     both = waves().reshape(2, ZH, ROWS, 256)
     return both.transpose(1, 0, 2, 3).reshape(ZH, 2 * ROWS, 256).astype(ml_dtypes.bfloat16)
+
+
+def grid_table():
+    rows = np.zeros((ZH, 2 * ROWS, 2 * GZ), ml_dtypes.bfloat16)
+    rows[:, :, :GY] = y_table()
+    return np.concatenate([rows, np.broadcast_to(z_table(), (ZH, 2 * GZ, 2 * GZ))], 1)
 
 
 def x_columns(planes, part):
@@ -89,7 +95,7 @@
                 keep = real & (other == coil)
                 cols += [x_columns(planes, part) * keep for part in range(2)]
         halo.append(np.concatenate(cols, 1))
-    return np.stack(main).astype(ml_dtypes.bfloat16), np.stack(halo).astype(ml_dtypes.bfloat16)
+    return np.stack(main + halo).astype(ml_dtypes.bfloat16)
 
 
 def tap_rows(first, second, lanes):
@@ -191,7 +197,7 @@
     return jnp.sum(jnp.where(hit, (1 << place).astype(jnp.float32), 0.0)).astype(jnp.int32)
 
 
-def grid_kernel(last, samples_ref, y_ref, z_ref, *refs):
+def grid_kernel(last, samples_ref, table_ref, *refs):
     if last:
         carry_ref, out_ref, pair_ref, dense_ref, acc_ref, list_ref = refs
     else:
@@ -206,23 +212,27 @@
         acc_ref[HALO:] = jnp.zeros((PLANES, PAIR, GZ), jnp.float32)
     else:
         acc_ref[...] = jnp.zeros((PLANES + HALO, PAIR, GZ), jnp.float32)
-    y_tab = y_ref[...]
+    y_tab = table_ref[: 2 * ROWS, :GY]
 
     def step(index, _):
         block = list_ref[index]
         for part in range(STEP):
             packed = gather(samples_ref, part * (LANES // UNIT), block * UNIT)
             build(packed, y_tab, pair_ref, dense_ref, part * LANES, LANES)
-        here = pl.ds(4 * (block // (CAP // UNIT)), SPAN)
-        product = lax.dot_general(
-            pair_ref[...], dense_ref[...], (((1,), (1,)), ((), ())), preferred_element_type=jnp.float32
-        )
-        acc_ref[here] = acc_ref[here] + product.reshape(SPAN, PAIR, GZ)
+        for plane in range(SPAN):
+            product = lax.dot_general(
+                pair_ref[plane * PAIR : (plane + 1) * PAIR],
+                dense_ref[...],
+                (((1,), (1,)), ((), ())),
+                preferred_element_type=jnp.float32,
+            )
+            here = 4 * (block // (CAP // UNIT)) + plane
+            acc_ref[here] = acc_ref[here] + product
         return 0
 
     lax.fori_loop(0, count, step, 0)
 
-    z_tab = z_ref[...]
+    z_tab = table_ref[2 * ROWS :]
     lines = transform_z(acc_ref[0:PLANES], z_tab)
     if last:
         edge = transform_z(acc_ref[PLANES:], z_tab)
@@ -244,19 +254,18 @@
             out_ref[owner, COILS + pair, :, here] = jnp.concatenate(pieces, 0).astype(jnp.bfloat16)
 
 
-def grid_chunk(samples, y_tab, z_tab, chunk, carry=None):
+def grid_chunk(samples, table, chunk, carry=None):
     last = carry is not None
     tiles = COILS + (COILS // 2 if last else 0)
     flops = 2 * SPAN * PAIR * GZ * SOURCES * CAP * BLOCKS // CHUNKS
     edges = (HALO, PAIR, GZ)
     in_specs = [
         pl.BlockSpec((SOURCES, 16, 128), lambda q: (0, 0, chunk)),
-        pl.BlockSpec((2 * ROWS, GY), lambda q: (0, 0)),
-        pl.BlockSpec((2 * GZ, 2 * GZ), lambda q: (0, 0)),
+        pl.BlockSpec((2 * ROWS + 2 * GZ, 2 * GZ), lambda q: (0, 0)),
     ]
     out_specs = [pl.BlockSpec((GROUPS, tiles, 16, 2 * GZ), lambda q: (0, 0, 0, 0))]
     out_shape = [jax.ShapeDtypeStruct((GROUPS, tiles, 16, 2 * GZ), jnp.bfloat16)]
-    operands = [samples, y_tab, z_tab]
+    operands = [samples, table]
     if last:
         in_specs.append(pl.BlockSpec(edges, lambda q: (0, 0, 0)))
         operands.append(carry)
@@ -281,50 +290,80 @@
     )(*operands)
 
 
-def combine_kernel(first_ref, second_ref, main_ref, edge_ref, own_ref, other_ref, out_ref):
+def combine_kernel(first_ref, second_ref, table_ref, own_hbm, other_hbm, out_ref, own_ref, other_ref, sems):
+    copies = [
+        pltpu.make_async_copy(own_hbm, own_ref, sems.at[0]),
+        pltpu.make_async_copy(other_hbm, other_ref, sems.at[1]),
+    ]
+    for copy in copies:
+        copy.start()
     core = lax.axis_index("core")
-    total = [None, None]
     depth = GROUPS * 16
-    for maps_ref, pair in ((own_ref, core), (other_ref, 1 - core)):
-        edge_rows = second_ref[:, COILS + pair].reshape(depth, GZ)
-        for coil in range(2):
-            image = jnp.dot(edge_ref[coil], edge_rows, preferred_element_type=jnp.float32)
-            for chunk, ref in enumerate((first_ref, second_ref)):
-                rows = ref[:, 2 * pair + coil].reshape(depth, GZ)
-                image = image + jnp.dot(main_ref[chunk], rows, preferred_element_type=jnp.float32)
-            image_re, image_im = image[:GX], image[GX:]
-            map_re = maps_ref[coil, 0].astype(jnp.float32)
-            map_im = maps_ref[coil, 1].astype(jnp.float32)
-            real = map_re * image_re + map_im * image_im
-            imag = map_re * image_im - map_im * image_re
-            total = [real, imag] if total[0] is None else [total[0] + real, total[1] + imag]
-    for part in range(2):
-        out_ref[:, part] = total[part].astype(jnp.bfloat16).reshape(8, GX // 8, GZ)
-
-
-def combine(first, second, own, other):
-    main_tab, edge_tab = x_tables()
-    depth = GROUPS * 16
-    maps = pl.BlockSpec((2, 2, GX, GZ), lambda y: (0, 0, 0, y))
+    for e in range(2):
+        lanes = slice(e * GZ, (e + 1) * GZ)
+        total = None
+        for side, (maps_ref, pair) in enumerate(((own_ref, core), (other_ref, 1 - core))):
+            edge_rows = second_ref[:, COILS + pair, :, lanes].reshape(depth, GZ)
+            for coil in range(2):
+                image = jnp.dot(
+                    table_ref[CHUNKS + coil], edge_rows, preferred_element_type=jnp.float32
+                )
+                for chunk, ref in enumerate((first_ref, second_ref)):
+                    rows = ref[:, 2 * pair + coil, :, lanes].reshape(depth, GZ)
+                    image = image + jnp.dot(
+                        table_ref[chunk], rows, preferred_element_type=jnp.float32
+                    )
+                if e == coil == 0:
+                    copies[side].wait()
+                image_re, image_im = image[:GX], image[GX:]
+                map_re = maps_ref[coil, 0, :, lanes].astype(jnp.float32)
+                map_im = maps_ref[coil, 1, :, lanes].astype(jnp.float32)
+                real = map_re * image_re + map_im * image_im
+                imag = map_re * image_im - map_im * image_re
+                total = [real, imag] if total is None else [total[0] + real, total[1] + imag]
+        for part in range(2):
+            out_ref[:, part, :, lanes] = total[part].astype(jnp.bfloat16).reshape(8, GX // 8, GZ)
+
+
+def combine(first, second, table, own, other):
+    vmem, hbm = pl.BlockSpec(memory_space=pltpu.VMEM), pl.BlockSpec(memory_space=pltpu.HBM)
     return pl.pallas_call(
         combine_kernel,
-        grid=(2,),
-        in_specs=[
-            pl.BlockSpec((GROUPS, COILS, 16, GZ), lambda y: (0, 0, 0, y)),
-            pl.BlockSpec((GROUPS, COILS + 2, 16, GZ), lambda y: (0, 0, 0, y)),
-            pl.BlockSpec((CHUNKS, 2 * GX, depth), lambda y: (0, 0, 0)),
-            pl.BlockSpec((2, 2 * GX, depth), lambda y: (0, 0, 0)),
-            maps,
-            maps,
+        in_specs=[vmem, vmem, vmem, hbm, hbm],
+        out_specs=vmem,
+        out_shape=jax.ShapeDtypeStruct((8, 2, GX // 8, 2 * GZ), jnp.bfloat16),
+        scratch_shapes=[
+            pltpu.VMEM((2, 2, GX, 2 * GZ), jnp.bfloat16),
+            pltpu.VMEM((2, 2, GX, 2 * GZ), jnp.bfloat16),
+            pltpu.SemaphoreType.DMA((2,)),
         ],
-        out_specs=pl.BlockSpec((8, 2, GX // 8, GZ), lambda y: (0, 0, 0, y)),
-        out_shape=jax.ShapeDtypeStruct((8, 2, GX // 8, 2 * GZ), jnp.bfloat16),
         compiler_params=pltpu.CompilerParams(vmem_limit_bytes=36 * 2**20),
         cost_estimate=pl.CostEstimate(
-            flops=2 * 4 * 2 * GX * 3 * depth * 2 * GZ, bytes_accessed=8 * 2**20, transcendentals=0
+            flops=2 * 4 * 2 * GX * 3 * GROUPS * 16 * 2 * GZ,
+            bytes_accessed=8 * 2**20,
+            transcendentals=0,
         ),
         name="combine",
-    )(first, second, jnp.asarray(main_tab), jnp.asarray(edge_tab), own, other)
+    )(first, second, table, own, other)
+
+
+def add_kernel(parts_ref, out_ref):
+    for half in range(2):
+        total = parts_ref[half].astype(jnp.float32)
+        for chip in range(1, 4):
+            total = total + parts_ref[2 * chip + half].astype(jnp.float32)
+        for e in range(2):
+            for part in range(2):
+                out_ref[part, :, 2 * half + e, :] = total[part, :, e * GZ : (e + 1) * GZ]
+
+
+def add(parts):
+    return pl.pallas_call(
+        add_kernel,
+        out_shape=jax.ShapeDtypeStruct((2, GX // 8, 4, GZ), jnp.float32),
+        compiler_params=pltpu.CompilerParams(vmem_limit_bytes=16 * 2**20),
+        name="add",
+    )(parts)
 
 
 def pack_kernel(values_ref, offsets_ref, cells_ref, slots_ref, out_ref):
@@ -365,10 +404,12 @@
     planes = ("zl", "x", "core")
     got = turn(packed, ("zh",) + planes)
     samples = got.reshape(SOURCES, 16, BLOCKS * CAP)
-    y_tab = lax.dynamic_index_in_dim(
-        jnp.asarray(y_table()), lax.axis_index("zh"), 0, keepdims=False
-    )
-    z_tab = jnp.asarray(z_table())
+
+    def pick(tables, axis):
+        here = lax.axis_index(axis)
+        return lax.dynamic_index_in_dim(jnp.asarray(tables), here, 0, keepdims=False)
+
+    table = pick(grid_table(), "zh")
     core = lax.axis_index("core")
 
     def maps(half):
@@ -376,13 +417,12 @@
         return rows.reshape(2, 2, GX, 2 * GZ)
 
     other = lax.ppermute(maps(1 - core), "core", [(0, 1), (1, 0)])
-    first, carry = grid_chunk(samples, y_tab, z_tab, 0)
+    first, carry = grid_chunk(samples, table, 0)
     first = turn(first, planes)
-    (second,) = grid_chunk(samples, y_tab, z_tab, 1, carry)
-    partial = combine(first, turn(second, planes), maps(core), other)
-    parts = turn(partial, ("y", "core")).reshape(4, 2, 2, GX // 8, 2, GZ)
-    image = jnp.sum(parts.astype(jnp.float32), axis=0)
-    return image.transpose(1, 2, 0, 3, 4).reshape(2, GX // 8, 4, GZ)
+    (second,) = grid_chunk(samples, table, 1, carry)
+    both = np.broadcast_to(x_tables()[None], (2, CHUNKS + 2, 2 * GX, GROUPS * 16))
+    partial = combine(first, turn(second, planes), pick(both, "core"), maps(core), other)
+    return add(turn(partial, ("y", "core")))
 
 
 def solution(mesh):

time: 139 us -> 135 us (0.971)
  local copies, waits for them, and re-layouts: 18.8 us -> 16.6 us
    unnamed x12 -> x6, local copies, waits for them, and re-layouts: 4.47 us -> 3.61 us
    pallas_call x1 -> x2, Pallas kernels: 3.73 us -> 3.84 us  [the longest x1 3.01 us: combine(): pl.pallas_call(combine_kernel, in_specs=[vmem, vmem, vmem, hbm, hbm], out...]
  transfers between devices with their start and end apart: 4 -> 4, of which waited for: 4 -> 4; matrix products, arithmetic and copies ran while one was open for 9% -> 10% of each run, Pallas kernels for 7% -> 7%
where the time goes in v7:
time: 135 us
  waiting for transfers between devices  43 us (32%)
  starting transfers between devices  36 us (27%)
  Pallas kernels  24.5 us (18%)
  local copies, waits for them, and re-layouts  16.6 us (12%)
  blocking collectives  14.5 us (11%)
    all_to_all x3, waiting for transfers between devices, turn(): return lax.all_to_all(array, axes, split_axis=0, concat_axis=0, tiled=True)  42.5 us
    all_to_all x3, starting transfers between devices, turn(): return lax.all_to_all(array, axes, split_axis=0, concat_axis=0, tiled=True)  33.8 us
    pallas_call x2, Pallas kernels, grid_chunk(): pl.pallas_call(lambda *refs: grid_kernel(last, *refs), grid=(1,), in_spec...  19 us
    all_to_all x1, blocking collectives, turn(): return lax.all_to_all(array, axes, split_axis=0, concat_axis=0, tiled=True)  14.5 us
    reshape x2, local copies, waits for them, and re-layouts, maps(): return rows.reshape(2, 2, GX, 2 * GZ)  4.59 us
    optimization_barrier x1, local copies, waits for them, and re-layouts, body(): packed, sensitivity = lax.optimization_barrier((packed, sensitivity))  4.26 us
    unnamed x6, local copies, waits for them, and re-layouts  3.61 us
    dynamic_slice x1, local copies, waits for them, and re-layouts, maps(): rows = lax.dynamic_slice_in_dim(sensitivity, 2 * half, 2, 3)  3.05 us
  transfers between devices with their start and end apart: 4, of which 4 were waited for; matrix products, arithmetic and copies ran while one was open for 10% of the time, Pallas kernels for 7%

profile of v7, /device:TPU:1, one launch (start us, length us, event | category | flops | bytes accessed | tf_op | source)
XLA Modules:
  0.0 134.6 jit_solution(2648647789984650073)
XLA Ops:
  0.0 1.7 %pack.1 = bf16[128,8,256]{2,1,0:T(8,128)(2,1)} custom-call(bf16[2,2,4096]{2,1,0:T(2,128)(2,1)} %values_ref.1, bf16[3,4096]{1,0:T(4,128)(2,1)} %offsets_ref.1, s32[1,4096]{1,0:T(1,128)} %bitcast.11, s32[1,4096]{1,0:T(1,128)} %bitcast.12), custom_call_target="tpu_custom_call" | custom-call | tf_op jit(solution)/shard_map/pack/pallas_call | solution.py:389
  1.7 20.4 %all-to-all-start = ((bf16[128,8,256]{2,1,0:T(8,128)(2,1)}), bf16[128,8,256]{2,1,0:T(8,128)(2,1)S(1)}, u32[]{:S(2)}, u32[]{:S(2)}) async-start(bf16[128,8,256]{2,1,0:T(8,128)(2,1)} %pack.1), calls=%async_computation | async-start | bytes 1048576 | tf_op jit(solution)/shard_map/all_to_all | solution.py:398
  22.1 1.1 dynamic-slice_bitcast_fusion.refs_1_
  23.2 29.7 %all-to-all-done = bf16[128,8,256]{2,1,0:T(8,128)(2,1)S(1)} async-done(((bf16[128,8,256]{2,1,0:T(8,128)(2,1)}), bf16[128,8,256]{2,1,0:T(8,128)(2,1)S(1)}, u32[]{:S(2)}, u32[]{:S(2)}) %all-to-all-start) | async-done | bytes 524320 | tf_op jit(solution)/shard_map/all_to_all | solution.py:398
  52.9 9.8 %grid_chunk.2 = (bf16[16,4,16,512]{3,2,1,0:T(8,128)(2,1)}, f32[4,256,256]{2,1,0:T(8,128)S(1)}) custom-call(bf16[64,16,256]{2,1,0:T(8,128)(2,1)S(1)} %bitcast.7, bf16[576,512]{1,0:T(8,128)(2,1)S(1)} %dynamic-slice_bitcast_fusion.refs_1_), custom_call_target="tpu_custom_call" | custom-call | flops 7516192768 | bytes 4194304 | tf_op jit(solution)/shard_map/grid_chunk/pallas_call | solution.py:275
  62.7 9.1 %all-to-all-start.1 = ((bf16[16,4,16,512]{3,2,1,0:T(8,128)(2,1)}), bf16[16,4,16,512]{3,2,1,0:T(8,128)(2,1)S(1)}, u32[]{:S(2)}, u32[]{:S(2)}) async-start(bf16[16,4,16,512]{3,2,1,0:T(8,128)(2,1)} %get-tuple-element.10), calls=%async_computation.1 | async-start | bytes 2097152 | tf_op jit(solution)/shard_map/all_to_all | solution.py:398
  71.8 9.2 %grid_chunk.3 = bf16[16,6,16,512]{3,2,1,0:T(8,128)(2,1)S(1)} custom-call(bf16[64,16,256]{2,1,0:T(8,128)(2,1)S(1)} %bitcast.8, bf16[576,512]{1,0:T(8,128)(2,1)S(1)} %dynamic-slice_bitcast_fusion.refs_1_, f32[4,256,256]{2,1,0:T(8,128)S(1)} %get-tuple-element.11.refs_2_), custom_call_target="tpu_custom_call" | custom-call | flops 7516192768 | bytes 4194304 | tf_op jit(solution)/shard_map/grid_chunk/pallas_call | solution.py:275
  81.0 0.0 copy-start.1
  81.0 1.2 copy-done.1
  82.2 5.4 %all-to-all-done.1.first_ref = bf16[16,4,16,512]{3,2,1,0:T(8,128)(2,1)S(1)} async-done(((bf16[16,4,16,512]{3,2,1,0:T(8,128)(2,1)}), bf16[16,4,16,512]{3,2,1,0:T(8,128)(2,1)S(1)}, u32[]{:S(2)}, u32[]{:S(2)}) %all-to-all-start.1) | async-done | bytes 1048608 | tf_op jit(solution)/shard_map/all_to_all | solution.py:398
  87.6 4.4 %all-to-all-start.2 = ((bf16[16,6,16,512]{3,2,1,0:T(8,128)(2,1)}), bf16[16,6,16,512]{3,2,1,0:T(8,128)(2,1)S(1)}, u32[]{:S(2)}, u32[]{:S(2)}) async-start(bf16[16,6,16,512]{3,2,1,0:T(8,128)(2,1)} %copy-done.1), calls=%async_computation.2 | async-start | bytes 3145728 | tf_op jit(solution)/shard_map/all_to_all | solution.py:398
  92.0 4.3 %copy.8 = bf16[2,2,256,4,256]{2,4,3,1,0:T(8,128)(2,1)} copy(bf16[2,2,256,4,256]{4,3,2,1,0:T(4,128)(2,1)} %param.11) | data formatting | bytes 4194304 | tf_op jit(solution)/shard_map/optimization_barrier | solution.py:403
  96.2 3.0 %constant_dynamic-slice_fusion.1 = (bf16[2,2,256,2,256]{2,4,3,1,0:T(8,128)(2,1)}, bf16[2,2,256,2,256]{2,4,3,1,0:T(8,128)(2,1)}) fusion(bf16[2,2,256,4,256]{2,4,3,1,0:T(8,128)(2,1)} %copy.8, s32[]{:T(128)S(6)} %select_n.17, s32[]{:T(128)S(6)} %select_n.16), kind=kLoop, calls=%fused_computation.2 | loop fusion | bytes 4194312 | tf_op jit(solution)/shard_map/dynamic_slice | solution.py:416
  99.3 2.3 %copy.10 = bf16[2,2,256,512]{3,2,1,0:T(8,128)(2,1)} copy(bf16[2,2,256,512]{2,3,1,0:T(8,128)(2,1)} %bitcast.10) | data formatting | bytes 2097152 | tf_op jit(solution)/shard_map/reshape | solution.py:417
  101.5 2.1 %collective-permute-start = (bf16[2,2,256,512]{3,2,1,0:T(8,128)(2,1)}, bf16[2,2,256,512]{3,2,1,0:T(8,128)(2,1)}, u32[]{:S(2)}, u32[]{:S(2)}) collective-permute-start(bf16[2,2,256,512]{3,2,1,0:T(8,128)(2,1)} %copy.10), channel_id=1, source_target_pairs={{0,1},{1,0},{2,3},{3,2},{4,5},{5,4},{6,7},{7,6},{8,9},{9,8},{10,11... | collective-permute-start | bytes 3145736 | tf_op jit(solution)/shard_map/ppermute | solution.py:419
  103.7 2.3 %copy.11.own_hbm = bf16[2,2,256,512]{3,2,1,0:T(8,128)(2,1)} copy(bf16[2,2,256,512]{2,3,1,0:T(8,128)(2,1)} %bitcast.9) | data formatting | bytes 2097152 | tf_op jit(solution)/shard_map/reshape | solution.py:417
  106.0 0.4 collective-permute-done.other_hbm
  106.4 7.4 %all-to-all-done.2.second_ref = bf16[16,6,16,512]{3,2,1,0:T(8,128)(2,1)S(1)} async-done(((bf16[16,6,16,512]{3,2,1,0:T(8,128)(2,1)}), bf16[16,6,16,512]{3,2,1,0:T(8,128)(2,1)S(1)}, u32[]{:S(2)}, u32[]{:S(2)}) %all-to-all-start.2) | async-done | bytes 1572896 | tf_op jit(solution)/shard_map/all_to_all | solution.py:398
  113.9 0.0 copy-start
  113.9 1.2 copy-done
  115.1 0.0 copy-start.2
  115.1 1.2 copy-done.2
  116.3 3.0 %combine.1 = bf16[8,2,32,512]{3,2,1,0:T(8,128)(2,1)S(1)} custom-call(bf16[16,4,16,512]{3,2,1,0:T(8,128)(2,1)S(1)} %all-to-all-done.1.first_ref, bf16[16,6,16,512]{3,2,1,0:T(8,128)(2,1)S(1)} %all-to-all-done.2.second_ref, bf16[4,512,256]{2,1,0:T(8,128)(2,1)S(1)} %copy-done.2, bf16[2,2,256,512]{3,2,1,0:T(8,128)(2,1)S(1)} %copy-done, ...), custom_call_target="tpu_custom_call" | custom-call | flops 1610612736 | bytes 8388608 | tf_op jit(solution)/shard_map/combine/pallas_call | solution.py:330
  119.3 14.5 %all_to_all.20.parts_ref = bf16[8,2,32,512]{3,2,1,0:T(8,128)(2,1)S(1)} all-to-all(bf16[8,2,32,512]{3,2,1,0:T(8,128)(2,1)S(1)} %combine.1), channel_id=1, replica_groups=mesh['zh'=8,'zl'=2,'x'=4,'y'=4,'core'=2] {'y','core'}, dimensions={0} | all-to-all | bytes 1048576 | tf_op jit(solution)/shard_map/all_to_all | solution.py:398
  133.8 0.8 add.19
Async XLA Ops:
  1.7 51.2 %all-to-all-start = ((bf16[128,8,256]{2,1,0:T(8,128)(2,1)}), bf16[128,8,256]{2,1,0:T(8,128)(2,1)S(1)}, u32[]{:S(2)}, u32[]{:S(2)}) async-start(bf16[128,8,256]{2,1,0:T(8,128)(2,1)} %pack.1), calls=%async_computation | async-start | bytes 1048576 | tf_op jit(solution)/shard_map/all_to_all | solution.py:398
  62.7 24.9 %all-to-all-start.1 = ((bf16[16,4,16,512]{3,2,1,0:T(8,128)(2,1)}), bf16[16,4,16,512]{3,2,1,0:T(8,128)(2,1)S(1)}, u32[]{:S(2)}, u32[]{:S(2)}) async-start(bf16[16,4,16,512]{3,2,1,0:T(8,128)(2,1)} %get-tuple-element.10), calls=%async_computation.1 | async-start | bytes 2097152 | tf_op jit(solution)/shard_map/all_to_all | solution.py:398
  81.0 1.2 copy-start.1
  87.6 26.3 %all-to-all-start.2 = ((bf16[16,6,16,512]{3,2,1,0:T(8,128)(2,1)}), bf16[16,6,16,512]{3,2,1,0:T(8,128)(2,1)S(1)}, u32[]{:S(2)}, u32[]{:S(2)}) async-start(bf16[16,6,16,512]{3,2,1,0:T(8,128)(2,1)} %copy-done.1), calls=%async_computation.2 | async-start | bytes 3145728 | tf_op jit(solution)/shard_map/all_to_all | solution.py:398
  101.5 4.9 %collective-permute-start = (bf16[2,2,256,512]{3,2,1,0:T(8,128)(2,1)}, bf16[2,2,256,512]{3,2,1,0:T(8,128)(2,1)}, u32[]{:S(2)}, u32[]{:S(2)}) collective-permute-start(bf16[2,2,256,512]{3,2,1,0:T(8,128)(2,1)} %copy.10), channel_id=1, source_target_pairs={{0,1},{1,0},{2,3},{3,2},{4,5},{5,4},{6,7},{7,6},{8,9},{9,8},{10,11... | collective-permute-start | bytes 3145736 | tf_op jit(solution)/shard_map/ppermute | solution.py:419
  113.9 1.2 copy-start
  115.1 1.2 copy-start.2

commit v8 on v7

--- a/solution.py
+++ b/solution.py
@@ -34,7 +34,7 @@
 HALF = PAIR // 2
 CHUNKS = 2
 PLANES = 8
-HALO = 4
+EDGE = 3
 
 
 def series():
@@ -79,23 +79,23 @@
 
 def x_tables():
     main = []
-    for chunk in range(CHUNKS):
+    for first in (PLANES + EDGE, 0):
         cols = []
         for group in range(GROUPS):
-            planes = (16 * group + PLANES * chunk + np.arange(PLANES) - 1) % GX
+            planes = (16 * group + first + np.arange(PLANES) - 1) % GX
             cols += [x_columns(planes, 0), x_columns(planes, 1)]
         main.append(np.concatenate(cols, 1))
-    halo = []
+    edge = []
     for coil in range(2):
         cols = []
         for group in range(GROUPS):
-            planes = (16 * group + 16 + np.arange(HALO) - 1) % GX
-            real = np.arange(HALO) < 3
+            planes = (16 * group + PLANES + np.arange(EDGE + 1) - 1) % GX
+            real = np.arange(EDGE + 1) < EDGE
             for other in range(2):
                 keep = real & (other == coil)
                 cols += [x_columns(planes, part) * keep for part in range(2)]
-        halo.append(np.concatenate(cols, 1))
-    return np.stack(main + halo).astype(ml_dtypes.bfloat16)
+        edge.append(np.concatenate(cols, 1))
+    return np.stack(main + edge).astype(ml_dtypes.bfloat16)
 
 
 def tap_rows(first, second, lanes):
@@ -207,11 +207,9 @@
     for place in range(128 // UNIT):
         list_ref[count] = place
         count = count + ((bits >> place) & 1)
+    acc_ref[...] = jnp.zeros(acc_ref.shape, jnp.float32)
     if last:
-        acc_ref[0:HALO] = carry_ref[...]
-        acc_ref[HALO:] = jnp.zeros((PLANES, PAIR, GZ), jnp.float32)
-    else:
-        acc_ref[...] = jnp.zeros((PLANES + HALO, PAIR, GZ), jnp.float32)
+        acc_ref[PLANES : PLANES + EDGE] = carry_ref[...]
     y_tab = table_ref[: 2 * ROWS, :GY]
 
     def step(index, _):
@@ -233,11 +231,12 @@
     lax.fori_loop(0, count, step, 0)
 
     z_tab = table_ref[2 * ROWS :]
-    lines = transform_z(acc_ref[0:PLANES], z_tab)
     if last:
+        lines = transform_z(acc_ref[0:PLANES], z_tab)
         edge = transform_z(acc_ref[PLANES:], z_tab)
     else:
-        carried_ref[...] = acc_ref[PLANES:]
+        lines = transform_z(acc_ref[EDGE : EDGE + PLANES], z_tab)
+        carried_ref[...] = acc_ref[0:EDGE]
     for row in range(ROWS):
         owner = (row // 4) * 2 + row % 4 // 2
         here = slice(row % 2 * GZ, (row % 2 + 1) * GZ)
@@ -258,9 +257,9 @@
     last = carry is not None
     tiles = COILS + (COILS // 2 if last else 0)
     flops = 2 * SPAN * PAIR * GZ * SOURCES * CAP * BLOCKS // CHUNKS
-    edges = (HALO, PAIR, GZ)
+    edges = (EDGE, PAIR, GZ)
     in_specs = [
-        pl.BlockSpec((SOURCES, 16, 128), lambda q: (0, 0, chunk)),
+        pl.BlockSpec((SOURCES, 16, 128), lambda q: (0, 0, CHUNKS - 1 - chunk)),
         pl.BlockSpec((2 * ROWS + 2 * GZ, 2 * GZ), lambda q: (0, 0)),
     ]
     out_specs = [pl.BlockSpec((GROUPS, tiles, 16, 2 * GZ), lambda q: (0, 0, 0, 0))]
@@ -281,7 +280,7 @@
         scratch_shapes=[
             pltpu.VMEM((SPAN * PAIR, STEP * LANES), jnp.bfloat16),
             pltpu.VMEM((GZ, STEP * LANES), jnp.bfloat16),
-            pltpu.VMEM((PLANES + HALO, PAIR, GZ), jnp.float32),
+            pltpu.VMEM((PLANES + EDGE + 1, PAIR, GZ), jnp.float32),
             pltpu.SMEM((9,), jnp.int32),
         ],
         compiler_params=pltpu.CompilerParams(vmem_limit_bytes=36 * 2**20),

time: 135 us -> 133 us (0.985)
  starting transfers between devices: 36 us -> 33.5 us
    all_to_all x3, starting transfers between devices: 33.8 us -> 31.4 us  [turn(): return lax.all_to_all(array, axes, split_axis=0, concat_axis=0, tiled=True)]
where the time goes in v8:
time: 133 us; the launch traced here: 132 us
  waiting for transfers between devices  43 us (32%)
  starting transfers between devices  33.5 us (25%)
  Pallas kernels  24.5 us (18%)
  local copies, waits for them, and re-layouts  16.6 us (12%)
  blocking collectives  14.5 us (11%)
    all_to_all x3, waiting for transfers between devices, turn(): return lax.all_to_all(array, axes, split_axis=0, concat_axis=0, tiled=True)  42.5 us
    all_to_all x3, starting transfers between devices, turn(): return lax.all_to_all(array, axes, split_axis=0, concat_axis=0, tiled=True)  31.4 us
    pallas_call x2, Pallas kernels, grid_chunk(): pl.pallas_call(lambda *refs: grid_kernel(last, *refs), grid=(1,), in_spec...  19 us
    all_to_all x1, blocking collectives, turn(): return lax.all_to_all(array, axes, split_axis=0, concat_axis=0, tiled=True)  14.5 us
    reshape x2, local copies, waits for them, and re-layouts, maps(): return rows.reshape(2, 2, GX, 2 * GZ)  4.59 us
    optimization_barrier x1, local copies, waits for them, and re-layouts, body(): packed, sensitivity = lax.optimization_barrier((packed, sensitivity))  4.26 us
    unnamed x6, local copies, waits for them, and re-layouts  3.61 us
    dynamic_slice x1, local copies, waits for them, and re-layouts, maps(): rows = lax.dynamic_slice_in_dim(sensitivity, 2 * half, 2, 3)  3.05 us
  transfers between devices with their start and end apart: 4, of which 4 were waited for; matrix products, arithmetic and copies ran while one was open for 10% of the time, Pallas kernels for 7%

profile of v8, /device:TPU:1, one launch (start us, length us, event | category | flops | bytes accessed | tf_op | source)
XLA Modules:
  0.0 132.2 jit_solution(1325622441457960416)
XLA Ops:
  0.0 1.7 %pack.1 = bf16[128,8,256]{2,1,0:T(8,128)(2,1)} custom-call(bf16[2,2,4096]{2,1,0:T(2,128)(2,1)} %values_ref.1, bf16[3,4096]{1,0:T(4,128)(2,1)} %offsets_ref.1, s32[1,4096]{1,0:T(1,128)} %bitcast.11, s32[1,4096]{1,0:T(1,128)} %bitcast.12), custom_call_target="tpu_custom_call" | custom-call | tf_op jit(solution)/shard_map/pack/pallas_call | solution.py:388
  1.7 20.4 %all-to-all-start = ((bf16[128,8,256]{2,1,0:T(8,128)(2,1)}), bf16[128,8,256]{2,1,0:T(8,128)(2,1)S(1)}, u32[]{:S(2)}, u32[]{:S(2)}) async-start(bf16[128,8,256]{2,1,0:T(8,128)(2,1)} %pack.1), calls=%async_computation | async-start | bytes 1048576 | tf_op jit(solution)/shard_map/all_to_all | solution.py:397
  22.1 1.1 dynamic-slice_bitcast_fusion.refs_1_
  23.2 29.7 %all-to-all-done = bf16[128,8,256]{2,1,0:T(8,128)(2,1)S(1)} async-done(((bf16[128,8,256]{2,1,0:T(8,128)(2,1)}), bf16[128,8,256]{2,1,0:T(8,128)(2,1)S(1)}, u32[]{:S(2)}, u32[]{:S(2)}) %all-to-all-start) | async-done | bytes 524320 | tf_op jit(solution)/shard_map/all_to_all | solution.py:397
  52.9 9.8 %grid_chunk.2 = (bf16[16,4,16,512]{3,2,1,0:T(8,128)(2,1)}, f32[3,256,256]{2,1,0:T(8,128)S(1)}) custom-call(bf16[64,16,256]{2,1,0:T(8,128)(2,1)S(1)} %bitcast.7, bf16[576,512]{1,0:T(8,128)(2,1)S(1)} %dynamic-slice_bitcast_fusion.refs_1_), custom_call_target="tpu_custom_call" | custom-call | flops 7516192768 | bytes 4194304 | tf_op jit(solution)/shard_map/grid_chunk/pallas_call | solution.py:274
  62.7 6.6 %all-to-all-start.1 = ((bf16[16,4,16,512]{3,2,1,0:T(8,128)(2,1)}), bf16[16,4,16,512]{3,2,1,0:T(8,128)(2,1)S(1)}, u32[]{:S(2)}, u32[]{:S(2)}) async-start(bf16[16,4,16,512]{3,2,1,0:T(8,128)(2,1)} %get-tuple-element.10), calls=%async_computation.1 | async-start | bytes 2097152 | tf_op jit(solution)/shard_map/all_to_all | solution.py:397
  69.3 9.2 %grid_chunk.3 = bf16[16,6,16,512]{3,2,1,0:T(8,128)(2,1)S(1)} custom-call(bf16[64,16,256]{2,1,0:T(8,128)(2,1)S(1)} %bitcast.8, bf16[576,512]{1,0:T(8,128)(2,1)S(1)} %dynamic-slice_bitcast_fusion.refs_1_, f32[3,256,256]{2,1,0:T(8,128)S(1)} %get-tuple-element.11.refs_2_), custom_call_target="tpu_custom_call" | custom-call | flops 7516192768 | bytes 4194304 | tf_op jit(solution)/shard_map/grid_chunk/pallas_call | solution.py:274
  78.6 0.0 copy-start.1
  78.6 1.2 copy-done.1
  79.7 5.4 %all-to-all-done.1.first_ref = bf16[16,4,16,512]{3,2,1,0:T(8,128)(2,1)S(1)} async-done(((bf16[16,4,16,512]{3,2,1,0:T(8,128)(2,1)}), bf16[16,4,16,512]{3,2,1,0:T(8,128)(2,1)S(1)}, u32[]{:S(2)}, u32[]{:S(2)}) %all-to-all-start.1) | async-done | bytes 1048608 | tf_op jit(solution)/shard_map/all_to_all | solution.py:397
  85.2 4.4 %all-to-all-start.2 = ((bf16[16,6,16,512]{3,2,1,0:T(8,128)(2,1)}), bf16[16,6,16,512]{3,2,1,0:T(8,128)(2,1)S(1)}, u32[]{:S(2)}, u32[]{:S(2)}) async-start(bf16[16,6,16,512]{3,2,1,0:T(8,128)(2,1)} %copy-done.1), calls=%async_computation.2 | async-start | bytes 3145728 | tf_op jit(solution)/shard_map/all_to_all | solution.py:397
  89.5 4.3 %copy.8 = bf16[2,2,256,4,256]{2,4,3,1,0:T(8,128)(2,1)} copy(bf16[2,2,256,4,256]{4,3,2,1,0:T(4,128)(2,1)} %param.11) | data formatting | bytes 4194304 | tf_op jit(solution)/shard_map/optimization_barrier | solution.py:402
  93.8 3.0 %constant_dynamic-slice_fusion.1 = (bf16[2,2,256,2,256]{2,4,3,1,0:T(8,128)(2,1)}, bf16[2,2,256,2,256]{2,4,3,1,0:T(8,128)(2,1)}) fusion(bf16[2,2,256,4,256]{2,4,3,1,0:T(8,128)(2,1)} %copy.8, s32[]{:T(128)S(6)} %select_n.17, s32[]{:T(128)S(6)} %select_n.16), kind=kLoop, calls=%fused_computation.2 | loop fusion | bytes 4194312 | tf_op jit(solution)/shard_map/dynamic_slice | solution.py:415
  96.8 2.3 %copy.10 = bf16[2,2,256,512]{3,2,1,0:T(8,128)(2,1)} copy(bf16[2,2,256,512]{2,3,1,0:T(8,128)(2,1)} %bitcast.10) | data formatting | bytes 2097152 | tf_op jit(solution)/shard_map/reshape | solution.py:416
  99.1 2.1 %collective-permute-start = (bf16[2,2,256,512]{3,2,1,0:T(8,128)(2,1)}, bf16[2,2,256,512]{3,2,1,0:T(8,128)(2,1)}, u32[]{:S(2)}, u32[]{:S(2)}) collective-permute-start(bf16[2,2,256,512]{3,2,1,0:T(8,128)(2,1)} %copy.10), channel_id=1, source_target_pairs={{0,1},{1,0},{2,3},{3,2},{4,5},{5,4},{6,7},{7,6},{8,9},{9,8},{10,11... | collective-permute-start | bytes 3145736 | tf_op jit(solution)/shard_map/ppermute | solution.py:418
  101.2 2.3 %copy.11.own_hbm = bf16[2,2,256,512]{3,2,1,0:T(8,128)(2,1)} copy(bf16[2,2,256,512]{2,3,1,0:T(8,128)(2,1)} %bitcast.9) | data formatting | bytes 2097152 | tf_op jit(solution)/shard_map/reshape | solution.py:416
  103.6 0.4 collective-permute-done.other_hbm
  104.0 7.4 %all-to-all-done.2.second_ref = bf16[16,6,16,512]{3,2,1,0:T(8,128)(2,1)S(1)} async-done(((bf16[16,6,16,512]{3,2,1,0:T(8,128)(2,1)}), bf16[16,6,16,512]{3,2,1,0:T(8,128)(2,1)S(1)}, u32[]{:S(2)}, u32[]{:S(2)}) %all-to-all-start.2) | async-done | bytes 1572896 | tf_op jit(solution)/shard_map/all_to_all | solution.py:397
  111.4 0.0 copy-start
  111.4 1.2 copy-done
  112.6 0.0 copy-start.2
  112.6 1.2 copy-done.2
  113.9 3.0 %combine.1 = bf16[8,2,32,512]{3,2,1,0:T(8,128)(2,1)S(1)} custom-call(bf16[16,4,16,512]{3,2,1,0:T(8,128)(2,1)S(1)} %all-to-all-done.1.first_ref, bf16[16,6,16,512]{3,2,1,0:T(8,128)(2,1)S(1)} %all-to-all-done.2.second_ref, bf16[4,512,256]{2,1,0:T(8,128)(2,1)S(1)} %copy-done.2, bf16[2,2,256,512]{3,2,1,0:T(8,128)(2,1)S(1)} %copy-done, ...), custom_call_target="tpu_custom_call" | custom-call | flops 1610612736 | bytes 8388608 | tf_op jit(solution)/shard_map/combine/pallas_call | solution.py:329
  116.9 14.5 %all_to_all.20.parts_ref = bf16[8,2,32,512]{3,2,1,0:T(8,128)(2,1)S(1)} all-to-all(bf16[8,2,32,512]{3,2,1,0:T(8,128)(2,1)S(1)} %combine.1), channel_id=1, replica_groups=mesh['zh'=8,'zl'=2,'x'=4,'y'=4,'core'=2] {'y','core'}, dimensions={0} | all-to-all | bytes 1048576 | tf_op jit(solution)/shard_map/all_to_all | solution.py:397
  131.4 0.8 add.19
Async XLA Ops:
  1.7 51.2 %all-to-all-start = ((bf16[128,8,256]{2,1,0:T(8,128)(2,1)}), bf16[128,8,256]{2,1,0:T(8,128)(2,1)S(1)}, u32[]{:S(2)}, u32[]{:S(2)}) async-start(bf16[128,8,256]{2,1,0:T(8,128)(2,1)} %pack.1), calls=%async_computation | async-start | bytes 1048576 | tf_op jit(solution)/shard_map/all_to_all | solution.py:397
  62.7 22.5 %all-to-all-start.1 = ((bf16[16,4,16,512]{3,2,1,0:T(8,128)(2,1)}), bf16[16,4,16,512]{3,2,1,0:T(8,128)(2,1)S(1)}, u32[]{:S(2)}, u32[]{:S(2)}) async-start(bf16[16,4,16,512]{3,2,1,0:T(8,128)(2,1)} %get-tuple-element.10), calls=%async_computation.1 | async-start | bytes 2097152 | tf_op jit(solution)/shard_map/all_to_all | solution.py:397
  78.6 1.2 copy-start.1
  85.2 26.3 %all-to-all-start.2 = ((bf16[16,6,16,512]{3,2,1,0:T(8,128)(2,1)}), bf16[16,6,16,512]{3,2,1,0:T(8,128)(2,1)S(1)}, u32[]{:S(2)}, u32[]{:S(2)}) async-start(bf16[16,6,16,512]{3,2,1,0:T(8,128)(2,1)} %copy-done.1), calls=%async_computation.2 | async-start | bytes 3145728 | tf_op jit(solution)/shard_map/all_to_all | solution.py:397
  99.1 4.9 %collective-permute-start = (bf16[2,2,256,512]{3,2,1,0:T(8,128)(2,1)}, bf16[2,2,256,512]{3,2,1,0:T(8,128)(2,1)}, u32[]{:S(2)}, u32[]{:S(2)}) collective-permute-start(bf16[2,2,256,512]{3,2,1,0:T(8,128)(2,1)} %copy.10), channel_id=1, source_target_pairs={{0,1},{1,0},{2,3},{3,2},{4,5},{5,4},{6,7},{7,6},{8,9},{9,8},{10,11... | collective-permute-start | bytes 3145736 | tf_op jit(solution)/shard_map/ppermute | solution.py:418
  111.4 1.2 copy-start
  112.6 1.2 copy-start.2

commit v9 on v8

--- a/solution.py
+++ b/solution.py
@@ -143,18 +143,20 @@
     for coil in range(COILS):
         row = (coil // 2) * 8 + (coil % 2) * 2
         value_re, value_im = packed[row : row + 1], packed[row + 1 : row + 2]
-        real.append((value_re * turn_re - value_im * turn_im).astype(jnp.bfloat16))
-        imag.append((value_re * turn_im + value_im * turn_re).astype(jnp.bfloat16))
+        real.append(value_re * turn_re - value_im * turn_im)
+        imag.append(value_re * turn_im + value_im * turn_re)
     values = real + imag
     row = lax.broadcasted_iota(jnp.int32, (8, lanes), 0)
     dense_x = jnp.zeros((8, lanes), jnp.float32)
     for tap in range(TAPS):
         dense_x = jnp.where(row == base_x + tap, taps_xy[tap : tap + 1], dense_x)
     for plane in range(SPAN):
-        weight = jnp.broadcast_to(dense_x[plane : plane + 1], (ROWS, lanes)).astype(jnp.bfloat16)
+        weight = dense_x[plane : plane + 1]
         for part in range(2 * COILS):
             start = plane * PAIR + part * ROWS
-            pair_ref[start : start + ROWS, at : at + lanes] = values[part] * weight
+            pair_ref[start : start + ROWS, at : at + lanes] = (values[part] * weight).astype(
+                jnp.bfloat16
+            )
 
 
 def transform_z(grid_planes, z_tab):
@@ -289,34 +291,40 @@
     )(*operands)
 
 
-def combine_kernel(first_ref, second_ref, table_ref, own_hbm, other_hbm, out_ref, own_ref, other_ref, sems):
-    copies = [
-        pltpu.make_async_copy(own_hbm, own_ref, sems.at[0]),
-        pltpu.make_async_copy(other_hbm, other_ref, sems.at[1]),
-    ]
-    for copy in copies:
-        copy.start()
+def combine_kernel(first_ref, second_ref, table_ref, other_hbm, out_ref, other_ref, sems):
+    fetch = pltpu.make_async_copy(other_hbm, other_ref, sems.at[0])
+    fetch.start()
     core = lax.axis_index("core")
     depth = GROUPS * 16
+
+    def tables(index):
+        rows, columns = 2 * GX * (index // 2), depth * (index % 2)
+        return table_ref[rows : rows + 2 * GX, columns : columns + depth]
+
+    def own(coil, part, lanes):
+        rows = 4 * GX + (2 * coil + part) * GX
+        return table_ref[rows : rows + GX, lanes]
+
+    def other(coil, part, lanes):
+        return other_ref[coil, part, :, lanes]
+
     for e in range(2):
         lanes = slice(e * GZ, (e + 1) * GZ)
         total = None
-        for side, (maps_ref, pair) in enumerate(((own_ref, core), (other_ref, 1 - core))):
+        for maps, pair in ((own, core), (other, 1 - core)):
             edge_rows = second_ref[:, COILS + pair, :, lanes].reshape(depth, GZ)
             for coil in range(2):
                 image = jnp.dot(
-                    table_ref[CHUNKS + coil], edge_rows, preferred_element_type=jnp.float32
+                    tables(CHUNKS + coil), edge_rows, preferred_element_type=jnp.float32
                 )
                 for chunk, ref in enumerate((first_ref, second_ref)):
                     rows = ref[:, 2 * pair + coil, :, lanes].reshape(depth, GZ)
-                    image = image + jnp.dot(
-                        table_ref[chunk], rows, preferred_element_type=jnp.float32
-                    )
-                if e == coil == 0:
-                    copies[side].wait()
+                    image = image + jnp.dot(tables(chunk), rows, preferred_element_type=jnp.float32)
+                if maps is other and e == coil == 0:
+                    fetch.wait()
                 image_re, image_im = image[:GX], image[GX:]
-                map_re = maps_ref[coil, 0, :, lanes].astype(jnp.float32)
-                map_im = maps_ref[coil, 1, :, lanes].astype(jnp.float32)
+                map_re = maps(coil, 0, lanes).astype(jnp.float32)
+                map_im = maps(coil, 1, lanes).astype(jnp.float32)
                 real = map_re * image_re + map_im * image_im
                 imag = map_re * image_im - map_im * image_re
                 total = [real, imag] if total is None else [total[0] + real, total[1] + imag]
@@ -324,17 +332,16 @@
             out_ref[:, part, :, lanes] = total[part].astype(jnp.bfloat16).reshape(8, GX // 8, GZ)
 
 
-def combine(first, second, table, own, other):
+def combine(first, second, table, other):
     vmem, hbm = pl.BlockSpec(memory_space=pltpu.VMEM), pl.BlockSpec(memory_space=pltpu.HBM)
     return pl.pallas_call(
         combine_kernel,
-        in_specs=[vmem, vmem, vmem, hbm, hbm],
+        in_specs=[vmem, vmem, vmem, hbm],
         out_specs=vmem,
         out_shape=jax.ShapeDtypeStruct((8, 2, GX // 8, 2 * GZ), jnp.bfloat16),
         scratch_shapes=[
             pltpu.VMEM((2, 2, GX, 2 * GZ), jnp.bfloat16),
-            pltpu.VMEM((2, 2, GX, 2 * GZ), jnp.bfloat16),
-            pltpu.SemaphoreType.DMA((2,)),
+            pltpu.SemaphoreType.DMA((1,)),
         ],
         compiler_params=pltpu.CompilerParams(vmem_limit_bytes=36 * 2**20),
         cost_estimate=pl.CostEstimate(
@@ -343,7 +350,7 @@
             transcendentals=0,
         ),
         name="combine",
-    )(first, second, table, own, other)
+    )(first, second, table, other)
 
 
 def add_kernel(parts_ref, out_ref):
@@ -419,8 +426,10 @@
     first, carry = grid_chunk(samples, table, 0)
     first = turn(first, planes)
     (second,) = grid_chunk(samples, table, 1, carry)
-    both = np.broadcast_to(x_tables()[None], (2, CHUNKS + 2, 2 * GX, GROUPS * 16))
-    partial = combine(first, turn(second, planes), pick(both, "core"), maps(core), other)
+    pairs = x_tables().reshape(2, 2, 2 * GX, GROUPS * 16).transpose(0, 2, 1, 3)
+    tables = jnp.asarray(pairs.reshape(4 * GX, 2 * GROUPS * 16))
+    tables = jnp.concatenate([tables, maps(core).reshape(4 * GX, 2 * GZ)], 0)
+    partial = combine(first, turn(second, planes), tables, other)
     return add(turn(partial, ("y", "core")))
 
 

time: 133 us -> 132 us (level)
  local copies, waits for them, and re-layouts: 16.6 us -> 9.57 us
  waiting for transfers between devices: 43 us -> 46.1 us
  Pallas kernels: 24.5 us -> 26.9 us
    unnamed x6 -> x5, local copies, waits for them, and re-layouts: 3.61 us -> 0.24 us
    all_to_all x3, waiting for transfers between devices: 42.5 us -> 45.1 us  [turn(): return lax.all_to_all(array, axes, split_axis=0, concat_axis=0, tiled=True)]
    reshape x2 -> x1, local copies, waits for them, and re-layouts: 4.59 us -> 2.28 us  [maps(): return rows.reshape(2, 2, GX, 2 * GZ)]
    optimization_barrier x1, local copies, waits for them, and re-layouts: 4.26 us -> 2.57 us  [body(): packed, sensitivity = lax.optimization_barrier((packed, sensitivity))]
    dynamic_slice x1 -> x2, local copies, waits for them, and re-layouts: 3.05 us -> 3.38 us  [maps(): rows = lax.dynamic_slice_in_dim(sensitivity, 2 * half, 2, 3)]
  transfers between devices with their start and end apart: 4 -> 4, of which waited for: 4 -> 4; matrix products, arithmetic and copies ran while one was open for 10% -> 7% of each run, Pallas kernels for 7% -> 8%
where the time goes in v9:
time: 132 us
  waiting for transfers between devices  46.1 us (35%)
  starting transfers between devices  34.4 us (26%)
  Pallas kernels  26.9 us (20%)
  blocking collectives  14.5 us (11%)
  local copies, waits for them, and re-layouts  9.57 us (7%)
    all_to_all x3, waiting for transfers between devices, turn(): return lax.all_to_all(array, axes, split_axis=0, concat_axis=0, tiled=True)  45.1 us
    all_to_all x3, starting transfers between devices, turn(): return lax.all_to_all(array, axes, split_axis=0, concat_axis=0, tiled=True)  32.1 us
    pallas_call x2, Pallas kernels, grid_chunk(): pl.pallas_call(lambda *refs: grid_kernel(last, *refs), grid=(1,), in_spec...  20.2 us
    all_to_all x1, blocking collectives, turn(): return lax.all_to_all(array, axes, split_axis=0, concat_axis=0, tiled=True)  14.5 us
    pallas_call x1, Pallas kernels, combine(): pl.pallas_call(combine_kernel, in_specs=[vmem, vmem, vmem, hbm], out_spec...  4.25 us
    dynamic_slice x2, local copies, waits for them, and re-layouts, maps(): rows = lax.dynamic_slice_in_dim(sensitivity, 2 * half, 2, 3)  3.38 us
  transfers between devices with their start and end apart: 4, of which 4 were waited for; matrix products, arithmetic and copies ran while one was open for 7% of the time, Pallas kernels for 8%

profile of v9, /device:TPU:1, one launch (start us, length us, event | category | flops | bytes accessed | tf_op | source)
XLA Modules:
  0.0 131.8 jit_solution(13531838795466610682)
XLA Ops:
  0.0 1.7 %pack.1 = bf16[128,8,256]{2,1,0:T(8,128)(2,1)} custom-call(bf16[2,2,4096]{2,1,0:T(2,128)(2,1)} %values_ref.1, bf16[3,4096]{1,0:T(4,128)(2,1)} %offsets_ref.1, s32[1,4096]{1,0:T(1,128)} %bitcast.14, s32[1,4096]{1,0:T(1,128)} %bitcast.15), custom_call_target="tpu_custom_call" | custom-call | tf_op jit(solution)/shard_map/pack/pallas_call | solution.py:395
  1.7 20.4 %all-to-all-start = ((bf16[128,8,256]{2,1,0:T(8,128)(2,1)}), bf16[128,8,256]{2,1,0:T(8,128)(2,1)S(1)}, u32[]{:S(2)}, u32[]{:S(2)}) async-start(bf16[128,8,256]{2,1,0:T(8,128)(2,1)} %pack.1), calls=%async_computation | async-start | bytes 1048576 | tf_op jit(solution)/shard_map/all_to_all | solution.py:404
  22.1 1.1 dynamic-slice_bitcast_fusion.refs_1_
  23.2 29.7 %all-to-all-done = bf16[128,8,256]{2,1,0:T(8,128)(2,1)S(1)} async-done(((bf16[128,8,256]{2,1,0:T(8,128)(2,1)}), bf16[128,8,256]{2,1,0:T(8,128)(2,1)S(1)}, u32[]{:S(2)}, u32[]{:S(2)}) %all-to-all-start) | async-done | bytes 524320 | tf_op jit(solution)/shard_map/all_to_all | solution.py:404
  52.9 9.8 %grid_chunk.2 = (bf16[16,4,16,512]{3,2,1,0:T(8,128)(2,1)}, f32[3,256,256]{2,1,0:T(8,128)S(1)}) custom-call(bf16[64,16,256]{2,1,0:T(8,128)(2,1)S(1)} %bitcast.9, bf16[576,512]{1,0:T(8,128)(2,1)S(1)} %dynamic-slice_bitcast_fusion.refs_1_), custom_call_target="tpu_custom_call" | custom-call | flops 7516192768 | bytes 4194304 | tf_op jit(solution)/shard_map/grid_chunk/pallas_call | solution.py:276
  62.7 6.7 %all-to-all-start.1 = ((bf16[16,4,16,512]{3,2,1,0:T(8,128)(2,1)}), bf16[16,4,16,512]{3,2,1,0:T(8,128)(2,1)S(1)}, u32[]{:S(2)}, u32[]{:S(2)}) async-start(bf16[16,4,16,512]{3,2,1,0:T(8,128)(2,1)} %get-tuple-element.10), calls=%async_computation.1 | async-start | bytes 2097152 | tf_op jit(solution)/shard_map/all_to_all | solution.py:404
  69.3 10.4 %grid_chunk.3 = bf16[16,6,16,512]{3,2,1,0:T(8,128)(2,1)} custom-call(bf16[64,16,256]{2,1,0:T(8,128)(2,1)S(1)} %bitcast.10, bf16[576,512]{1,0:T(8,128)(2,1)S(1)} %dynamic-slice_bitcast_fusion.refs_1_, f32[3,256,256]{2,1,0:T(8,128)S(1)} %get-tuple-element.11.refs_2_), custom_call_target="tpu_custom_call" | custom-call | flops 7516192768 | bytes 4194304 | tf_op jit(solution)/shard_map/grid_chunk/pallas_call | solution.py:276
  79.7 0.0 copy-start
  79.7 5.4 %all-to-all-done.1.first_ref = bf16[16,4,16,512]{3,2,1,0:T(8,128)(2,1)S(1)} async-done(((bf16[16,4,16,512]{3,2,1,0:T(8,128)(2,1)}), bf16[16,4,16,512]{3,2,1,0:T(8,128)(2,1)S(1)}, u32[]{:S(2)}, u32[]{:S(2)}) %all-to-all-start.1) | async-done | bytes 1048608 | tf_op jit(solution)/shard_map/all_to_all | solution.py:404
  85.2 5.0 %all-to-all-start.2 = ((bf16[16,6,16,512]{3,2,1,0:T(8,128)(2,1)}), bf16[16,6,16,512]{3,2,1,0:T(8,128)(2,1)}, u32[]{:S(2)}, u32[]{:S(2)}) async-start(bf16[16,6,16,512]{3,2,1,0:T(8,128)(2,1)} %grid_chunk.3), calls=%async_computation.2 | async-start | bytes 3145728 | tf_op jit(solution)/shard_map/all_to_all | solution.py:404
  90.2 0.0 copy-done
  90.2 2.6 %copy.8 = bf16[2,2,256,4,256]{2,4,3,1,0:T(8,128)(2,1)} copy(bf16[2,2,256,4,256]{4,3,2,1,0:T(4,128)(2,1)S(1)} %copy-done) | data formatting | bytes 4194304 | tf_op jit(solution)/shard_map/optimization_barrier | solution.py:409
  92.7 2.3 %constant_dynamic-slice_fusion = bf16[2,2,256,2,256]{2,4,3,1,0:T(8,128)(2,1)} fusion(bf16[2,2,256,4,256]{2,4,3,1,0:T(8,128)(2,1)} %copy.8, s32[]{:T(128)S(6)} %select_n.12), kind=kLoop, calls=%fused_computation.2 | loop fusion | bytes 2097156 | tf_op jit(solution)/shard_map/dynamic_slice | solution.py:422
  95.0 2.3 %copy.9 = bf16[2,2,256,512]{3,2,1,0:T(8,128)(2,1)} copy(bf16[2,2,256,512]{2,3,1,0:T(8,128)(2,1)} %bitcast.11) | data formatting | bytes 2097152 | tf_op jit(solution)/shard_map/reshape | solution.py:423
  97.3 2.4 %collective-permute-start = (bf16[2,2,256,512]{3,2,1,0:T(8,128)(2,1)}, bf16[2,2,256,512]{3,2,1,0:T(8,128)(2,1)}, u32[]{:S(2)}, u32[]{:S(2)}) collective-permute-start(bf16[2,2,256,512]{3,2,1,0:T(8,128)(2,1)} %copy.9), channel_id=1, source_target_pairs={{0,1},{1,0},{2,3},{3,2},{4,5},{5,4},{6,7},{7,6},{8,9},{9,8},{10,11... | collective-permute-start | bytes 3145736 | tf_op jit(solution)/shard_map/ppermute | solution.py:425
  99.7 0.0 copy-start.1
  99.7 1.1 constant_dynamic-slice_fusion.1
  100.8 0.2 copy.10
  101.0 0.0 copy-done.1
  101.0 0.1 pad_maximum_fusion.table_ref
  101.2 1.0 collective-permute-done.other_hbm
  102.2 10.0 %all-to-all-done.2.second_ref = bf16[16,6,16,512]{3,2,1,0:T(8,128)(2,1)} async-done(((bf16[16,6,16,512]{3,2,1,0:T(8,128)(2,1)}), bf16[16,6,16,512]{3,2,1,0:T(8,128)(2,1)}, u32[]{:S(2)}, u32[]{:S(2)}) %all-to-all-start.2) | async-done | bytes 1572896 | tf_op jit(solution)/shard_map/all_to_all | solution.py:404
  112.2 4.3 %combine.1 = bf16[8,2,32,512]{3,2,1,0:T(8,128)(2,1)S(1)} custom-call(bf16[16,4,16,512]{3,2,1,0:T(8,128)(2,1)S(1)} %all-to-all-done.1.first_ref, bf16[16,6,16,512]{3,2,1,0:T(8,128)(2,1)} %all-to-all-done.2.second_ref, bf16[2048,512]{1,0:T(8,128)(2,1)S(1)} %pad_maximum_fusion.table_ref, bf16[2,2,256,512]{3,2,1,0:T(8,128)(2,1)} %collective-permute-done.other_hbm), custom_call_target="tpu_custom_call" | custom-call | flops 1610612736 | bytes 8388608 | tf_op jit(solution)/shard_map/combine/pallas_call | solution.py:337
  116.4 14.5 %all_to_all.20.parts_ref = bf16[8,2,32,512]{3,2,1,0:T(8,128)(2,1)S(1)} all-to-all(bf16[8,2,32,512]{3,2,1,0:T(8,128)(2,1)S(1)} %combine.1), channel_id=1, replica_groups=mesh['zh'=8,'zl'=2,'x'=4,'y'=4,'core'=2] {'y','core'}, dimensions={0} | all-to-all | bytes 1048576 | tf_op jit(solution)/shard_map/all_to_all | solution.py:404
  130.9 0.8 add.14
Async XLA Ops:
  1.7 51.2 %all-to-all-start = ((bf16[128,8,256]{2,1,0:T(8,128)(2,1)}), bf16[128,8,256]{2,1,0:T(8,128)(2,1)S(1)}, u32[]{:S(2)}, u32[]{:S(2)}) async-start(bf16[128,8,256]{2,1,0:T(8,128)(2,1)} %pack.1), calls=%async_computation | async-start | bytes 1048576 | tf_op jit(solution)/shard_map/all_to_all | solution.py:404
  62.7 22.5 %all-to-all-start.1 = ((bf16[16,4,16,512]{3,2,1,0:T(8,128)(2,1)}), bf16[16,4,16,512]{3,2,1,0:T(8,128)(2,1)S(1)}, u32[]{:S(2)}, u32[]{:S(2)}) async-start(bf16[16,4,16,512]{3,2,1,0:T(8,128)(2,1)} %get-tuple-element.10), calls=%async_computation.1 | async-start | bytes 2097152 | tf_op jit(solution)/shard_map/all_to_all | solution.py:404
  79.7 10.4 %copy-start = (bf16[2,2,256,4,256]{4,3,2,1,0:T(4,128)(2,1)S(1)}, bf16[2,2,256,4,256]{4,3,2,1,0:T(4,128)(2,1)}, u32[]{:S(2)}) copy-start(bf16[2,2,256,4,256]{4,3,2,1,0:T(4,128)(2,1)} %param.11) | copy-start | bytes 6291460
  85.2 27.0 %all-to-all-start.2 = ((bf16[16,6,16,512]{3,2,1,0:T(8,128)(2,1)}), bf16[16,6,16,512]{3,2,1,0:T(8,128)(2,1)}, u32[]{:S(2)}, u32[]{:S(2)}) async-start(bf16[16,6,16,512]{3,2,1,0:T(8,128)(2,1)} %grid_chunk.3), calls=%async_computation.2 | async-start | bytes 3145728 | tf_op jit(solution)/shard_map/all_to_all | solution.py:404
  97.3 4.9 %collective-permute-start = (bf16[2,2,256,512]{3,2,1,0:T(8,128)(2,1)}, bf16[2,2,256,512]{3,2,1,0:T(8,128)(2,1)}, u32[]{:S(2)}, u32[]{:S(2)}) collective-permute-start(bf16[2,2,256,512]{3,2,1,0:T(8,128)(2,1)} %copy.9), channel_id=1, source_target_pairs={{0,1},{1,0},{2,3},{3,2},{4,5},{5,4},{6,7},{7,6},{8,9},{9,8},{10,11... | collective-permute-start | bytes 3145736 | tf_op jit(solution)/shard_map/ppermute | solution.py:425
  99.7 1.3 %copy-start.1 = (bf16[1024,512]{1,0:T(8,128)(2,1)S(1)}, bf16[1024,512]{1,0:T(8,128)(2,1)}, u32[]{:S(2)}) copy-start(bf16[1024,512]{1,0:T(8,128)(2,1)} %constant.28.clone) | copy-start | bytes 3145732

commit v10 on v9

--- a/solution.py
+++ b/solution.py
@@ -169,23 +169,23 @@
     return jnp.swapaxes(along.reshape(planes, HALF, 2 * GZ), 0, 1)
 
 
-def gather(samples_ref, start, offset):
+def gather(samples_ref, start, offset, lanes):
     per = 128 // UNIT
     lane = lax.broadcasted_iota(jnp.int32, (16, 128), 1) // UNIT
     pieces = []
     for piece in range(LANES // 128):
         joined = None
         for k in range(per):
-            rows = samples_ref[start + piece * per + k].astype(jnp.float32)
+            rows = samples_ref[start + piece * per + k, :, lanes].astype(jnp.float32)
             rows = pltpu.roll(rows, (128 + UNIT * k - offset) % 128, 1)
             joined = rows if joined is None else jnp.where(lane == k, rows, joined)
         pieces.append(joined)
     return jnp.concatenate(pieces, 1)
 
 
-def filled(samples_ref):
+def filled(samples_ref, lanes):
     def step(index, seen):
-        return jnp.maximum(seen, jnp.abs(samples_ref[index].astype(jnp.float32)))
+        return jnp.maximum(seen, jnp.abs(samples_ref[index, :, lanes].astype(jnp.float32)))
 
     seen = lax.fori_loop(0, SOURCES, step, jnp.zeros((16, 128), jnp.float32), unroll=8)
     row = lax.broadcasted_iota(jnp.int32, (16, 128), 0)
@@ -204,7 +204,9 @@
         carry_ref, out_ref, pair_ref, dense_ref, acc_ref, list_ref = refs
     else:
         out_ref, carried_ref, pair_ref, dense_ref, acc_ref, list_ref = refs
-    bits = filled(samples_ref)
+    first = 0 if last else 128
+    lanes = slice(first, first + 128)
+    bits = filled(samples_ref, lanes)
     count = jnp.int32(0)
     for place in range(128 // UNIT):
         list_ref[count] = place
@@ -217,7 +219,7 @@
     def step(index, _):
         block = list_ref[index]
         for part in range(STEP):
-            packed = gather(samples_ref, part * (LANES // UNIT), block * UNIT)
+            packed = gather(samples_ref, part * (LANES // UNIT), block * UNIT, lanes)
             build(packed, y_tab, pair_ref, dense_ref, part * LANES, LANES)
         for plane in range(SPAN):
             product = lax.dot_general(
@@ -260,22 +262,19 @@
     tiles = COILS + (COILS // 2 if last else 0)
     flops = 2 * SPAN * PAIR * GZ * SOURCES * CAP * BLOCKS // CHUNKS
     edges = (EDGE, PAIR, GZ)
-    in_specs = [
-        pl.BlockSpec((SOURCES, 16, 128), lambda q: (0, 0, CHUNKS - 1 - chunk)),
-        pl.BlockSpec((2 * ROWS + 2 * GZ, 2 * GZ), lambda q: (0, 0)),
-    ]
-    out_specs = [pl.BlockSpec((GROUPS, tiles, 16, 2 * GZ), lambda q: (0, 0, 0, 0))]
+    vmem = pl.BlockSpec(memory_space=pltpu.VMEM)
+    in_specs = [vmem, vmem]
+    out_specs = [vmem]
     out_shape = [jax.ShapeDtypeStruct((GROUPS, tiles, 16, 2 * GZ), jnp.bfloat16)]
     operands = [samples, table]
     if last:
-        in_specs.append(pl.BlockSpec(edges, lambda q: (0, 0, 0)))
+        in_specs.append(vmem)
         operands.append(carry)
     else:
-        out_specs.append(pl.BlockSpec(edges, lambda q: (0, 0, 0)))
+        out_specs.append(vmem)
         out_shape.append(jax.ShapeDtypeStruct(edges, jnp.float32))
     return pl.pallas_call(
         lambda *refs: grid_kernel(last, *refs),
-        grid=(1,),
         in_specs=in_specs,
         out_specs=out_specs,
         out_shape=out_shape,

time: 132 us -> 132 us (level)
  no operation moved by 1% of the time
where the time goes in v10:
time: 132 us
  waiting for transfers between devices  46.2 us (35%)
  starting transfers between devices  34.4 us (26%)
  Pallas kernels  26.8 us (20%)
  blocking collectives  14.5 us (11%)
  local copies, waits for them, and re-layouts  9.57 us (7%)
    all_to_all x3, waiting for transfers between devices, turn(): return lax.all_to_all(array, axes, split_axis=0, concat_axis=0, tiled=True)  45.2 us
    all_to_all x3, starting transfers between devices, turn(): return lax.all_to_all(array, axes, split_axis=0, concat_axis=0, tiled=True)  32.1 us
    pallas_call x2, Pallas kernels, grid_chunk(): pl.pallas_call(lambda *refs: grid_kernel(last, *refs), in_specs=in_specs,...  20.1 us
    all_to_all x1, blocking collectives, turn(): return lax.all_to_all(array, axes, split_axis=0, concat_axis=0, tiled=True)  14.5 us
    pallas_call x1, Pallas kernels, combine(): pl.pallas_call(combine_kernel, in_specs=[vmem, vmem, vmem, hbm], out_spec...  4.25 us
    dynamic_slice x2, local copies, waits for them, and re-layouts, maps(): rows = lax.dynamic_slice_in_dim(sensitivity, 2 * half, 2, 3)  3.38 us
  transfers between devices with their start and end apart: 4, of which 4 were waited for; matrix products, arithmetic and copies ran while one was open for 7% of the time, Pallas kernels for 8%

profile of v10, /device:TPU:1, one launch (start us, length us, event | category | flops | bytes accessed | tf_op | source)
XLA Modules:
  0.0 131.7 jit_solution(1959636364227251568)
XLA Ops:
  0.0 1.7 %pack.1 = bf16[128,8,256]{2,1,0:T(8,128)(2,1)} custom-call(bf16[2,2,4096]{2,1,0:T(2,128)(2,1)} %values_ref.1, bf16[3,4096]{1,0:T(4,128)(2,1)} %offsets_ref.1, s32[1,4096]{1,0:T(1,128)} %bitcast.14, s32[1,4096]{1,0:T(1,128)} %bitcast.15), custom_call_target="tpu_custom_call" | custom-call | tf_op jit(solution)/shard_map/pack/pallas_call | solution.py:394
  1.7 20.4 %all-to-all-start = ((bf16[128,8,256]{2,1,0:T(8,128)(2,1)}), bf16[128,8,256]{2,1,0:T(8,128)(2,1)S(1)}, u32[]{:S(2)}, u32[]{:S(2)}) async-start(bf16[128,8,256]{2,1,0:T(8,128)(2,1)} %pack.1), calls=%async_computation | async-start | bytes 1048576 | tf_op jit(solution)/shard_map/all_to_all | solution.py:403
  22.1 1.1 dynamic-slice_bitcast_fusion.refs_1_
  23.2 29.7 %all-to-all-done = bf16[128,8,256]{2,1,0:T(8,128)(2,1)S(1)} async-done(((bf16[128,8,256]{2,1,0:T(8,128)(2,1)}), bf16[128,8,256]{2,1,0:T(8,128)(2,1)S(1)}, u32[]{:S(2)}, u32[]{:S(2)}) %all-to-all-start) | async-done | bytes 524320 | tf_op jit(solution)/shard_map/all_to_all | solution.py:403
  52.9 9.7 %grid_chunk.2 = (bf16[16,4,16,512]{3,2,1,0:T(8,128)(2,1)}, f32[3,256,256]{2,1,0:T(8,128)S(1)}) custom-call(bf16[64,16,256]{2,1,0:T(8,128)(2,1)S(1)} %bitcast.9, bf16[576,512]{1,0:T(8,128)(2,1)S(1)} %dynamic-slice_bitcast_fusion.refs_1_), custom_call_target="tpu_custom_call" | custom-call | flops 7516192768 | bytes 4194304 | tf_op jit(solution)/shard_map/grid_chunk/pallas_call | solution.py:276
  62.6 6.7 %all-to-all-start.1 = ((bf16[16,4,16,512]{3,2,1,0:T(8,128)(2,1)}), bf16[16,4,16,512]{3,2,1,0:T(8,128)(2,1)S(1)}, u32[]{:S(2)}, u32[]{:S(2)}) async-start(bf16[16,4,16,512]{3,2,1,0:T(8,128)(2,1)} %get-tuple-element.10), calls=%async_computation.1 | async-start | bytes 2097152 | tf_op jit(solution)/shard_map/all_to_all | solution.py:403
  69.3 10.4 %grid_chunk.3 = bf16[16,6,16,512]{3,2,1,0:T(8,128)(2,1)} custom-call(bf16[64,16,256]{2,1,0:T(8,128)(2,1)S(1)} %bitcast.10, bf16[576,512]{1,0:T(8,128)(2,1)S(1)} %dynamic-slice_bitcast_fusion.refs_1_, f32[3,256,256]{2,1,0:T(8,128)S(1)} %get-tuple-element.11.refs_2_), custom_call_target="tpu_custom_call" | custom-call | flops 7516192768 | bytes 4194304 | tf_op jit(solution)/shard_map/grid_chunk/pallas_call | solution.py:276
  79.6 0.0 copy-start
  79.6 5.5 %all-to-all-done.1.first_ref = bf16[16,4,16,512]{3,2,1,0:T(8,128)(2,1)S(1)} async-done(((bf16[16,4,16,512]{3,2,1,0:T(8,128)(2,1)}), bf16[16,4,16,512]{3,2,1,0:T(8,128)(2,1)S(1)}, u32[]{:S(2)}, u32[]{:S(2)}) %all-to-all-start.1) | async-done | bytes 1048608 | tf_op jit(solution)/shard_map/all_to_all | solution.py:403
  85.1 5.0 %all-to-all-start.2 = ((bf16[16,6,16,512]{3,2,1,0:T(8,128)(2,1)}), bf16[16,6,16,512]{3,2,1,0:T(8,128)(2,1)}, u32[]{:S(2)}, u32[]{:S(2)}) async-start(bf16[16,6,16,512]{3,2,1,0:T(8,128)(2,1)} %grid_chunk.3), calls=%async_computation.2 | async-start | bytes 3145728 | tf_op jit(solution)/shard_map/all_to_all | solution.py:403
  90.1 0.0 copy-done
  90.1 2.6 %copy.8 = bf16[2,2,256,4,256]{2,4,3,1,0:T(8,128)(2,1)} copy(bf16[2,2,256,4,256]{4,3,2,1,0:T(4,128)(2,1)S(1)} %copy-done) | data formatting | bytes 4194304 | tf_op jit(solution)/shard_map/optimization_barrier | solution.py:408
  92.7 2.3 %constant_dynamic-slice_fusion = bf16[2,2,256,2,256]{2,4,3,1,0:T(8,128)(2,1)} fusion(bf16[2,2,256,4,256]{2,4,3,1,0:T(8,128)(2,1)} %copy.8, s32[]{:T(128)S(6)} %select_n.12), kind=kLoop, calls=%fused_computation.2 | loop fusion | bytes 2097156 | tf_op jit(solution)/shard_map/dynamic_slice | solution.py:421
  95.0 2.3 %copy.9 = bf16[2,2,256,512]{3,2,1,0:T(8,128)(2,1)} copy(bf16[2,2,256,512]{2,3,1,0:T(8,128)(2,1)} %bitcast.11) | data formatting | bytes 2097152 | tf_op jit(solution)/shard_map/reshape | solution.py:422
  97.3 2.4 %collective-permute-start = (bf16[2,2,256,512]{3,2,1,0:T(8,128)(2,1)}, bf16[2,2,256,512]{3,2,1,0:T(8,128)(2,1)}, u32[]{:S(2)}, u32[]{:S(2)}) collective-permute-start(bf16[2,2,256,512]{3,2,1,0:T(8,128)(2,1)} %copy.9), channel_id=1, source_target_pairs={{0,1},{1,0},{2,3},{3,2},{4,5},{5,4},{6,7},{7,6},{8,9},{9,8},{10,11... | collective-permute-start | bytes 3145736 | tf_op jit(solution)/shard_map/ppermute | solution.py:424
  99.6 0.0 copy-start.1
  99.7 1.1 constant_dynamic-slice_fusion.1
  100.7 0.2 copy.10
  101.0 0.0 copy-done.1
  101.0 0.1 pad_maximum_fusion.table_ref
  101.1 1.0 collective-permute-done.other_hbm
  102.1 10.0 %all-to-all-done.2.second_ref = bf16[16,6,16,512]{3,2,1,0:T(8,128)(2,1)} async-done(((bf16[16,6,16,512]{3,2,1,0:T(8,128)(2,1)}), bf16[16,6,16,512]{3,2,1,0:T(8,128)(2,1)}, u32[]{:S(2)}, u32[]{:S(2)}) %all-to-all-start.2) | async-done | bytes 1572896 | tf_op jit(solution)/shard_map/all_to_all | solution.py:403
  112.1 4.3 %combine.1 = bf16[8,2,32,512]{3,2,1,0:T(8,128)(2,1)S(1)} custom-call(bf16[16,4,16,512]{3,2,1,0:T(8,128)(2,1)S(1)} %all-to-all-done.1.first_ref, bf16[16,6,16,512]{3,2,1,0:T(8,128)(2,1)} %all-to-all-done.2.second_ref, bf16[2048,512]{1,0:T(8,128)(2,1)S(1)} %pad_maximum_fusion.table_ref, bf16[2,2,256,512]{3,2,1,0:T(8,128)(2,1)} %collective-permute-done.other_hbm), custom_call_target="tpu_custom_call" | custom-call | flops 1610612736 | bytes 8388608 | tf_op jit(solution)/shard_map/combine/pallas_call | solution.py:336
  116.4 14.5 %all_to_all.20.parts_ref = bf16[8,2,32,512]{3,2,1,0:T(8,128)(2,1)S(1)} all-to-all(bf16[8,2,32,512]{3,2,1,0:T(8,128)(2,1)S(1)} %combine.1), channel_id=1, replica_groups=mesh['zh'=8,'zl'=2,'x'=4,'y'=4,'core'=2] {'y','core'}, dimensions={0} | all-to-all | bytes 1048576 | tf_op jit(solution)/shard_map/all_to_all | solution.py:403
  130.9 0.8 add.14
Async XLA Ops:
  1.7 51.2 %all-to-all-start = ((bf16[128,8,256]{2,1,0:T(8,128)(2,1)}), bf16[128,8,256]{2,1,0:T(8,128)(2,1)S(1)}, u32[]{:S(2)}, u32[]{:S(2)}) async-start(bf16[128,8,256]{2,1,0:T(8,128)(2,1)} %pack.1), calls=%async_computation | async-start | bytes 1048576 | tf_op jit(solution)/shard_map/all_to_all | solution.py:403
  62.6 22.5 %all-to-all-start.1 = ((bf16[16,4,16,512]{3,2,1,0:T(8,128)(2,1)}), bf16[16,4,16,512]{3,2,1,0:T(8,128)(2,1)S(1)}, u32[]{:S(2)}, u32[]{:S(2)}) async-start(bf16[16,4,16,512]{3,2,1,0:T(8,128)(2,1)} %get-tuple-element.10), calls=%async_computation.1 | async-start | bytes 2097152 | tf_op jit(solution)/shard_map/all_to_all | solution.py:403
  79.6 10.5 %copy-start = (bf16[2,2,256,4,256]{4,3,2,1,0:T(4,128)(2,1)S(1)}, bf16[2,2,256,4,256]{4,3,2,1,0:T(4,128)(2,1)}, u32[]{:S(2)}) copy-start(bf16[2,2,256,4,256]{4,3,2,1,0:T(4,128)(2,1)} %param.11) | copy-start | bytes 6291460
  85.1 27.0 %all-to-all-start.2 = ((bf16[16,6,16,512]{3,2,1,0:T(8,128)(2,1)}), bf16[16,6,16,512]{3,2,1,0:T(8,128)(2,1)}, u32[]{:S(2)}, u32[]{:S(2)}) async-start(bf16[16,6,16,512]{3,2,1,0:T(8,128)(2,1)} %grid_chunk.3), calls=%async_computation.2 | async-start | bytes 3145728 | tf_op jit(solution)/shard_map/all_to_all | solution.py:403
  97.3 4.9 %collective-permute-start = (bf16[2,2,256,512]{3,2,1,0:T(8,128)(2,1)}, bf16[2,2,256,512]{3,2,1,0:T(8,128)(2,1)}, u32[]{:S(2)}, u32[]{:S(2)}) collective-permute-start(bf16[2,2,256,512]{3,2,1,0:T(8,128)(2,1)} %copy.9), channel_id=1, source_target_pairs={{0,1},{1,0},{2,3},{3,2},{4,5},{5,4},{6,7},{7,6},{8,9},{9,8},{10,11... | collective-permute-start | bytes 3145736 | tf_op jit(solution)/shard_map/ppermute | solution.py:424
  99.6 1.3 %copy-start.1 = (bf16[1024,512]{1,0:T(8,128)(2,1)S(1)}, bf16[1024,512]{1,0:T(8,128)(2,1)}, u32[]{:S(2)}) copy-start(bf16[1024,512]{1,0:T(8,128)(2,1)} %constant.28.clone) | copy-start | bytes 3145732
